TPU v7x, 32 devices: a whole 2x2x4 slice. The times are simulated.
32 devices in a mesh: dp: 8 (over y, x, core), mp: 4 (over z).
Axes of the slice: x: 2, y: 2, z: 4, core: 2. Of those that a mesh axis runs over, the one named last changes fastest.
Arguments:
- tokens: bfloat16 [8192, 1024], P(('dp', 'mp')), may hold values from -6 to 6
- seg_ids: int32 [8192], P('dp'), may hold values from 0 to 4, as said below
- cotangent: bfloat16 [8192, 1024], P(('dp', 'mp')), may hold values from -6 to 6
- first_gain: float32 [1024], replicated, may hold values from 0.1 to 1.9
- first_shift: float32 [1024], replicated, may hold values from -3 to 3
- project_weight: bfloat16 [3, 1024, 1024], P(None, None, 'mp'), may hold values from -0.1875 to 0.1875
- project_bias: float32 [3, 1024], P(None, 'mp'), may hold values from -3 to 3
- out_weight: bfloat16 [1024, 1024], P('mp'), may hold values from -0.5 to 0.5
- out_bias: float32 [1024], replicated, may hold values from -3 to 3
- second_gain: float32 [1024], replicated, may hold values from 0.1 to 1.9
- second_shift: float32 [1024], replicated, may hold values from -3 to 3
- up_weight: bfloat16 [1024, 4096], P(None, 'mp'), may hold values from -0.1875 to 0.1875
- up_bias: float32 [4096], P('mp'), may hold values from -3 to 3
- down_weight: bfloat16 [4096, 1024], P('mp'), may hold values from -0.125 to 0.125
- down_bias: float32 [1024], replicated, may hold values from -3 to 3
Outputs:
- output: bfloat16 [8192, 1024], P(('dp', 'mp'))
- tokens_grad: bfloat16 [8192, 1024], P(('dp', 'mp'))
- first_gain_grad: float32 [1024], replicated
- first_shift_grad: float32 [1024], replicated
- project_weight_grad: float32 [3, 1024, 1024], P(None, None, 'mp')
- project_bias_grad: float32 [3, 1024], P(None, 'mp')
- out_weight_grad: float32 [1024, 1024], P('mp')
- out_bias_grad: float32 [1024], replicated
- second_gain_grad: float32 [1024], replicated
- second_shift_grad: float32 [1024], replicated
- up_weight_grad: float32 [1024, 4096], P(None, 'mp')
- up_bias_grad: float32 [4096], P('mp')
- down_weight_grad: float32 [4096, 1024], P('mp')
- down_bias_grad: float32 [1024], replicated
Inputs may be any that keep to these rules, and one draw needn't show every extreme that they name: `seg_ids`: within a segment the numbers never fall; equal numbers mark one document, and in every segment one document runs from the segment's first quarter through its third quarter.
All inputs are finite; a program needn't handle non-finite values.
Results may differ from a plain program's by a relative error of at most 0.018.
Values may be sent and summed in bfloat16 or wider, within the bound.
A program may use at most 128 MiB of HBM per device.

v0:
```python
import math

import jax
import jax.numpy as jnp
from jax import lax
from jax.sharding import PartitionSpec as P

HD = 128


EPS = 1e-05


def layer_norm(values, gain, shift):
    mean = jnp.mean(values, -1, keepdims=True)
    centered = values - mean
    var = jnp.mean(centered * centered, -1, keepdims=True)
    scale = lax.rsqrt(var + EPS)
    normed = centered * scale
    return (normed * gain + shift, normed, scale)


def norm_back(grad, normed, scale, gain):
    gain_grad = jnp.sum(grad * normed, 0)
    shift_grad = jnp.sum(grad, 0)
    scaled = grad * gain
    values_grad = scale * (
        scaled
        - jnp.mean(scaled, -1, keepdims=True)
        - normed * jnp.mean(scaled * normed, -1, keepdims=True)
    )
    return (values_grad, gain_grad, shift_grad)


def smooth(values):
    return jax.nn.gelu(values, approximate=True)


def contract_rows(left, right):
    return lax.dot_general(
        left, right, (((0,), (0,)), ((), ())), preferred_element_type=jnp.float32
    )


def times_transposed(left, right):
    return lax.dot_general(
        left, right, (((1,), (1,)), ((), ())), preferred_element_type=jnp.float32
    )


def masked_scores(query_block, keys_all, doc_query, doc_keys, place_query, place_keys, factor):
    scores = (
        jnp.einsum("qhd,khd->hqk", query_block, keys_all, preferred_element_type=jnp.float32)
        * factor
    )
    allowed = (doc_query[:, None] == doc_keys[None, :]) & (
        place_query[:, None] >= place_keys[None, :]
    )
    return jnp.where(allowed[None], scores, -1e30)


def shards(
    tokens,
    seg_ids,
    cotangent,
    first_gain,
    first_shift,
    project_weight,
    project_bias,
    out_weight,
    out_bias,
    second_gain,
    second_shift,
    up_weight,
    up_bias,
    down_weight,
    down_bias,
):
    rows = tokens.shape[0]
    width = tokens.shape[1]
    length = rows * lax.axis_size("mp")
    share = project_weight.shape[2]
    heads = share // HD
    factor = 1.0 / math.sqrt(HD)
    span = min(512, length)
    count_blocks = length // span
    joined_weight = jnp.transpose(project_weight, (1, 0, 2)).reshape(width, 3 * share)
    joined_bias = project_bias.reshape(3 * share)
    places = jnp.arange(length, dtype=jnp.int32)
    starts = jnp.arange(count_blocks, dtype=jnp.int32) * span
    inputs = tokens.astype(jnp.float32)
    first_out, first_normed, first_scale = layer_norm(inputs, first_gain, first_shift)
    first_low = first_out.astype(jnp.bfloat16)
    first_all = lax.all_gather(first_low, "mp", axis=0, tiled=True)
    mixed = (
        jnp.dot(first_all, joined_weight, preferred_element_type=jnp.float32) + joined_bias
    ).astype(jnp.bfloat16)
    queries = mixed[:, :share].reshape(length, heads, HD)
    keys_all = mixed[:, share : 2 * share].reshape(length, heads, HD)
    values_all = mixed[:, 2 * share :].reshape(length, heads, HD)

    def forward_block(start):
        query_block = lax.dynamic_slice_in_dim(queries, start, span, 0)
        doc_query = lax.dynamic_slice_in_dim(seg_ids, start, span, 0)
        place_query = start + jnp.arange(span, dtype=jnp.int32)
        scores = masked_scores(
            query_block, keys_all, doc_query, seg_ids, place_query, places, factor
        )
        peak = jnp.max(scores, -1, keepdims=True)
        expo = jnp.exp(scores - peak)
        total = jnp.sum(expo, -1, keepdims=True)
        probs = (expo / total).astype(jnp.bfloat16)
        context = jnp.einsum("hqk,khd->qhd", probs, values_all, preferred_element_type=jnp.float32)
        return (context.astype(jnp.bfloat16).reshape(span, share), (peak + jnp.log(total))[..., 0])

    context, logsum = lax.map(forward_block, starts)
    context = context.reshape(length, share)
    attended = lax.psum_scatter(
        jnp.dot(context, out_weight, preferred_element_type=jnp.float32).astype(jnp.bfloat16),
        "mp",
        scatter_dimension=0,
        tiled=True,
    ).astype(jnp.float32)
    middle = inputs + (attended + out_bias)
    second_out, second_normed, second_scale = layer_norm(middle, second_gain, second_shift)
    second_low = second_out.astype(jnp.bfloat16)
    second_all = lax.all_gather(second_low, "mp", axis=0, tiled=True)
    pre = jnp.dot(second_all, up_weight, preferred_element_type=jnp.float32) + up_bias
    activated, smooth_back = jax.vjp(smooth, pre)
    hidden_low = activated.astype(jnp.bfloat16)
    reduced = lax.psum_scatter(
        jnp.dot(hidden_low, down_weight, preferred_element_type=jnp.float32).astype(jnp.bfloat16),
        "mp",
        scatter_dimension=0,
        tiled=True,
    ).astype(jnp.float32)
    output = (middle + (reduced + down_bias)).astype(jnp.bfloat16)
    grad_output = cotangent.astype(jnp.float32)
    grad_all = lax.all_gather(cotangent, "mp", axis=0, tiled=True)
    down_grad = contract_rows(hidden_low, grad_all)
    hidden_grad = times_transposed(grad_all, down_weight)
    pre_low = smooth_back(hidden_grad)[0].astype(jnp.bfloat16)
    up_grad = contract_rows(second_all, pre_low)
    upbias_grad = jnp.sum(pre_low.astype(jnp.float32), 0)
    up_grad, upbias_grad, down_grad = lax.psum((up_grad, upbias_grad, down_grad), "dp")
    second_grad = lax.psum_scatter(
        times_transposed(pre_low, up_weight).astype(jnp.bfloat16),
        "mp",
        scatter_dimension=0,
        tiled=True,
    ).astype(jnp.float32)
    middle_part, second_gain_grad, second_shift_grad = norm_back(
        second_grad, second_normed, second_scale, second_gain
    )
    middle_grad = grad_output + middle_part
    middle_low = middle_grad.astype(jnp.bfloat16)
    outbias_grad = jnp.sum(middle_low.astype(jnp.float32), 0)
    downbias_grad = jnp.sum(grad_output, 0)
    middle_all = lax.all_gather(middle_low, "mp", axis=0, tiled=True)
    outw_grad = contract_rows(context, middle_all)
    context_grad = (
        times_transposed(middle_all, out_weight).astype(jnp.bfloat16).reshape(length, heads, HD)
    )

    def back_block(carry, item):
        keys_grad, values_grad = carry
        start, block_sum = item
        query_block = lax.dynamic_slice_in_dim(queries, start, span, 0)
        doc_query = lax.dynamic_slice_in_dim(seg_ids, start, span, 0)
        place_query = start + jnp.arange(span, dtype=jnp.int32)
        scores = masked_scores(
            query_block, keys_all, doc_query, seg_ids, place_query, places, factor
        )
        probs = jnp.exp(scores - block_sum[..., None])
        upstream = lax.dynamic_slice_in_dim(context_grad, start, span, 0)
        values_grad = values_grad + jnp.einsum(
            "hqk,qhd->khd", probs.astype(jnp.bfloat16), upstream, preferred_element_type=jnp.float32
        )
        probs_grad = jnp.einsum(
            "qhd,khd->hqk", upstream, values_all, preferred_element_type=jnp.float32
        )
        scores_grad = probs * (probs_grad - jnp.sum(probs * probs_grad, -1, keepdims=True))
        scores_low = scores_grad.astype(jnp.bfloat16)
        query_grad = (
            jnp.einsum("hqk,khd->qhd", scores_low, keys_all, preferred_element_type=jnp.float32)
            * factor
        )
        keys_grad = (
            keys_grad
            + jnp.einsum(
                "hqk,qhd->khd", scores_low, query_block, preferred_element_type=jnp.float32
            )
            * factor
        )
        return ((keys_grad, values_grad), query_grad)

    empty = jnp.zeros((length, heads, HD), jnp.float32)
    (keys_grad, values_grad), query_grad = lax.scan(back_block, (empty, empty), (starts, logsum))
    mixed_low = jnp.concatenate(
        [
            query_grad.reshape(length, share),
            keys_grad.reshape(length, share),
            values_grad.reshape(length, share),
        ],
        1,
    ).astype(jnp.bfloat16)
    project_grad = jnp.transpose(
        contract_rows(first_all, mixed_low).reshape(width, 3, share), (1, 0, 2)
    )
    pbias_grad = jnp.sum(mixed_low.astype(jnp.float32), 0).reshape(3, share)
    first_grad = lax.psum_scatter(
        times_transposed(mixed_low, joined_weight).astype(jnp.bfloat16),
        "mp",
        scatter_dimension=0,
        tiled=True,
    ).astype(jnp.float32)
    input_part, first_gain_grad, first_shift_grad = norm_back(
        first_grad, first_normed, first_scale, first_gain
    )
    tokens_grad = (middle_grad + input_part).astype(jnp.bfloat16)
    project_grad, pbias_grad, outw_grad = lax.psum((project_grad, pbias_grad, outw_grad), "dp")
    (
        first_gain_grad,
        first_shift_grad,
        outbias_grad,
        second_gain_grad,
        second_shift_grad,
        downbias_grad,
    ) = lax.psum(
        (
            first_gain_grad,
            first_shift_grad,
            outbias_grad,
            second_gain_grad,
            second_shift_grad,
            downbias_grad,
        ),
        ("dp", "mp"),
    )
    return (
        output,
        tokens_grad,
        first_gain_grad,
        first_shift_grad,
        project_grad,
        pbias_grad,
        outw_grad,
        outbias_grad,
        second_gain_grad,
        second_shift_grad,
        up_grad,
        upbias_grad,
        down_grad,
        downbias_grad,
    )


def solution(mesh):
    in_specs = (
        P(("dp", "mp"), None),
        P("dp"),
        P(("dp", "mp"), None),
        P(),
        P(),
        P(None, None, "mp"),
        P(None, "mp"),
        P("mp", None),
        P(),
        P(),
        P(),
        P(None, "mp"),
        P("mp"),
        P("mp", None),
        P(),
    )
    out_specs = (
        P(("dp", "mp"), None),
        P(("dp", "mp"), None),
        P(),
        P(),
        P(None, None, "mp"),
        P(None, "mp"),
        P("mp", None),
        P(),
        P(),
        P(),
        P(None, "mp"),
        P("mp"),
        P("mp", None),
        P(),
    )
    return jax.shard_map(shards, mesh=mesh, in_specs=in_specs, out_specs=out_specs, check_vma=False)
```

profile of v0, /device:TPU:0, one launch (start us, length us, event | category | flops | bytes accessed | tf_op | source)
XLA Modules:
  0.0 657.7 jit_solution(1240454123998325487)
XLA Ops:
  9.9 2.1 fusion.62
  12.9 2.6 copy.40
  15.5 45.4 %all-gather.5.cloned.1.call-done = bf16[1024,1024]{1,0:T(8,128)(2,1)} async-done(((bf16[256,1024]{1,0:T(8,128)(2,1)}), bf16[1024,1024]{1,0:T(8,128)(2,1)}) %all-gather.5.cloned.1.call-update) | async-done | bytes 2097168 | tf_op jit(solution)/shard_map/all_gather | solution.py:94
  60.9 3.9 add_convert_fusion
  68.2 19.3 %while.28 = (s32[]{:T(128)}, bf16[2,512,256]{2,1,0:T(8,128)(2,1)}, f32[2,2,512]{2,1,0:T(2,128)S(1)}, s32[2]{0:T(128)S(1)}, s32[1024]{0:T(1024)S(1)}, /*index=5*/...) while((s32[]{:T(128)}, bf16[2,512,256]{2,1,0:T(8,128)(2,1)}, ...), condition=%wide.region_5.6_spmd.clone, body=%wide.region_2.5_spmd.clone.sunk | while | flops 551157248 | bytes 19445972 | solution.py:116
  72.0 2.1 fusion.132
  81.7 2.1 fusion.132
  87.5 3.3 convolution_convert_fusion.2
  90.8 42.7 %reduce-scatter.5.cloned.1.call-done = bf16[256,1024]{1,0:T(8,128)(2,1)} async-done(((bf16[1024,1024]{1,0:T(8,128)(2,1)}), bf16[256,1024]{1,0:T(8,128)(2,1)}) %reduce-scatter.5.cloned.1.call-update) | async-done | bytes 524304 | tf_op jit(solution)/shard_map/reduce_scatter | solution.py:118
  136.2 2.1 add_convert_fusion.2
  139.2 44.6 %all-gather.7.cloned.1.call-done = bf16[1024,1024]{1,0:T(8,128)(2,1)} async-done(((bf16[256,1024]{1,0:T(8,128)(2,1)}), bf16[1024,1024]{1,0:T(8,128)(2,1)}) %all-gather.7.cloned.1.call-update) | async-done | bytes 2097168 | tf_op jit(solution)/shard_map/all_gather | solution.py:127
  183.8 6.6 fusion.79
  190.4 39.6 %all-gather.9.cloned.1.call-done = bf16[1024,1024]{1,0:T(8,128)(2,1)} async-done(((bf16[256,1024]{1,0:T(8,128)(2,1)}), bf16[1024,1024]{1,0:T(8,128)(2,1)}) %all-gather.9.cloned.1.call-update) | async-done | bytes 2097168 | tf_op jit(solution)/shard_map/all_gather | solution.py:139
  230.0 7.5 %convert_reduce_fusion = (f32[1024]{0:T(1024)S(1)}, bf16[1024,1024]{1,0:T(8,128)(2,1)S(1)}) fusion(f32[1024,1024]{1,0:T(8,128)} %fusion.79, f32[1024]{0:T(1024)S(1)} %copy-done.32, bf16[1024,1024]{1,0:T(8,128)(2,1)} %all-gather.9.cloned.1.call-done, bf16[1024,1024]{1,0:T(8,128)(2,1)S(1)} %copy-done), kind=kOutput, calls=%fused_computation.61 | convolution fusion | flops 2171599872 | bytes 10493952 | tf_op jit(solution)/shard_map/dot_general | solution.py:46
  238.8 3.7 convolution_convert_fusion
  242.6 6.3 convolution_convert_fusion.1
  249.0 36.3 %reduce-scatter.9.cloned.1.call-done = bf16[256,1024]{1,0:T(8,128)(2,1)} async-done(((bf16[1024,1024]{1,0:T(8,128)(2,1)}), bf16[256,1024]{1,0:T(8,128)(2,1)}) %reduce-scatter.9.cloned.1.call-update) | async-done | bytes 524304 | tf_op jit(solution)/shard_map/reduce_scatter | solution.py:146
  285.3 1.8 fusion.72
  287.1 44.1 %reduce-scatter.7.cloned.1.call-done = bf16[256,1024]{1,0:T(8,128)(2,1)} async-done(((bf16[1024,1024]{1,0:T(8,128)(2,1)}), bf16[256,1024]{1,0:T(8,128)(2,1)}) %reduce-scatter.7.cloned.1.call-update) | async-done | bytes 524304 | tf_op jit(solution)/shard_map/reduce_scatter | solution.py:131
  331.2 3.6 convert_reduce_fusion.6
  335.4 44.8 %all-gather.11.cloned.1.call-done = bf16[1024,1024]{1,0:T(8,128)(2,1)} async-done(((bf16[256,1024]{1,0:T(8,128)(2,1)}), bf16[1024,1024]{1,0:T(8,128)(2,1)}) %all-gather.11.cloned.1.call-update) | async-done | bytes 2097168 | tf_op jit(solution)/shard_map/all_gather | solution.py:159
  380.3 3.2 convolution_convert_fusion.4
  383.5 26.7 %while.29 = (s32[]{:T(128)}, f32[1024,2,128]{0,2,1:T(8,128)S(1)}, f32[1024,2,128]{0,2,1:T(8,128)}, bf16[2,512,2,128]{3,1,2,0:T(8,128)(2,1)}, s32[2]{0:T(128)S(1)...) while((s32[]{:T(128)}, f32[1024,2,128]{0,2,1:T(8,128)S(1)}, ...), condition=%wide.region_15.16_spmd.clone, body=%wide.region_13.15_spmd.clone.sunk | while | flops 1360920064 | bytes 55617904 | solution.py:198
  387.5 1.7 fusion.144
  389.2 1.6 fusion.147
  390.8 2.0 multiply_reduce_fusion.3
  395.0 1.8 fusion.146
  400.8 1.7 fusion.144
  402.5 1.6 fusion.147
  404.2 2.0 multiply_reduce_fusion.3
  408.3 1.8 fusion.146
  410.2 1.6 copy.48
  413.9 4.7 convolution_convert_fusion.3
  419.0 6.8 %fusion.81 = f32[1024,1024]{1,0:T(8,128)} fusion(bf16[1024,1024]{1,0:T(8,128)(2,1)} %all-gather.7.cloned.1.call-done, bf16[1024,1024]{1,0:T(8,128)(2,1)} %copy-done.34), kind=kOutput, calls=%fused_computation.126 | convolution fusion | flops 2147483648 | bytes 8388608 | tf_op jit(solution)/shard_map/dot_general | solution.py:40
  425.7 5.1 fusion.76
  430.8 3.5 fusion.75
  434.3 3.8 copy.51
  438.1 2.7 fusion.80
  442.4 15.2 %all-reduce.1 = (f32[3,256]{1,0:T(4,128)}, f32[1024]{0:T(1024)}) all-reduce(f32[3,256]{1,0:T(4,128)S(1)} %reshape.270, f32[1024]{0:T(1024)S(1)} %get-tuple-element.283), channel_id=1, replica_groups=mesh['dp'=8,'mp'=4] {'dp'}, use_global_device_ids=true, to_apply=%region_25.26 | all-reduce | flops 1792 | bytes 14336 | tf_op jit(solution)/shard_map/psum | solution.py:221
  457.6 3.8 reduce-scatter.11.cloned.1.call-done
  461.4 1.6 fusion.73
  463.0 40.9 %all-reduce = (f32[1024]{0:T(1024)}, f32[1024]{0:T(1024)}, f32[1024]{0:T(1024)}, f32[1024]{0:T(1024)}, f32[1024]{0:T(1024)}, /*index=5*/f32[1024]{0:T(1024)}) all-reduce(f32[1024]{0:T(1024)S(1)} %get-tuple-element.227, f32[1024]{0:T(1024)S(1)} %get-tuple-element.232, ...), channel_id=1, replica_groups=mesh['dp'=8,'mp'=4] {'dp','mp'}, use_global_device_ids=true, to_apply=%region_20.21 | all-reduce | flops 6144 | bytes 49152 | tf_op jit(solution)/shard_map/psum | solution.py:229
  503.9 2.3 fusion.66
  506.1 134.0 %all-reduce.5.cloned.1.call-done = (f32[3,1024,256]{2,1,0:T(8,128)}, f32[256,1024]{1,0:T(8,128)}, f32[1024,1024]{1,0:T(8,128)}, f32[1024,1024]{1,0:T(8,128)}) async-done(((f32[3,1024,256]{2,1,0:T(8,128)}, f32[256,1024]{1,0:T(8,128)}, f32[1024,1024]{1,0:T(8,128)}, f32[1024,1024]{1,0:T(8,128)}), (f32[3,1024,256]{2,1,0:T(8,128)}, f32[256,1024]{1,0:T(8,128)}, f32[1024,1024]{1,0:T(8,128)}, ...) | async-done | bytes 12582928 | tf_op jit(solution)/shard_map/psum | solution.py:221
  640.1 3.9 copy.92
  645.0 2.1 copy.94
  647.2 1.6 copy-done.3
  648.7 2.0 copy.95
  (161 shorter events, 36.6 us)
Async XLA Ops:
  7.2 222.8 %copy-start = (bf16[1024,1024]{1,0:T(8,128)(2,1)S(1)}, bf16[1024,1024]{1,0:T(8,128)(2,1)}, u32[]{:S(2)}) copy-start(bf16[1024,1024]{1,0:T(8,128)(2,1)} %param.32) | copy-start | bytes 6291460
  7.2 53.7 %all-gather.5.cloned.1.call-start = ((), (), s32[]{:S(2)}) async-start(), calls=%async_computation.4 | async-start | bytes 2621440 | tf_op jit(solution)/shard_map/all_gather | solution.py:94
  8.6 52.3 %copy-start.23 = (f32[256]{0:T(256)}, f32[256]{0:T(256)S(1)}, u32[]{:S(2)}) copy-start(f32[256]{0:T(256)S(1)} %broadcast_multiply_fusion.5) | copy-start | bytes 3076
  9.9 51.0 %copy-start.25 = (f32[256]{0:T(256)}, f32[256]{0:T(256)S(1)}, u32[]{:S(2)}) copy-start(f32[256]{0:T(256)S(1)} %add_rsqrt_fusion.1) | copy-start | bytes 3076
  12.1 121.4 %reduce-scatter.5.cloned.1.call-start = ((), (), s32[]{:S(2)}) async-start(), calls=%async_computation.5 | async-start | bytes 2621440 | tf_op jit(solution)/shard_map/reduce_scatter | solution.py:118
  64.8 3.4 copy-start.17
  72.0 3.3 copy-start.12
  81.7 3.3 copy-start.12
  87.4 46.1 %copy-start.2 = (bf16[256,1024]{1,0:T(8,128)(2,1)S(1)}, bf16[256,1024]{1,0:T(8,128)(2,1)}, u32[]{:S(2)}) copy-start(bf16[256,1024]{1,0:T(8,128)(2,1)} %param.19) | copy-start | bytes 1572868
  87.5 46.1 %copy-start.20 = (f32[1024]{0:T(1024)S(1)}, f32[1024]{0:T(1024)}, u32[]{:S(2)}) copy-start(f32[1024]{0:T(1024)} %param.27) | copy-start | bytes 12292
  87.5 48.8 %copy-start.21 = (f32[1024]{0:T(1024)S(1)}, f32[1024]{0:T(1024)}, u32[]{:S(2)}) copy-start(f32[1024]{0:T(1024)} %param.28) | copy-start | bytes 12292
  87.5 48.8 %copy-start.27 = (f32[1024]{0:T(1024)S(1)}, f32[1024]{0:T(1024)}, u32[]{:S(2)}) copy-start(f32[1024]{0:T(1024)} %param.29) | copy-start | bytes 12292
  90.8 93.0 %all-gather.7.cloned.1.call-start = ((), (), s32[]{:S(2)}) async-start(), calls=%async_computation.6 | async-start | bytes 2621440 | tf_op jit(solution)/shard_map/all_gather | solution.py:127
  138.4 91.6 %all-gather.9.cloned.1.call-start = ((), (), s32[]{:S(2)}) async-start(), calls=%async_computation.8 | async-start | bytes 2621440 | tf_op jit(solution)/shard_map/all_gather | solution.py:139
  139.0 91.0 %copy-start.32 = (f32[1024]{0:T(1024)S(1)}, f32[1024]{0:T(1024)}, u32[]{:S(2)}) copy-start(f32[1024]{0:T(1024)} %param.31) | copy-start | bytes 12292
  139.0 146.3 %reduce-scatter.9.cloned.1.call-start = ((), (), s32[]{:S(2)}) async-start(), calls=%async_computation.9 | async-start | bytes 2621440 | tf_op jit(solution)/shard_map/reduce_scatter | solution.py:146
  230.0 8.8 %copy-start.29 = (bf16[1024,1024]{1,0:T(8,128)(2,1)S(1)}, bf16[1024,1024]{1,0:T(8,128)(2,1)}, u32[]{:S(2)}) copy-start(bf16[1024,1024]{1,0:T(8,128)(2,1)} %param.30) | copy-start | bytes 6291460
  237.5 1.3 copy-start.34
  242.5 88.7 %copy-start.28 = (f32[1024]{0:T(1024)S(1)}, f32[1024]{0:T(1024)}, u32[]{:S(2)}) copy-start(f32[1024]{0:T(1024)} %param.33) | copy-start | bytes 12292
  242.6 88.7 %reduce-scatter.7.cloned.1.call-start = ((), (), s32[]{:S(2)}) async-start(), calls=%async_computation.7 | async-start | bytes 2621440 | tf_op jit(solution)/shard_map/reduce_scatter | solution.py:131
  248.9 86.2 %copy-start.13 = (bf16[1024,2,128]{0,2,1:T(8,128)(2,1)S(1)}, bf16[1024,2,128]{0,2,1:T(8,128)(2,1)}, u32[]{:S(2)}) copy-start(bf16[1024,2,128]{0,2,1:T(8,128)(2,1)} %get-tuple-element.558) | copy-start | bytes 1572868
  249.0 131.3 %all-gather.11.cloned.1.call-start = ((), (), s32[]{:S(2)}) async-start(), calls=%async_computation.10 | async-start | bytes 2621440 | tf_op jit(solution)/shard_map/all_gather | solution.py:159
  334.8 126.5 %reduce-scatter.11.cloned.1.call-start = ((), (), s32[]{:S(2)}) async-start(), calls=%async_computation.11 | async-start | bytes 2621440 | tf_op jit(solution)/shard_map/reduce_scatter | solution.py:211
  386.0 3.1 copy-start.6
  386.0 3.1 copy-start.14
  390.8 2.0 copy-start.15
  392.8 1.4 copy-start.18
  395.0 1.9 copy-start.19
  399.4 3.1 copy-start.6
  399.4 3.1 copy-start.14
  404.2 2.0 copy-start.15
  406.2 1.4 copy-start.18
  408.3 1.9 copy-start.19
  412.2 18.6 %copy-start.8 = (bf16[1024,256]{1,0:T(8,128)(2,1)}, bf16[1024,256]{1,0:T(8,128)(2,1)S(1)}, u32[]{:S(2)}) copy-start(bf16[1024,256]{1,0:T(8,128)(2,1)S(1)} %copy.54) | copy-start | bytes 1572868
  413.9 16.9 %copy-start.10 = (bf16[1024,256]{1,0:T(8,128)(2,1)}, bf16[1024,256]{1,0:T(8,128)(2,1)S(1)}, u32[]{:S(2)}) copy-start(bf16[1024,256]{1,0:T(8,128)(2,1)S(1)} %copy.55) | copy-start | bytes 1572868
  418.6 221.5 %all-reduce.5.cloned.1.call-start = ((), (), s32[]{:S(2)}) async-start(), calls=%async_computation.12 | async-start | bytes 25165824 | tf_op jit(solution)/shard_map/psum | solution.py:221
  418.9 6.8 %copy-start.31 = (bf16[1024,1024]{1,0:T(8,128)(2,1)S(1)}, bf16[1024,1024]{1,0:T(8,128)(2,1)}, u32[]{:S(2)}) copy-start(bf16[1024,1024]{1,0:T(8,128)(2,1)} %all-gather.9.cloned.1.call-done) | copy-start | bytes 6291460
  419.0 6.8 %copy-start.33 = (f32[1024,1024]{1,0:T(8,128)S(1)}, f32[1024,1024]{1,0:T(8,128)}, u32[]{:S(2)}) copy-start(f32[1024,1024]{1,0:T(8,128)} %fusion.79) | copy-start | bytes 12582916
  425.7 5.1 copy-start.30
  434.3 3.8 copy-start.7
  440.9 20.5 %copy-start.22 = (f32[1024]{0:T(1024)S(1)}, f32[1024]{0:T(1024)}, u32[]{:S(2)}) copy-start(f32[1024]{0:T(1024)} %param.22) | copy-start | bytes 12292
  440.9 20.5 %copy-start.24 = (f32[256]{0:T(256)S(1)}, f32[256]{0:T(256)}, u32[]{:S(2)}) copy-start(f32[256]{0:T(256)} %copy-done.23) | copy-start | bytes 3076
  440.9 20.5 %copy-start.26 = (f32[256]{0:T(256)S(1)}, f32[256]{0:T(256)}, u32[]{:S(2)}) copy-start(f32[256]{0:T(256)} %copy-done.25) | copy-start | bytes 3076
  440.9 63.0 %copy-start.5 = (f32[256,1024]{1,0:T(8,128)S(1)}, f32[256,1024]{1,0:T(8,128)}, u32[]{:S(2)}) copy-start(f32[256,1024]{1,0:T(8,128)} %get-tuple-element.287) | copy-start | bytes 3145732
  640.1 3.9 copy-start.16
  640.1 4.9 copy-start.4
  645.0 3.7 copy-start.3
  645.0 5.7 copy-start.1
  (2 other events, 2.3 us)
Sparse Core Ops, SparseCore 0:
  12.2 48.6 all-gather.4
  90.9 42.5 reduce-scatter.4
  138.5 45.2 all-gather.6
  185.3 44.6 all-gather.8
  242.7 42.5 reduce-scatter.8
  288.0 43.1 reduce-scatter.6
  335.0 45.2 all-gather.10
  418.8 42.5 reduce-scatter.10
  466.5 173.5 all-reduce.4
where the time goes:
time: 665 us; the launch traced here: 658 us
  waiting for transfers between devices  436 us (66%)
  matrix products  80.4 us (12%)
  blocking collectives  56.1 us (8%)
  other arithmetic  31 us (5%)
  local copies, waits for them, and re-layouts  30.5 us (5%)
  between operations  14.6 us (2%)
  loops' own time  8.14 us (1%)
    psum x1, waiting for transfers between devices, shards(): lax.psum((project_grad, pbias_grad, outw_grad), 'dp')  134 us
    all_gather x1, waiting for transfers between devices, shards(): first_all = lax.all_gather(first_low, 'mp', axis=0, tiled=True)  45.4 us
    all_gather x1, waiting for transfers between devices, shards(): middle_all = lax.all_gather(middle_low, 'mp', axis=0, tiled=True)  44.8 us
    all_gather x1, waiting for transfers between devices, shards(): second_all = lax.all_gather(second_low, 'mp', axis=0, tiled=True)  44.6 us
    reduce_scatter x1, waiting for transfers between devices, shards(): lax.psum_scatter(jnp.dot(hidden_low, down_weight, preferred_element_type=...  44.1 us
    reduce_scatter x1, waiting for transfers between devices, shards(): lax.psum_scatter(jnp.dot(context, out_weight, preferred_element_type=jnp....  42.7 us
    psum x1, blocking collectives, shards(): lax.psum((first_gain_grad, first_shift_grad, outbias_grad, second_gain_gr...  40.9 us
    all_gather x1, waiting for transfers between devices, shards(): grad_all = lax.all_gather(cotangent, 'mp', axis=0, tiled=True)  39.6 us
  transfers between devices with their start and end apart: 9, of which 9 were waited for; matrix products, arithmetic and copies ran while one was open for 7% of the time, Pallas kernels for 0%

commit v1 on v0

--- a/solution.py
+++ b/solution.py
@@ -3,12 +3,306 @@
 import jax
 import jax.numpy as jnp
 from jax import lax
+from jax.experimental import pallas as pl
+from jax.experimental.pallas import tpu as pltpu
 from jax.sharding import PartitionSpec as P
 
 HD = 128
-
-
 EPS = 1e-05
+BF = jnp.bfloat16
+F32 = jnp.float32
+MESH = pl.DeviceIdType.MESH
+VMEM = pltpu.VMEM
+DMA = pltpu.SemaphoreType.DMA
+
+
+def mm(left, right):
+    return jnp.dot(left, right, preferred_element_type=F32)
+
+
+def mm_nt(left, right):
+    return lax.dot_general(left, right, (((1,), (1,)), ((), ())), preferred_element_type=F32)
+
+
+def mm_tn(left, right):
+    return lax.dot_general(left, right, (((0,), (0,)), ((), ())), preferred_element_type=F32)
+
+
+class Place:
+    def __init__(self):
+        self.z = lax.axis_index("mp")
+        self.dp = lax.axis_index("dp")
+        self.d = lax.rem(self.dp, 8)
+        self.base = self.dp - self.d
+        self.core = lax.rem(self.d, 2)
+        self.bit_x = lax.rem(self.d // 2, 2)
+        self.bit_y = self.d // 4
+        self.sibling = self.d + 1 - 2 * self.core
+        step_x = 2 - 4 * self.bit_x
+        step_y = 4 - 8 * self.bit_y
+        self.chips = (self.d + step_x, self.d + step_y, self.d + step_x + step_y)
+
+    def along(self, z):
+        return {"dp": self.dp, "mp": z}
+
+    def plane(self, d):
+        return {"dp": self.base + d, "mp": self.z}
+
+
+def remote(src, dst, ss, rs, device):
+    return pltpu.make_async_remote_copy(
+        src_ref=src, dst_ref=dst, send_sem=ss, recv_sem=rs, device_id=device, device_id_type=MESH
+    )
+
+
+def barrier(devices):
+    sem = pltpu.get_barrier_semaphore()
+    for device in devices:
+        pl.semaphore_signal(sem, 1, device_id=device, device_id_type=MESH)
+    return lambda: pl.semaphore_wait(sem, len(devices))
+
+
+def norm(values):
+    mean = jnp.mean(values, -1, keepdims=True)
+    centered = values - mean
+    var = jnp.mean(centered * centered, -1, keepdims=True)
+    scale = lax.rsqrt(var + EPS)
+    return centered * scale, scale
+
+
+class Line:
+    def __init__(self, place, buf, ss, rs, pieces):
+        self.p, self.buf, self.ss, self.rs, self.pieces = place, buf, ss, rs, pieces
+        self.rows = buf.shape[1] // pieces
+
+    def _copy(self, s, c, target, slot):
+        view = self.buf.at[s, pl.ds(c * self.rows, self.rows)]
+        return remote(view, view, self.ss.at[slot, c], self.rs.at[s, c], self.p.along(target))
+
+    def _each(self, c, act):
+        z = self.p.z
+        for slot, off in enumerate((1, -1, 2, -2)):
+            if off > 0:
+                ok = z < 4 - off
+            else:
+                ok = z >= -off
+
+            @pl.when(ok)
+            def _():
+                act(self._copy(z, c, z + off, slot))
+
+    def send(self, c):
+        self._each(c, lambda copy: copy.start())
+
+    def _passed(self, c, act):
+        z = self.p.z
+
+        @pl.when(z == 2)
+        def _():
+            act(self._copy(0, c, 3, 4))
+
+        @pl.when(z == 1)
+        def _():
+            act(self._copy(3, c, 0, 4))
+
+    def order(self, k):
+        return lax.rem(self.p.z + k * (1 - 2 * (self.p.z // 2)) + 4, 4)
+
+    def take(self, k):
+        s = self.order(k)
+        for c in range(self.pieces):
+            self._copy(s, c, self.p.z, 0).wait_recv()
+            if k == 2:
+                self._passed(c, lambda copy: copy.start())
+        return s
+
+    def finish(self):
+        for c in range(self.pieces):
+            self._each(c, lambda copy: copy.wait_send())
+            self._passed(c, lambda copy: copy.wait_send())
+
+
+def softmax_block(mixed, h, r, share, rows, segc, segr, factor):
+    width = (r + 1) * rows
+    top = r * rows
+    q = mixed[top : top + rows, h * HD : (h + 1) * HD]
+    k = mixed[0:width, share + h * HD : share + (h + 1) * HD]
+    scores = mm_nt(q, k) * factor
+    place_q = top + lax.broadcasted_iota(jnp.int32, (rows, width), 0)
+    place_k = lax.broadcasted_iota(jnp.int32, (rows, width), 1)
+    allowed = (segc[top : top + rows, :] == segr[:, 0:width]) & (place_q >= place_k)
+    return jnp.where(allowed, scores, -1e30)
+
+
+def front(
+    x_ref, segr, segc, g1, b1, wq, bq, ow, ob, g2, b2,
+    first_out, mixed_out, own_out, ctx_out, lse_out, middle_out, second_out,
+    first, mixed, own, ctx, outw, lse,
+    ss_first, rs_first, ss_ctx, rs_ctx, ss_wz, rs_wz, ss_wp, rs_wp, ss_ws, rs_ws, sem_out,
+):
+    p = Place()
+    z = p.z
+    rows, width = x_ref.shape
+    share = wq.shape[2]
+    heads = share // HD
+    factor = 1.0 / math.sqrt(HD)
+    slab = ow.shape[0] // 8
+    others = [lax.rem(z + k, 4) for k in (1, 2, 3)]
+    enter = barrier([p.along(t) for t in others] + [p.plane(t) for t in p.chips] + [p.plane(p.sibling)])
+    line = Line(p, first, ss_first, rs_first, 2)
+    half = rows // 2
+
+    def first_norm(c):
+        block = x_ref[c * half : (c + 1) * half, :].astype(F32)
+        normed, _ = norm(block)
+        first[pl.ds(z, 1), c * half : (c + 1) * half, :] = (normed * g1[...] + b1[...]).astype(BF)[None]
+
+    first_norm(0)
+    enter()
+    line.send(0)
+    first_norm(1)
+    line.send(1)
+
+    def slab_z(k, zz):
+        return remote(
+            ow.at[pl.ds(p.d * slab, slab)], outw.at[z, pl.ds(p.d * slab, slab)],
+            ss_wz.at[k], rs_wz.at[z], p.along(zz),
+        )
+
+    for k, t in enumerate(others):
+        slab_z(k, t).start()
+    outw[pl.ds(z, 1)] = ow[...][None]
+
+    def project(s):
+        for t in range(3):
+            part = mm(first[pl.ds(s, 1)][0], wq[t]) + bq[t : t + 1, :]
+            mixed[pl.ds(pl.multiple_of(s * rows, rows), rows), t * share : (t + 1) * share] = part.astype(BF)
+
+    project(z)
+    for k in (1, 2):
+        project(line.take(k))
+
+    def slab_view(t, who):
+        return outw.at[t, pl.ds(who * slab, slab)]
+
+    for k, t in enumerate(others):
+        remote(slab_view(t, p.d), slab_view(t, p.d), ss_wz.at[k], rs_wz.at[t], p.along(z)).wait_recv()
+
+    def slab_p(i, k, t):
+        return remote(
+            slab_view(t, p.d), slab_view(t, p.d), ss_wp.at[i, k], rs_wp.at[i, k], p.plane(p.chips[i])
+        )
+
+    for i in range(3):
+        for k, t in enumerate(others):
+            slab_p(i, k, t).start()
+    project(line.take(3))
+
+    def ctx_send(r, k):
+        return remote(own.at[r], ctx.at[z], ss_ctx.at[r], rs_ctx.at[z], p.along(r))
+
+    for r in reversed(range(4)):
+        for h in range(heads):
+            scores = softmax_block(mixed, h, r, share, rows, segc, segr, factor)
+            peak = jnp.max(scores, -1, keepdims=True)
+            expo = jnp.exp(scores - peak)
+            total = jnp.sum(expo, -1, keepdims=True)
+            probs = (expo / total).astype(BF)
+            v = mixed[0 : (r + 1) * rows, 2 * share + h * HD : 2 * share + (h + 1) * HD]
+            own[r, :, h * HD : (h + 1) * HD] = mm(probs, v).astype(BF)
+            lse[h, r * rows : (r + 1) * rows, :] = jnp.broadcast_to(peak + jnp.log(total), (rows, HD))
+
+        @pl.when(z != r)
+        def _():
+            ctx_send(r, 0).start()
+
+        @pl.when(z == r)
+        def _():
+            ctx[r] = own[r]
+
+        if r == 3:
+            def slab_s(i, k, who, t):
+                return remote(
+                    slab_view(t, who), slab_view(t, who), ss_ws.at[i, k], rs_ws.at[i, k], p.plane(p.sibling)
+                )
+
+            for k, t in enumerate(others):
+                slab_s(3, k, p.d, t).start()
+            for i in range(3):
+                for k, t in enumerate(others):
+                    remote(
+                        slab_view(t, p.chips[i]), slab_view(t, p.chips[i]), ss_wp.at[i, k], rs_wp.at[i, k],
+                        p.plane(p.d),
+                    ).wait_recv()
+                    slab_s(i, k, p.chips[i], t).start()
+
+    for i in range(4):
+        who = p.sibling if i == 3 else p.chips[i] + p.sibling - p.d
+        for k, t in enumerate(others):
+            remote(slab_view(t, who), slab_view(t, who), ss_ws.at[i, k], rs_ws.at[i, k], p.plane(p.d)).wait_recv()
+
+    attended = mm(ctx[pl.ds(z, 1)][0], outw[pl.ds(z, 1)][0])
+    for t in others:
+        remote(own.at[0], ctx.at[t], ss_ctx.at[0], rs_ctx.at[t], p.along(z)).wait_recv()
+        attended = attended + mm(ctx[pl.ds(t, 1)][0], outw[pl.ds(t, 1)][0])
+    middle = x_ref[...].astype(F32) + (attended + ob[...])
+    middle_out[...] = middle
+    normed, _ = norm(middle)
+    second_out[...] = (normed * g2[...] + b2[...]).astype(BF)
+
+    outs = [
+        pltpu.make_async_copy(a, b, sem_out.at[i])
+        for i, (a, b) in enumerate(
+            ((first, first_out), (mixed, mixed_out), (own, own_out), (ctx, ctx_out), (lse, lse_out))
+        )
+    ]
+    for copy in outs:
+        copy.start()
+    line.finish()
+    for k, t in enumerate(others):
+        slab_z(k, t).wait_send()
+        for i in range(3):
+            slab_p(i, k, t).wait_send()
+            slab_s(i, k, p.chips[i], t).wait_send()
+        slab_s(3, k, p.d, t).wait_send()
+    for r in range(4):
+
+        @pl.when(z != r)
+        def _():
+            ctx_send(r, 0).wait_send()
+
+    for copy in outs:
+        copy.wait()
+
+
+def run_front(x, seg_ids, g1, b1, wq, bq, ow, ob, g2, b2):
+    rows, width = x.shape
+    share = wq.shape[2]
+    length = 4 * rows
+    vm = pl.BlockSpec(memory_space=VMEM)
+    hbm = pl.BlockSpec(memory_space=pl.ANY)
+    heads = share // HD
+    shapes = [
+        ((4, rows, width), BF), ((length, 3 * share), BF), ((4, rows, share), BF), ((4, rows, share), BF),
+        ((heads, length, HD), F32), ((rows, width), F32), ((rows, width), BF),
+    ]
+    return pl.pallas_call(
+        front,
+        out_shape=[jax.ShapeDtypeStruct(s, t) for s, t in shapes],
+        in_specs=[vm] * 11,
+        out_specs=[hbm] * 5 + [vm] * 2,
+        scratch_shapes=[
+            VMEM((4, rows, width), BF), VMEM((length, 3 * share), BF), VMEM((4, rows, share), BF),
+            VMEM((4, rows, share), BF), VMEM((4, share, width), BF), VMEM((heads, length, HD), F32),
+            DMA((5, 2)), DMA((4, 2)), DMA((4,)), DMA((4,)), DMA((3,)), DMA((4,)),
+            DMA((3, 3)), DMA((3, 3)), DMA((4, 3)), DMA((4, 3)), DMA((5,)),
+        ],
+        compiler_params=pltpu.CompilerParams(collective_id=0, has_side_effects=True, vmem_limit_bytes=60 << 20),
+        name="front",
+    )(
+        x, seg_ids.reshape(1, length), seg_ids.reshape(length, 1), g1.reshape(1, width), b1.reshape(1, width),
+        wq, bq, ow, ob.reshape(1, width), g2.reshape(1, width), b2.reshape(1, width),
+    )
 
 
 def layer_norm(values, gain, shift):
@@ -89,41 +383,18 @@
     places = jnp.arange(length, dtype=jnp.int32)
     starts = jnp.arange(count_blocks, dtype=jnp.int32) * span
     inputs = tokens.astype(jnp.float32)
-    first_out, first_normed, first_scale = layer_norm(inputs, first_gain, first_shift)
-    first_low = first_out.astype(jnp.bfloat16)
-    first_all = lax.all_gather(first_low, "mp", axis=0, tiled=True)
-    mixed = (
-        jnp.dot(first_all, joined_weight, preferred_element_type=jnp.float32) + joined_bias
-    ).astype(jnp.bfloat16)
+    _, first_normed, first_scale = layer_norm(inputs, first_gain, first_shift)
+    first_all, mixed, context, ctx_rows, lse, middle, second_low = run_front(
+        tokens, seg_ids, first_gain, first_shift, project_weight, project_bias, out_weight, out_bias,
+        second_gain, second_shift,
+    )
+    first_all = first_all.reshape(length, width)
+    context = context.reshape(length, share)
     queries = mixed[:, :share].reshape(length, heads, HD)
     keys_all = mixed[:, share : 2 * share].reshape(length, heads, HD)
     values_all = mixed[:, 2 * share :].reshape(length, heads, HD)
-
-    def forward_block(start):
-        query_block = lax.dynamic_slice_in_dim(queries, start, span, 0)
-        doc_query = lax.dynamic_slice_in_dim(seg_ids, start, span, 0)
-        place_query = start + jnp.arange(span, dtype=jnp.int32)
-        scores = masked_scores(
-            query_block, keys_all, doc_query, seg_ids, place_query, places, factor
-        )
-        peak = jnp.max(scores, -1, keepdims=True)
-        expo = jnp.exp(scores - peak)
-        total = jnp.sum(expo, -1, keepdims=True)
-        probs = (expo / total).astype(jnp.bfloat16)
-        context = jnp.einsum("hqk,khd->qhd", probs, values_all, preferred_element_type=jnp.float32)
-        return (context.astype(jnp.bfloat16).reshape(span, share), (peak + jnp.log(total))[..., 0])
-
-    context, logsum = lax.map(forward_block, starts)
-    context = context.reshape(length, share)
-    attended = lax.psum_scatter(
-        jnp.dot(context, out_weight, preferred_element_type=jnp.float32).astype(jnp.bfloat16),
-        "mp",
-        scatter_dimension=0,
-        tiled=True,
-    ).astype(jnp.float32)
-    middle = inputs + (attended + out_bias)
-    second_out, second_normed, second_scale = layer_norm(middle, second_gain, second_shift)
-    second_low = second_out.astype(jnp.bfloat16)
+    logsum = lse[:, :, 0].reshape(heads, count_blocks, span).transpose(1, 0, 2)
+    _, second_normed, second_scale = layer_norm(middle, second_gain, second_shift)
     second_all = lax.all_gather(second_low, "mp", axis=0, tiled=True)
     pre = jnp.dot(second_all, up_weight, preferred_element_type=jnp.float32) + up_bias
     activated, smooth_back = jax.vjp(smooth, pre)

time: 665 us -> 609 us (0.916)
  waiting for transfers between devices: 436 us -> 342 us
  Pallas kernels: 0 us -> 79.4 us
  matrix products: 80.4 us -> 61.8 us
  other arithmetic: 31 us -> 16.6 us
    pallas_call x0 -> x1, Pallas kernels: none -> 79.4 us  [run_front(): pl.pallas_call(front, out_shape=[jax.ShapeDtypeStruct(s, t) for s, t in s...]
    all_gather x1 -> x0, waiting for transfers between devices: 45.4 us -> none  [shards(): first_all = lax.all_gather(first_low, 'mp', axis=0, tiled=True)]
    reduce_scatter x1 -> x0, waiting for transfers between devices: 42.7 us -> none  [shards(): lax.psum_scatter(jnp.dot(context, out_weight, preferred_element_type=jnp....]
    dot_general x4 -> x0, matrix products: 10.2 us -> none  [the longest x1 3.86 us: shards(): jnp.dot(first_all, joined_weight, preferred_element_type=jnp.float32)]
    unnamed x67 -> x50, local copies, waits for them, and re-layouts: 18.5 us -> 19.3 us
  transfers between devices with their start and end apart: 9 -> 7, of which waited for: 9 -> 7; matrix products, arithmetic and copies ran while one was open for 7% -> 8% of each run, Pallas kernels for 0% -> 0%
where the time goes in v1:
time: 609 us; the launch traced here: 603 us
  waiting for transfers between devices  342 us (56%)
  Pallas kernels  79.4 us (13%)
  matrix products  61.8 us (10%)
  blocking collectives  55.4 us (9%)
  local copies, waits for them, and re-layouts  27.4 us (4%)
  other arithmetic  16.6 us (3%)
  between operations  14.8 us (2%)
    psum x1, waiting for transfers between devices, shards(): lax.psum((project_grad, pbias_grad, outw_grad), 'dp')  134 us
    pallas_call x1, Pallas kernels, run_front(): pl.pallas_call(front, out_shape=[jax.ShapeDtypeStruct(s, t) for s, t in s...  79.4 us
    reduce_scatter x1, waiting for transfers between devices, shards(): lax.psum_scatter(jnp.dot(hidden_low, down_weight, preferred_element_type=...  44.4 us
    all_gather x1, waiting for transfers between devices, shards(): second_all = lax.all_gather(second_low, 'mp', axis=0, tiled=True)  43.3 us
    psum x1, blocking collectives, shards(): lax.psum((first_gain_grad, first_shift_grad, outbias_grad, second_gain_gr...  40.9 us
    all_gather x1, waiting for transfers between devices, shards(): grad_all = lax.all_gather(cotangent, 'mp', axis=0, tiled=True)  39.7 us
    all_gather x1, waiting for transfers between devices, shards(): middle_all = lax.all_gather(middle_low, 'mp', axis=0, tiled=True)  38.4 us
    reduce_scatter x1, waiting for transfers between devices, shards(): lax.psum_scatter(times_transposed(pre_low, up_weight).astype(jnp.bfloat16...  35.8 us
  transfers between devices with their start and end apart: 7, of which 7 were waited for; matrix products, arithmetic and copies ran while one was open for 8% of the time, Pallas kernels for 0%

profile of v1, /device:TPU:0, one launch (start us, length us, event | category | flops | bytes accessed | tf_op | source)
XLA Modules:
  0.0 602.7 jit_solution(18330097870622120571)
XLA Ops:
  7.2 1.8 copy.39.segc
  9.1 79.4 %front.1 = (bf16[4,256,1024]{2,1,0:T(8,128)(2,1)}, bf16[1024,768]{1,0:T(8,128)(2,1)}, bf16[4,256,256]{2,1,0:T(8,128)(2,1)}, bf16[4,256,256]{2,1,0:T(8,128)(2,1)}...) custom-call(bf16[256,1024]{1,0:T(8,128)(2,1)} %x_ref.1, s32[1,1024]{1,0:T(1,128)} %bitcast.110, ...), custom_call_target="tpu_custom_call" | custom-call | tf_op jit(solution)/shard_map/front/pallas_call | solution.py:289
  89.5 43.3 %all-gather.4.cloned.1.call-done = bf16[1024,1024]{1,0:T(8,128)(2,1)} async-done(((bf16[256,1024]{1,0:T(8,128)(2,1)}), bf16[1024,1024]{1,0:T(8,128)(2,1)}) %all-gather.4.cloned.1.call-update) | async-done | bytes 2097168 | tf_op jit(solution)/shard_map/all_gather | solution.py:398
  132.8 6.6 %fusion.60 = f32[1024,1024]{1,0:T(8,128)} fusion(bf16[1024,1024]{1,0:T(8,128)(2,1)} %all-gather.4.cloned.1.call-done, bf16[1024,1024]{1,0:T(8,128)(2,1)} %param.28), kind=kOutput, calls=%fused_computation.103 | convolution fusion | flops 2147483648 | bytes 8388608 | tf_op jit(solution)/shard_map/dot_general | solution.py:399
  139.4 39.7 %all-gather.6.cloned.1.call-done = bf16[1024,1024]{1,0:T(8,128)(2,1)} async-done(((bf16[256,1024]{1,0:T(8,128)(2,1)}), bf16[1024,1024]{1,0:T(8,128)(2,1)}) %all-gather.6.cloned.1.call-update) | async-done | bytes 2097168 | tf_op jit(solution)/shard_map/all_gather | solution.py:410
  179.1 7.5 %convert_reduce_fusion = (f32[1024]{0:T(1024)S(1)}, bf16[1024,1024]{1,0:T(8,128)(2,1)S(1)}) fusion(f32[1024,1024]{1,0:T(8,128)} %fusion.60, f32[1024]{0:T(1024)S(1)} %copy-done.22, bf16[1024,1024]{1,0:T(8,128)(2,1)} %all-gather.6.cloned.1.call-done, bf16[1024,1024]{1,0:T(8,128)(2,1)S(1)} %copy-done), kind=kOutput, calls=%fused_computation.43 | convolution fusion | flops 2171599872 | bytes 10493952 | tf_op jit(solution)/shard_map/dot_general | solution.py:340
  186.6 1.3 copy-done.24
  187.9 3.7 convolution_convert_fusion
  191.7 6.4 %convolution_convert_fusion.1 = bf16[1024,1024]{1,0:T(8,128)(2,1)} fusion(bf16[1024,1024]{1,0:T(8,128)(2,1)S(1)} %copy-done, f32[1024,1024]{1,0:T(8,128)} %fusion.60, f32[1024]{0:T(1024)S(1)} %copy-done.22), kind=kOutput, calls=%fused_computation.48 | convolution fusion | flops 2159017984 | bytes 8392704 | tf_op jit(solution)/shard_map/dot_general | solution.py:403
  198.6 35.8 %reduce-scatter.6.cloned.1.call-done = bf16[256,1024]{1,0:T(8,128)(2,1)} async-done(((bf16[1024,1024]{1,0:T(8,128)(2,1)}), bf16[256,1024]{1,0:T(8,128)(2,1)}) %reduce-scatter.6.cloned.1.call-update) | async-done | bytes 524304 | tf_op jit(solution)/shard_map/reduce_scatter | solution.py:417
  234.4 1.6 fusion.55
  236.0 44.4 %reduce-scatter.4.cloned.1.call-done = bf16[256,1024]{1,0:T(8,128)(2,1)} async-done(((bf16[1024,1024]{1,0:T(8,128)(2,1)}), bf16[256,1024]{1,0:T(8,128)(2,1)}) %reduce-scatter.4.cloned.1.call-update) | async-done | bytes 524304 | tf_op jit(solution)/shard_map/reduce_scatter | solution.py:402
  280.4 3.2 convert_reduce_fusion.6
  283.9 2.6 copy.48
  286.9 2.4 slice_bitcast_fusion
  289.4 1.3 copy_bitcast_fusion.2
  290.7 38.4 %all-gather.8.cloned.1.call-done = bf16[1024,1024]{1,0:T(8,128)(2,1)} async-done(((bf16[256,1024]{1,0:T(8,128)(2,1)}), bf16[1024,1024]{1,0:T(8,128)(2,1)}) %all-gather.8.cloned.1.call-update) | async-done | bytes 2097168 | tf_op jit(solution)/shard_map/all_gather | solution.py:430
  329.1 2.4 convolution_convert_fusion.3
  331.5 23.1 %while.15 = (s32[]{:T(128)}, f32[1024,2,128]{0,2,1:T(8,128)S(1)}, f32[1024,2,128]{0,2,1:T(8,128)}, bf16[2,512,2,128]{3,1,2,0:T(8,128)(2,1)}, s32[2]{0:T(128)S(1)...) while((s32[]{:T(128)}, f32[1024,2,128]{0,2,1:T(8,128)S(1)}, ...), condition=%wide.region_10.0_spmd.clone, body=%wide.region_8.10_spmd.clone.sunk | while | flops 1360920064 | bytes 54053200 | solution.py:469
  334.1 0.7 iota_add_fusion.2
  336.4 1.6 fusion.111
  338.1 2.0 multiply_reduce_fusion.3
  340.1 1.3 multiply_convert_fusion.5
  341.4 0.8 fusion.112
  348.0 1.6 fusion.111
  349.6 2.0 multiply_reduce_fusion.3
  351.6 1.3 multiply_convert_fusion.5
  353.0 0.8 fusion.112
  354.6 1.6 copy.45
  356.6 1.3 convert.14
  358.1 4.6 convolution_convert_fusion.2
  363.1 6.8 %fusion.62 = f32[1024,1024]{1,0:T(8,128)} fusion(bf16[1024,1024]{1,0:T(8,128)(2,1)} %all-gather.4.cloned.1.call-done, bf16[1024,1024]{1,0:T(8,128)(2,1)} %copy-done.24), kind=kOutput, calls=%fused_computation.105 | convolution fusion | flops 2147483648 | bytes 8388608 | tf_op jit(solution)/shard_map/dot_general | solution.py:334
  369.9 5.0 fusion.58
  375.0 1.6 copy.49
  376.6 3.6 fusion.61
  380.3 3.6 convolution_bitcast_fusion
  383.9 1.0 copy-done.3
  385.6 14.5 %all-reduce.1 = (f32[3,256]{1,0:T(4,128)}, f32[1024]{0:T(1024)}) all-reduce(f32[3,256]{1,0:T(4,128)S(1)} %reshape.210, f32[1024]{0:T(1024)S(1)} %get-tuple-element.195), channel_id=1, replica_groups=mesh['dp'=8,'mp'=4] {'dp'}, use_global_device_ids=true, to_apply=%region_20.21 | all-reduce | flops 1792 | bytes 14336 | tf_op jit(solution)/shard_map/psum | solution.py:492
  400.1 5.4 reduce-scatter.8.cloned.1.call-done
  405.5 1.6 fusion.56
  407.1 40.9 %all-reduce = (f32[1024]{0:T(1024)}, f32[1024]{0:T(1024)}, f32[1024]{0:T(1024)}, f32[1024]{0:T(1024)}, f32[1024]{0:T(1024)}, /*index=5*/f32[1024]{0:T(1024)}) all-reduce(f32[1024]{0:T(1024)S(1)} %get-tuple-element.155, f32[1024]{0:T(1024)S(1)} %get-tuple-element.160, ...), channel_id=1, replica_groups=mesh['dp'=8,'mp'=4] {'dp','mp'}, use_global_device_ids=true, to_apply=%region_15.0 | all-reduce | flops 6144 | bytes 49152 | tf_op jit(solution)/shard_map/psum | solution.py:500
  448.0 2.3 fusion.49
  450.3 134.5 %all-reduce.5.cloned.1.call-done = (f32[3,1024,256]{2,1,0:T(8,128)}, f32[256,1024]{1,0:T(8,128)}, f32[1024,1024]{1,0:T(8,128)}, f32[1024,1024]{1,0:T(8,128)}) async-done(((f32[3,1024,256]{2,1,0:T(8,128)}, f32[256,1024]{1,0:T(8,128)}, f32[1024,1024]{1,0:T(8,128)}, f32[1024,1024]{1,0:T(8,128)}), (f32[3,1024,256]{2,1,0:T(8,128)}, f32[256,1024]{1,0:T(8,128)}, f32[1024,1024]{1,0:T(8,128)}, ...) | async-done | bytes 12582928 | tf_op jit(solution)/shard_map/psum | solution.py:492
  584.8 3.9 copy.96
  588.7 1.0 copy.97
  589.7 2.1 copy.98
  591.8 1.6 copy-done.4
  593.4 2.0 copy.99
  (111 shorter events, 10.9 us)
Async XLA Ops:
  7.2 171.9 %copy-start = (bf16[1024,1024]{1,0:T(8,128)(2,1)S(1)}, bf16[1024,1024]{1,0:T(8,128)(2,1)}, u32[]{:S(2)}) copy-start(bf16[1024,1024]{1,0:T(8,128)(2,1)} %param.30) | copy-start | bytes 6291460
  7.2 125.7 %all-gather.4.cloned.1.call-start = ((), (), s32[]{:S(2)}) async-start(), calls=%async_computation.3 | async-start | bytes 2621440 | tf_op jit(solution)/shard_map/all_gather | solution.py:398
  88.5 90.6 %all-gather.6.cloned.1.call-start = ((), (), s32[]{:S(2)}) async-start(), calls=%async_computation.5 | async-start | bytes 2621440 | tf_op jit(solution)/shard_map/all_gather | solution.py:410
  89.3 89.8 %copy-start.22 = (f32[1024]{0:T(1024)S(1)}, f32[1024]{0:T(1024)}, u32[]{:S(2)}) copy-start(f32[1024]{0:T(1024)} %param.29) | copy-start | bytes 12292
  89.3 145.1 %reduce-scatter.6.cloned.1.call-start = ((), (), s32[]{:S(2)}) async-start(), calls=%async_computation.6 | async-start | bytes 2621440 | tf_op jit(solution)/shard_map/reduce_scatter | solution.py:417
  179.1 8.8 %copy-start.19 = (bf16[1024,1024]{1,0:T(8,128)(2,1)S(1)}, bf16[1024,1024]{1,0:T(8,128)(2,1)}, u32[]{:S(2)}) copy-start(bf16[1024,1024]{1,0:T(8,128)(2,1)} %param.28) | copy-start | bytes 6291460
  186.6 1.3 copy-start.24
  191.7 6.5 %copy-start.2 = (f32[256,1024]{1,0:T(8,128)S(1)}, f32[256,1024]{1,0:T(8,128)}, u32[]{:S(2)}) copy-start(f32[256,1024]{1,0:T(8,128)} %get-tuple-element.84) | copy-start | bytes 3145732
  191.7 88.7 %reduce-scatter.4.cloned.1.call-start = ((), (), s32[]{:S(2)}) async-start(), calls=%async_computation.4 | async-start | bytes 2621440 | tf_op jit(solution)/shard_map/reduce_scatter | solution.py:402
  198.1 36.3 %copy-start.17 = (f32[1024]{0:T(1024)S(1)}, f32[1024]{0:T(1024)}, u32[]{:S(2)}) copy-start(f32[1024]{0:T(1024)} %param.26) | copy-start | bytes 12292
  198.1 82.2 %copy-start.7 = (bf16[256,1024]{1,0:T(8,128)(2,1)S(1)}, bf16[256,1024]{1,0:T(8,128)(2,1)}, u32[]{:S(2)}) copy-start(bf16[256,1024]{1,0:T(8,128)(2,1)} %param.19) | copy-start | bytes 1572868
  198.1 82.2 %copy-start.18 = (f32[1024]{0:T(1024)S(1)}, f32[1024]{0:T(1024)}, u32[]{:S(2)}) copy-start(f32[1024]{0:T(1024)} %param.31) | copy-start | bytes 12292
  198.2 130.9 %all-gather.8.cloned.1.call-start = ((), (), s32[]{:S(2)}) async-start(), calls=%async_computation.7 | async-start | bytes 2621440 | tf_op jit(solution)/shard_map/all_gather | solution.py:430
  280.4 6.1 %copy-start.11 = (f32[2,1024,128]{2,1,0:T(8,128)S(1)}, f32[2,1024,128]{2,1,0:T(8,128)}, u32[]{:S(2)}) copy-start(f32[2,1024,128]{2,1,0:T(8,128)} %get-tuple-element.87) | copy-start | bytes 3145732
  283.6 121.9 %reduce-scatter.8.cloned.1.call-start = ((), (), s32[]{:S(2)}) async-start(), calls=%async_computation.8 | async-start | bytes 2621440 | tf_op jit(solution)/shard_map/reduce_scatter | solution.py:482
  290.7 40.8 %copy-start.15 = (s32[1024]{0:T(1024)S(1)}, s32[1024]{0:T(1024)}, u32[]{:S(2)}) copy-start(s32[1024]{0:T(1024)} %param.18) | copy-start | bytes 12292
  334.0 2.4 copy-start.9
  338.1 2.0 copy-start.10
  340.0 1.4 copy-start.13
  342.2 0.9 copy-start.14
  345.6 2.4 copy-start.9
  349.6 2.0 copy-start.10
  351.6 1.4 copy-start.13
  353.8 0.9 copy-start.14
  362.8 222.0 %all-reduce.5.cloned.1.call-start = ((), (), s32[]{:S(2)}) async-start(), calls=%async_computation.9 | async-start | bytes 25165824 | tf_op jit(solution)/shard_map/psum | solution.py:492
  363.1 6.8 %copy-start.21 = (bf16[1024,1024]{1,0:T(8,128)(2,1)S(1)}, bf16[1024,1024]{1,0:T(8,128)(2,1)}, u32[]{:S(2)}) copy-start(bf16[1024,1024]{1,0:T(8,128)(2,1)} %all-gather.6.cloned.1.call-done) | copy-start | bytes 6291460
  363.1 6.8 %copy-start.23 = (f32[1024,1024]{1,0:T(8,128)S(1)}, f32[1024,1024]{1,0:T(8,128)}, u32[]{:S(2)}) copy-start(f32[1024,1024]{1,0:T(8,128)} %fusion.60) | copy-start | bytes 12582916
  376.6 3.6 copy-start.8
  376.6 3.6 copy-start.20
  383.8 1.0 copy-start.3
  383.8 21.7 %copy-start.16 = (f32[1024]{0:T(1024)S(1)}, f32[1024]{0:T(1024)}, u32[]{:S(2)}) copy-start(f32[1024]{0:T(1024)} %param.20) | copy-start | bytes 12292
  384.9 63.1 %copy-start.6 = (f32[256,1024]{1,0:T(8,128)S(1)}, f32[256,1024]{1,0:T(8,128)}, u32[]{:S(2)}) copy-start(f32[256,1024]{1,0:T(8,128)} %get-tuple-element.199) | copy-start | bytes 3145732
  584.8 3.9 copy-start.12
  584.8 4.9 copy-start.5
  589.7 3.7 copy-start.4
  589.7 5.7 copy-start.1
Sparse Core Ops, SparseCore 0:
  88.7 44.1 all-gather.3
  134.4 44.6 all-gather.5
  191.8 42.5 reduce-scatter.5
  237.2 43.1 reduce-scatter.3
  283.8 45.2 all-gather.7
  362.9 42.5 reduce-scatter.7
  411.2 173.5 all-reduce.4

commit v2 on v1

v2 whole, which is shorter than its diff:
```python
import math

import jax
import jax.numpy as jnp
from jax import lax
from jax.experimental import pallas as pl
from jax.experimental.pallas import tpu as pltpu
from jax.sharding import PartitionSpec as P

HD = 128
EPS = 1e-05
BF = jnp.bfloat16
F32 = jnp.float32
MESH = pl.DeviceIdType.MESH
VMEM = pltpu.VMEM
DMA = pltpu.SemaphoreType.DMA


def mm(left, right):
    return jnp.dot(left, right, preferred_element_type=F32)


def mm_nt(left, right):
    return lax.dot_general(left, right, (((1,), (1,)), ((), ())), preferred_element_type=F32)


def mm_tn(left, right):
    return lax.dot_general(left, right, (((0,), (0,)), ((), ())), preferred_element_type=F32)


class Place:
    def __init__(self):
        self.z = lax.axis_index("mp")
        self.dp = lax.axis_index("dp")
        self.d = lax.rem(self.dp, 8)
        self.base = self.dp - self.d
        self.core = lax.rem(self.d, 2)
        self.bit_x = lax.rem(self.d // 2, 2)
        self.bit_y = self.d // 4
        self.sibling = self.d + 1 - 2 * self.core
        self.step_x = 2 - 4 * self.bit_x
        self.step_y = 4 - 8 * self.bit_y

    def chip(self, i):
        return self.d + (i % 2) * self.step_x + (i // 2) * self.step_y

    def along(self, z):
        return {"dp": self.dp, "mp": z}

    def plane(self, d):
        return {"dp": self.base + d, "mp": self.z}


def remote(src, dst, ss, rs, device):
    return pltpu.make_async_remote_copy(
        src_ref=src, dst_ref=dst, send_sem=ss, recv_sem=rs, device_id=device, device_id_type=MESH
    )


def barrier(devices):
    sem = pltpu.get_barrier_semaphore()
    for device in devices:
        pl.semaphore_signal(sem, 1, device_id=device, device_id_type=MESH)
    return lambda: pl.semaphore_wait(sem, len(devices))


def norm(values):
    mean = jnp.mean(values, -1, keepdims=True)
    centered = values - mean
    var = jnp.mean(centered * centered, -1, keepdims=True)
    scale = lax.rsqrt(var + EPS)
    return centered * scale, scale


class Line:
    def __init__(self, place, view, source, ss, rs, pieces):
        self.p, self.view, self.source, self.ss, self.rs, self.pieces = place, view, source, ss, rs, pieces

    def _copy(self, s, c, target, slot, source=None):
        view = self.view(s, c)
        source = view if source is None else source
        return remote(source, view, self.ss.at[slot, c], self.rs.at[s, c], self.p.along(target))

    def _each(self, c, act):
        z = self.p.z
        for slot, off in enumerate((1, -1, 2, -2)):
            ok = z < 4 - off if off > 0 else z >= -off

            @pl.when(ok)
            def _():
                act(self._copy(z, c, z + off, slot, self.source(c)))

    def send(self, c):
        self._each(c, lambda copy: copy.start())

    def _passed(self, c, act):
        z = self.p.z

        @pl.when(z == 2)
        def _():
            act(self._copy(0, c, 3, 4))

        @pl.when(z == 1)
        def _():
            act(self._copy(3, c, 0, 4))

    def order(self, k):
        return lax.rem(self.p.z + k * (1 - 2 * (self.p.z // 2)) + 4, 4)

    def take(self, k):
        s = self.order(k)
        for c in range(self.pieces):
            self._copy(s, c, self.p.z, 0).wait_recv()
            if k == 2:
                self._passed(c, lambda copy: copy.start())
        return s

    def finish(self):
        for c in range(self.pieces):
            self._each(c, lambda copy: copy.wait_send())
            self._passed(c, lambda copy: copy.wait_send())


class Plane:
    def __init__(self, place, view, ss, rs):
        self.p, self.view, self.ss, self.rs = place, view, ss, rs

    def _own(self, i):
        p = self.p
        to = p.sibling if i == 0 else p.chip(i)
        return remote(self.view(p.d), self.view(p.d), self.ss.at[i], self.rs.at[i], p.plane(to))

    def _second(self, i, who):
        p = self.p
        return remote(self.view(who), self.view(who), self.ss.at[3 + i], self.rs.at[3 + i], p.plane(p.sibling))

    def send(self):
        for i in (1, 2, 3, 0):
            self._own(i).start()

    def take(self, i):
        p = self.p
        who = p.sibling if i == 0 else p.chip(i)
        remote(self.view(who), self.view(who), self.ss.at[i], self.rs.at[i], p.plane(p.d)).wait_recv()
        if i:
            self._second(i, who).start()

    def take_second(self, i):
        p = self.p
        who = p.chip(i) + p.sibling - p.d
        self._second(i, who).wait_recv()

    def finish(self):
        for i in range(4):
            self._own(i).wait_send()
            if i:
                self._second(i, self.p.chip(i)).wait_send()


def softmax_block(mixed, h, r, share, rows, segc, segr, factor):
    width = (r + 1) * rows
    top = r * rows
    q = mixed[top : top + rows, h * HD : (h + 1) * HD]
    k = mixed[0:width, share + h * HD : share + (h + 1) * HD]
    scores = mm_nt(q, k) * factor
    place_q = top + lax.broadcasted_iota(jnp.int32, (rows, width), 0)
    place_k = lax.broadcasted_iota(jnp.int32, (rows, width), 1)
    allowed = (segc[top : top + rows, :] == segr[:, 0:width]) & (place_q >= place_k)
    return jnp.where(allowed, scores, -1e30)


GELU_A = 0.7978845608
GELU_B = 0.044715


def gelu_parts(v):
    square = v * v
    t = jnp.tanh(GELU_A * v * (1.0 + GELU_B * square))
    half = 0.5 * (1.0 + t)
    slope = half + 0.5 * v * (1.0 - t * t) * (GELU_A * (1.0 + 3.0 * GELU_B * square))
    return v * half, slope


def front(
    x_ref, cot, segr, segc, g1, b1, wq, bq, ow, ob, g2, b2, upw, upb, dww, dwb,
    first_out, mixed_out, own_out, lse_out, dctx_out, ug_out, owg_out, output, dmid_out, dg_out, ubg_out, small_out,
    first, mixed, own, ctx, outw, lse, up, down, ub, dy, second, hidden, dpre,
    ds_part, ds_got, ds_sum, ds_in, o_part, o_got, o_sum, o_in, dg, dg_in, ug, owg, dcs, dctx,
    ss_first, rs_first, ss_ctx, rs_ctx, ss_wz, rs_wz, ss_wp, rs_wp, ss_cot, rs_cot, ss_up, rs_up, ss_dn, rs_dn,
    ss_ub, rs_ub, ss_sec, rs_sec, ss_dg, rs_dg, ss_ds, rs_ds, ss_do, rs_do, ss_og, rs_og, ss_oo, rs_oo,
    ss_dc, rs_dc, sem_out, sem_in,
):
    p = Place()
    z = p.z
    rows, width = x_ref.shape
    share = wq.shape[2]
    heads = share // HD
    factor = 1.0 / math.sqrt(HD)
    slab = ow.shape[0] // 8
    part = upw.shape[1] // 8
    others = [lax.rem(z + k, 4) for k in (1, 2, 3)]
    enter = barrier([p.along(t) for t in others] + [p.plane(p.chip(i)) for i in (1, 2, 3)] + [p.plane(p.sibling)])
    half = rows // 2
    line = Line(
        p, lambda s, c: first.at[s, pl.ds(c * half, half)], lambda c: first.at[z, pl.ds(c * half, half)],
        ss_first, rs_first, 2,
    )

    def first_norm(c):
        block = x_ref[c * half : (c + 1) * half, :].astype(F32)
        normed, _ = norm(block)
        first[pl.ds(z, 1), c * half : (c + 1) * half, :] = (normed * g1[...] + b1[...]).astype(BF)[None]

    first_norm(0)
    enter()
    line.send(0)
    first_norm(1)
    line.send(1)

    mine = pl.ds(pl.multiple_of(p.d * slab, slab), slab)

    def slab_z(k, t):
        return remote(ow.at[mine], outw.at[z, mine], ss_wz.at[k], rs_wz.at[z], p.along(t))

    for k, t in enumerate(others):
        slab_z(k, t).start()
    outw[pl.ds(z, 1), mine] = ow[mine, :][None]
    slabs = Plane(p, lambda who: outw.at[:, pl.ds(who * slab, slab)], ss_wp, rs_wp)
    dy[pl.ds(p.d, 1)] = cot[...][None]
    grads = Plane(p, lambda who: dy.at[who], ss_cot, rs_cot)
    grads.send()

    def project(s):
        for t in range(3):
            part = mm(first[pl.ds(s, 1)][0], wq[t]) + bq[t : t + 1, :]
            mixed[pl.ds(pl.multiple_of(s * rows, rows), rows), t * share : (t + 1) * share] = part.astype(BF)

    project(z)
    for k in (1, 2):
        project(line.take(k))
    for t in others:
        remote(outw.at[t, mine], outw.at[t, mine], ss_wz.at[0], rs_wz.at[t], p.along(z)).wait_recv()
    slabs.send()

    mine_part = pl.ds(pl.multiple_of(p.d * part, part), part)

    def up_view(s):
        return up.at[:, pl.ds(pl.multiple_of(s * part, part), part)]

    def down_view(s):
        return down.at[pl.ds(pl.multiple_of(s * part, part), part)]

    def up_copy(k, s, t):
        return remote(upw.at[:, mine_part], up_view(s), ss_up.at[k], rs_up.at[s], p.along(t))

    def down_copy(k, s, t):
        return remote(dww.at[mine_part], down_view(s), ss_dn.at[k], rs_dn.at[s], p.along(t))

    def bias_copy(k, s, t):
        return remote(upb.at[p.d], ub.at[s], ss_ub.at[k], rs_ub.at[s], p.along(t))

    local_in = [
        pltpu.make_async_copy(upw.at[:, mine_part], up_view(z), sem_in.at[0]),
        pltpu.make_async_copy(dww.at[mine_part], down_view(z), sem_in.at[1]),
        pltpu.make_async_copy(upb.at[p.d], ub.at[z], sem_in.at[2]),
    ]
    for copy in local_in:
        copy.start()
    for k, t in enumerate(others):
        bias_copy(k, z, t).start()
        up_copy(k, z, t).start()
    project(line.take(3))

    def ctx_send(r):
        return remote(own.at[r], ctx.at[z], ss_ctx.at[r], rs_ctx.at[z], p.along(r))

    for r in reversed(range(4)):
        for h in range(heads):
            scores = softmax_block(mixed, h, r, share, rows, segc, segr, factor)
            peak = jnp.max(scores, -1, keepdims=True)
            expo = jnp.exp(scores - peak)
            total = jnp.sum(expo, -1, keepdims=True)
            probs = (expo / total).astype(BF)
            v = mixed[0 : (r + 1) * rows, 2 * share + h * HD : 2 * share + (h + 1) * HD]
            own[r, :, h * HD : (h + 1) * HD] = mm(probs, v).astype(BF)
            lse[h, r * rows : (r + 1) * rows, :] = jnp.broadcast_to(peak + jnp.log(total), (rows, HD))

        @pl.when(z != r)
        def _():
            ctx_send(r).start()

        @pl.when(z == r)
        def _():
            ctx[r] = own[r]

        if r == 3:
            for i in (1, 2, 3):
                slabs.take(i)
        if r == 2:
            for i in (1, 2, 3):
                grads.take(i)
    for k, t in enumerate(others):
        down_copy(k, z, t).start()
    outs = [
        pltpu.make_async_copy(a, b, sem_out.at[i])
        for i, (a, b) in enumerate(((first, first_out), (mixed, mixed_out), (own, own_out), (lse, lse_out)))
    ]
    for copy in outs:
        copy.start()
    slabs.take(0)
    for i in (1, 2, 3):
        slabs.take_second(i)
    attended = mm(ctx[pl.ds(z, 1)][0], outw[pl.ds(z, 1)][0])
    for t in others:
        remote(own.at[0], ctx.at[t], ss_ctx.at[0], rs_ctx.at[t], p.along(z)).wait_recv()
        attended = attended + mm(ctx[pl.ds(t, 1)][0], outw[pl.ds(t, 1)][0])
    middle = x_ref[...].astype(F32) + (attended + ob[...])
    dmid_out[...] = middle
    normed, _ = norm(middle)
    second[pl.ds(p.d, 1)] = (normed * g2[...] + b2[...]).astype(BF)[None]
    seconds = Plane(p, lambda who: second.at[who], ss_sec, rs_sec)
    seconds.send()

    grads.take(0)
    for i in (1, 2, 3):
        grads.take_second(i)
    for copy in local_in:
        copy.wait()
    for k, t in enumerate(others):
        bias_copy(k, t, z).wait_recv()
        up_copy(k, t, z).wait_recv()
        down_copy(k, t, z).wait_recv()
    up_bias = jnp.concatenate([ub[q] for q in range(4)], 1)

    def give(parts, got, ss, rs, i):
        return remote(parts.at[i, 1 - p.core], got.at[i], ss.at[i], rs.at[i], p.plane(p.sibling))

    def ship(sums, into, ss, rs, i):
        return remote(sums.at[i - 1], into.at[i - 1], ss.at[i - 1], rs.at[i - 1], p.plane(p.chip(i)))

    def summed(parts, got, i):
        return parts[pl.ds(i, 1), pl.ds(p.core, 1)][0, 0].astype(F32) + got[pl.ds(i, 1)][0].astype(F32)

    def feed(i, carry):
        @pl.when(i == 0)
        def _():
            seconds.take(0)

        @pl.when(i > 0)
        def _():
            who = p.chip(i)
            seconds_take(i)
            other = who + p.sibling - p.d
            seconds._second(i, other).wait_recv()

        pair = pl.ds(p.chip(i) - p.core, 2)
        tokens = second[pair].reshape(2 * rows, width)
        pre = mm(tokens, up[...]) + up_bias
        value, slope = gelu_parts(pre)
        value = value.astype(BF)
        hidden[pair] = value.reshape(2, rows, 4 * part)
        back = mm_nt(dy[pair].reshape(2 * rows, width), down[...])
        back = (back * slope).astype(BF)
        dpre[pair] = back.reshape(2, rows, 4 * part)
        ds_part[pl.ds(i, 1)] = mm_nt(back, up[...]).astype(BF).reshape(1, 2, rows, width)
        give(ds_part, ds_got, ss_ds, rs_ds, i).start()
        o_part[pl.ds(i, 1)] = mm(value, down[...]).astype(BF).reshape(1, 2, rows, width)
        give(o_part, o_got, ss_do, rs_do, i).start()
        give(ds_part, ds_got, ss_ds, rs_ds, i).wait_recv()

        @pl.when(i > 0)
        def _():
            ds_sum[pl.ds(i - 1, 1)] = summed(ds_part, ds_got, i).astype(BF)[None]
            ship(ds_sum, ds_in, ss_og, rs_og, i).start()

        return carry

    def seconds_take(i):
        who = p.chip(i)
        remote(second.at[who], second.at[who], ss_sec.at[i], rs_sec.at[i], p.plane(p.d)).wait_recv()
        seconds._second(i, who).start()

    lax.fori_loop(0, 4, feed, 0)
    for i in range(4):
        give(o_part, o_got, ss_do, rs_do, i).wait_recv()
        if i:
            o_sum[i - 1] = summed(o_part, o_got, i).astype(BF)
            ship(o_sum, o_in, ss_oo, rs_oo, i).start()

    def quarter(q):
        return pl.ds(pl.multiple_of(q * part, part), part)

    def dg_copy(k, s, t):
        return remote(dg.at[quarter(t)], dg_in.at[k], ss_dg.at[k], rs_dg.at[k], p.along(t))

    all_dy = dy[...].reshape(8 * rows, width)
    for c in range(2):
        cols = slice(c * 2 * part, (c + 1) * 2 * part)
        dg[cols, :] = mm_tn(hidden[:, :, cols].reshape(8 * rows, 2 * part), all_dy).astype(BF)
    for k, t in enumerate(others):
        dg_copy(k, z, t).start()

    total = summed(ds_part, ds_got, 0)
    for i in (1, 2, 3):
        ship(ds_sum, ds_in, ss_og, rs_og, i).wait_recv()
        total = total + ds_in[i - 1].astype(F32)
    middle = dmid_out[...]
    normed, scale = norm(middle)
    grad = cot[...].astype(F32)
    scaled = total * g2[...]
    dmiddle = grad + scale * (
        scaled - jnp.mean(scaled, -1, keepdims=True) - normed * jnp.mean(scaled * normed, -1, keepdims=True)
    )
    low = dmiddle.astype(BF)
    for t in range(4):
        dcs[t] = mm_nt(low, outw[t]).astype(BF)

    def dc_copy(k, t):
        return remote(dcs.at[t], dctx.at[z], ss_dc.at[k], rs_dc.at[z], p.along(t))

    for k, t in enumerate(others):
        dc_copy(k, t).start()
    dctx[pl.ds(z, 1)] = dcs[pl.ds(z, 1)]
    small_out[...] = jnp.concatenate(
        [
            jnp.sum(total * normed, 0, keepdims=True), jnp.sum(total, 0, keepdims=True),
            jnp.sum(low.astype(F32), 0, keepdims=True), jnp.sum(grad, 0, keepdims=True),
            jnp.zeros((4, width), F32),
        ],
        0,
    )
    for t in range(4):
        owg[t] = mm_tn(ctx[t], low).astype(BF)
    all_dpre = dpre[...].reshape(8 * rows, 4 * part)
    ubg_out[...] = jnp.sum(all_dpre.astype(F32), 0, keepdims=True)
    for c in range(4):
        cols = slice(c * width // 4, (c + 1) * width // 4)
        ug[cols, :] = mm_tn(second[:, :, cols].reshape(8 * rows, width // 4), all_dpre).astype(BF)
    late = [
        pltpu.make_async_copy(a, b, sem_out.at[4 + i])
        for i, (a, b) in enumerate(((ug, ug_out), (owg, owg_out)))
    ]
    for copy in late:
        copy.start()
    reduced = summed(o_part, o_got, 0)
    for i in (1, 2, 3):
        ship(o_sum, o_in, ss_oo, rs_oo, i).wait_recv()
        reduced = reduced + o_in[i - 1].astype(F32)
    output[...] = (middle + (reduced + dwb[...])).astype(BF)
    dmid_out[...] = dmiddle
    down_sum = dg[quarter(z), :].astype(F32)
    for k in range(3):
        dg_copy(k, z, z).wait_recv()
        down_sum = down_sum + dg_in[k].astype(F32)
    dg_out[...] = down_sum.astype(BF)
    for k, t in enumerate(others):
        remote(dcs.at[0], dctx.at[t], ss_dc.at[k], rs_dc.at[t], p.along(z)).wait_recv()
    last = pltpu.make_async_copy(dctx, dctx_out, sem_out.at[6])
    last.start()

    line.finish()
    slabs.finish()
    grads.finish()
    seconds.finish()
    for k, t in enumerate(others):
        slab_z(k, t).wait_send()
        bias_copy(k, z, t).wait_send()
        up_copy(k, z, t).wait_send()
        down_copy(k, z, t).wait_send()
        dg_copy(k, z, t).wait_send()
        dc_copy(k, t).wait_send()
    for r in range(4):

        @pl.when(z != r)
        def _():
            ctx_send(r).wait_send()

        give(ds_part, ds_got, ss_ds, rs_ds, r).wait_send()
        give(o_part, o_got, ss_do, rs_do, r).wait_send()
        if r:
            ship(ds_sum, ds_in, ss_og, rs_og, r).wait_send()
            ship(o_sum, o_in, ss_oo, rs_oo, r).wait_send()
    for copy in outs + late + [last]:
        copy.wait()


def run_front(x, cot, seg_ids, g1, b1, wq, bq, ow, ob, g2, b2, upw, upb, dww, dwb):
    rows, width = x.shape
    share = wq.shape[2]
    length = 4 * rows
    vm = pl.BlockSpec(memory_space=VMEM)
    hbm = pl.BlockSpec(memory_space=pl.ANY)
    heads = share // HD
    part = upw.shape[1] // 8
    outs = [
        (hbm, (4, rows, width), BF), (hbm, (length, 3 * share), BF), (hbm, (4, rows, share), BF),
        (hbm, (heads, length, HD), F32), (hbm, (4, rows, share), BF), (hbm, (width, 4 * part), BF),
        (hbm, (4, share, width), BF), (vm, (rows, width), BF), (vm, (rows, width), F32), (vm, (part, width), BF),
        (vm, (1, 4 * part), F32), (vm, (8, width), F32),
    ]
    token = (rows, width)
    return pl.pallas_call(
        front,
        out_shape=[jax.ShapeDtypeStruct(s, t) for _, s, t in outs],
        in_specs=[vm] * 12 + [hbm, vm, hbm, vm],
        out_specs=[m for m, _, _ in outs],
        scratch_shapes=[
            VMEM((4,) + token, BF), VMEM((length, 3 * share), BF), VMEM((4, rows, share), BF),
            VMEM((4, rows, share), BF), VMEM((4, share, width), BF), VMEM((heads, length, HD), F32),
            VMEM((width, 4 * part), BF), VMEM((4 * part, width), BF), VMEM((4, 1, part), F32),
            VMEM((8,) + token, BF), VMEM((8,) + token, BF), VMEM((8, rows, 4 * part), BF), VMEM((8, rows, 4 * part), BF),
            VMEM((4, 2) + token, BF), VMEM((4,) + token, BF), VMEM((3,) + token, BF), VMEM((3,) + token, BF),
            VMEM((4, 2) + token, BF), VMEM((4,) + token, BF), VMEM((3,) + token, BF), VMEM((3,) + token, BF),
            VMEM((4 * part, width), BF), VMEM((3, part, width), BF), VMEM((width, 4 * part), BF),
            VMEM((4, share, width), BF), VMEM((4, rows, share), BF), VMEM((4, rows, share), BF),
            DMA((5, 2)), DMA((4, 2)), DMA((4,)), DMA((4,)), DMA((3,)), DMA((4,)),
            DMA((7,)), DMA((7,)), DMA((7,)), DMA((7,)), DMA((3,)), DMA((4,)), DMA((3,)), DMA((4,)),
            DMA((3,)), DMA((4,)), DMA((7,)), DMA((7,)), DMA((3,)), DMA((3,)), DMA((4,)), DMA((4,)),
            DMA((4,)), DMA((4,)), DMA((3,)), DMA((3,)), DMA((3,)), DMA((3,)), DMA((3,)), DMA((4,)),
            DMA((7,)), DMA((3,)),
        ],
        compiler_params=pltpu.CompilerParams(collective_id=0, has_side_effects=True, vmem_limit_bytes=63 << 20),
        name="front",
    )(
        x, cot, seg_ids.reshape(1, length), seg_ids.reshape(length, 1), g1.reshape(1, width), b1.reshape(1, width),
        wq, bq, ow, ob.reshape(1, width), g2.reshape(1, width), b2.reshape(1, width),
        upw, upb.reshape(8, 1, part), dww, dwb.reshape(1, width),
    )


class PlaneSum:
    def __init__(self, place, view, got, sums, into, ss, rs):
        self.p, self.view, self.got, self.sums, self.into, self.ss, self.rs = place, view, got, sums, into, ss, rs

    def _give(self, i):
        p = self.p
        who = p.chip(i) + p.sibling - p.d
        return remote(self.view(who), self.got.at[i], self.ss.at[i], self.rs.at[i], p.plane(p.sibling))

    def _ship(self, i):
        p = self.p
        return remote(
            self.sums.at[i - 1], self.into.at[i - 1], self.ss.at[3 + i], self.rs.at[3 + i], p.plane(p.chip(i))
        )

    def give(self):
        for i in (1, 2, 3, 0):
            self._give(i).start()

    def _both(self, i):
        return self.view(self.p.chip(i))[...].astype(F32) + self.got[i].astype(F32)

    def ship(self):
        for i in (1, 2, 3):
            self._give(i).wait_recv()
            self.sums[i - 1] = self._both(i).astype(BF)
            self._ship(i).start()

    def total(self):
        self._give(0).wait_recv()
        total = self._both(0)
        for i in (1, 2, 3):
            self._ship(i).wait_recv()
            total = total + self.into[i - 1].astype(F32)
        return total

    def finish(self):
        for i in range(4):
            self._give(i).wait_send()
            if i:
                self._ship(i).wait_send()


def rear(
    first, mixed, own, lse, dctx, segr, segc, wq, x_ref, dmid, g1, ug, dg, owg, ubg, small,
    tokens_grad, small_out, pg_out, pb_out, owg_out, upg_out, ubg_out, dng_out,
    acc, dmixed, delta, parts, in_end, in_mid, fwd, pg, pg_got, pg_sum, pg_in, pga, pb, dga, uga, uba, oga,
    og_got, og_sum, og_in, ogz, ogz_in, ug_in, ub_in, sm, sm_in, smp, pg_f, owg_f, upg_f, dng_f,
    ss_dg, rs_dg, ss_og, rs_og, ss_oz, rs_oz, ss_oa, rs_oa, ss_ug, rs_ug, ss_ua, rs_ua, ss_ub, rs_ub, ss_ba, rs_ba,
    ss_pg, rs_pg, ss_pa, rs_pa, ss_pb, rs_pb, ss_end, rs_end, ss_mid, rs_mid, ss_sm, rs_sm, ss_sp, rs_sp, sem_out,
):
    p = Place()
    z = p.z
    rows, width = x_ref.shape
    share = wq.shape[2]
    heads = share // HD
    factor = 1.0 / math.sqrt(HD)
    slab = owg.shape[1] // 8
    part = dg.shape[0]
    line = width // 8
    others = [lax.rem(z + k, 4) for k in (1, 2, 3)]
    enter = barrier([p.along(t) for t in others] + [p.plane(p.chip(i)) for i in (1, 2, 3)] + [p.plane(p.sibling)])
    low_half = 1 - z // 2
    inner = lax.rem(z + 1, 4) // 2
    toward = z + 2 * low_half - 1
    outward = z + 1 - 2 * low_half

    for h in range(heads):
        cols = slice(h * HD, (h + 1) * HD)
        product = dctx[:, :, cols].astype(F32) * own[:, :, cols].astype(F32)
        delta[h] = jnp.broadcast_to(jnp.sum(product, -1, keepdims=True).reshape(4 * rows, 1), (4 * rows, HD))
    for t in range(3):
        acc[t] = jnp.zeros((4 * rows, share), F32)
    enter()

    down_all = Plane(p, lambda who: dga.at[who], ss_dg, rs_dg)
    dga[pl.ds(p.d, 1)] = dg[...][None]
    down_all.send()
    out_sum = PlaneSum(p, lambda who: owg.at[:, pl.ds(who * slab, slab)], og_got, og_sum, og_in, ss_og, rs_og)
    out_sum.give()

    def quarter(q):
        return pl.ds(pl.multiple_of(q * part, part), part)

    def ug_copy(k, t):
        return remote(ug.at[:, quarter(t)], ug_in.at[k], ss_ug.at[k], rs_ug.at[k], p.along(t))

    def ub_copy(k, t):
        return remote(ubg.at[t], ub_in.at[k], ss_ub.at[k], rs_ub.at[k], p.along(t))

    for k, t in enumerate(others):
        ub_copy(k, t).start()
        ug_copy(k, t).start()

    pieces = 4
    piece = rows // pieces

    def chunk(c):
        return pl.ds(c * piece, piece)

    def from_end(g, c):
        return remote(
            parts.at[g, chunk(c)], in_end.at[g, chunk(c)], ss_end.at[g, c], rs_end.at[g, c], p.along(toward)
        )

    def from_mid(g, c):
        return remote(
            fwd.at[g, chunk(c)], in_mid.at[g, chunk(c)], ss_mid.at[g, c], rs_mid.at[g, c], p.along(toward)
        )

    def to_end(c):
        return remote(fwd.at[2, chunk(c)], in_end.at[0, chunk(c)], ss_mid.at[2, c], rs_end.at[0, c], p.along(outward))

    def strip(index):
        return pl.ds(pl.multiple_of(index * rows, rows), rows)

    for g in range(4):

        def block(e, carry):
            i = (g + e) + low_half * (3 - g - (g + e))
            j = g + low_half * (3 - (g + e) - g)
            qs, ks = strip(i), strip(j)
            place_q = i * rows + lax.broadcasted_iota(jnp.int32, (rows, rows), 0)
            place_k = j * rows + lax.broadcasted_iota(jnp.int32, (rows, rows), 1)
            allowed = (segc[qs, :] == segr[:, ks]) & (place_q >= place_k)
            for h in range(heads):
                cols = slice(h * HD, (h + 1) * HD)
                q = mixed[qs, cols]
                k = mixed[ks, share + h * HD : share + (h + 1) * HD]
                v = mixed[ks, 2 * share + h * HD : 2 * share + (h + 1) * HD]
                up = dctx[pl.ds(i, 1), :, cols][0]
                scores = jnp.where(allowed, mm_nt(q, k) * factor, -1e30)
                probs = jnp.exp(scores - lse[h, qs, 0:1])
                acc[2, ks, cols] += mm_tn(probs.astype(BF), up)
                back = (probs * (mm_nt(up, v) - delta[h, qs, 0:1])).astype(BF)
                acc[0, qs, cols] += mm(back, k)
                acc[1, ks, cols] += mm_tn(back, q)
            return carry

        lax.fori_loop(0, 4 - g, block, 0)
        r = g + low_half * (3 - 2 * g)
        total = None
        for t in range(3):
            value = acc[t, strip(r), :]
            low = (value * factor if t < 2 else value).astype(BF)
            dmixed[strip(r), t * share : (t + 1) * share] = low
            term = mm_nt(low, wq[t])
            total = term if total is None else total + term
        parts[g] = total.astype(BF)
        if g < 3:

            @pl.when(inner == 0)
            def _():
                for c in range(pieces):
                    from_end(g, c).start()

        if g == 1:
            out_sum.ship()

    whole = first[...].reshape(4 * rows, width)
    for t in range(3):
        cols = slice(t * share, (t + 1) * share)
        pg[:, cols] = mm_tn(whole, dmixed[:, cols]).astype(BF)
    pb[pl.ds(p.d, 1)] = jnp.sum(dmixed[...].astype(F32), 0, keepdims=True)[None]
    pg_sums = PlaneSum(p, lambda who: pg.at[pl.ds(pl.multiple_of(who * line, line), line)], pg_got, pg_sum, pg_in, ss_pg, rs_pg)
    pg_sums.give()
    pb_all = Plane(p, lambda who: pb.at[who], ss_pb, rs_pb)
    pb_all.send()
    pg_sums.ship()

    @pl.when(inner == 1)
    def _():
        for c in range(pieces):
            from_end(0, c).wait_recv()
            fwd[0, chunk(c)] = (parts[0, chunk(c)].astype(F32) + in_end[0, chunk(c)].astype(F32)).astype(BF)
            from_mid(0, c).start()
        for c in range(pieces):
            from_mid(0, c).wait_recv()
            fwd[2, chunk(c)] = (parts[3, chunk(c)].astype(F32) + in_mid[0, chunk(c)].astype(F32)).astype(BF)
            to_end(c).start()

    og_total = out_sum.total().astype(BF)
    ogz[...] = og_total

    def oz_copy(k, t):
        return remote(ogz.at[t], ogz_in.at[k], ss_oz.at[k], rs_oz.at[k], p.along(t))

    for k, t in enumerate(others):
        oz_copy(k, t).start()
    for i in (1, 2, 3):
        down_all.take(i)
        pb_all.take(i)
    up_sum = ug[:, quarter(z)].astype(F32)
    ub_sum = ubg[pl.ds(z, 1)][0]
    for k, t in enumerate(others):
        ug_copy(k, t).wait_recv()
        ub_copy(k, t).wait_recv()
        up_sum = up_sum + ug_in[k].astype(F32)
        ub_sum = ub_sum + ub_in[k]
    uga[pl.ds(p.d, 1)] = up_sum.astype(BF)[None]
    uba[pl.ds(p.d, 1)] = ub_sum[None]
    up_all = Plane(p, lambda who: uga.at[who], ss_ua, rs_ua)
    ub_all = Plane(p, lambda who: uba.at[who], ss_ba, rs_ba)
    pg_all = Plane(p, lambda who: pga.at[who], ss_pa, rs_pa)
    pga[pl.ds(p.d, 1)] = pg_sums.total().astype(BF)[None]
    pg_all.send()
    up_all.send()
    ub_all.send()

    @pl.when(inner == 1)
    def _():
        for c in range(pieces):
            from_end(1, c).wait_recv()
            fwd[1, chunk(c)] = (parts[1, chunk(c)].astype(F32) + in_end[1, chunk(c)].astype(F32)).astype(BF)
            from_mid(1, c).start()

    down_all.take(0)
    pb_all.take(0)
    for i in (1, 2, 3):
        down_all.take_second(i)
        pb_all.take_second(i)
    for who in range(8):
        dng_f[who * part : (who + 1) * part, :] = dga[who].astype(F32)
    pb_out[...] = jnp.sum(pb[...], 0)
    out_copies = [pltpu.make_async_copy(dng_f, dng_out, sem_out.at[0])]
    out_copies[0].start()
    oz_sum = ogz[pl.ds(z, 1)][0].astype(F32)
    for k, t in enumerate(others):
        oz_copy(k, t).wait_recv()
        oz_sum = oz_sum + ogz_in[k].astype(F32)
    oga[pl.ds(p.d, 1)] = oz_sum.astype(BF)[None]
    og_all = Plane(p, lambda who: oga.at[who], ss_oa, rs_oa)
    og_all.send()
    block_x = x_ref[...].astype(F32)
    normed, scale = norm(block_x)
    for i in (1, 2, 3):
        pg_all.take(i)

    @pl.when(inner == 0)
    def _():
        for c in range(pieces):
            to_end(c).wait_recv()
        acc[0, 0:rows, :] = (parts[3, :, 0:share].astype(F32) + in_end[0, :, 0:share].astype(F32))
        acc[0, rows : 2 * rows, :] = parts[3, :, share : 2 * share].astype(F32) + in_end[0, :, share : 2 * share].astype(F32)
        acc[0, 2 * rows : 3 * rows, :] = (
            parts[3, :, 2 * share : 3 * share].astype(F32) + in_end[0, :, 2 * share : 3 * share].astype(F32)
        )
        acc[0, 3 * rows : 4 * rows, :] = parts[3, :, 3 * share :].astype(F32) + in_end[0, :, 3 * share :].astype(F32)

    @pl.when(inner == 1)
    def _():
        for c in range(pieces):
            from_end(2, c).wait_recv()
            from_mid(1, c).wait_recv()
        for n in range(4):
            cols = slice(n * share, (n + 1) * share)
            acc[0, n * rows : (n + 1) * rows, :] = (
                parts[2, :, cols].astype(F32) + in_end[2, :, cols].astype(F32) + in_mid[1, :, cols].astype(F32)
            )

    total = jnp.concatenate([acc[0, n * rows : (n + 1) * rows, :] for n in range(4)], 1)
    scaled = total * g1[...]
    back = scale * (
        scaled - jnp.mean(scaled, -1, keepdims=True) - normed * jnp.mean(scaled * normed, -1, keepdims=True)
    )
    tokens_grad[...] = (dmid[...] + back).astype(BF)
    sm[...] = jnp.concatenate(
        [
            small[0:4, :], jnp.sum(total * normed, 0, keepdims=True), jnp.sum(total, 0, keepdims=True),
            jnp.zeros((2, width), F32),
        ],
        0,
    )

    def sm_copy(k, t):
        return remote(sm, sm_in.at[k], ss_sm.at[k], rs_sm.at[k], p.along(t))

    for k, t in enumerate(others):
        sm_copy(k, t).start()
    for i in (1, 2, 3):
        up_all.take(i)
        ub_all.take(i)
        og_all.take(i)
    sm_sum = sm[...]
    for k, t in enumerate(others):
        sm_copy(k, t).wait_recv()
        sm_sum = sm_sum + sm_in[k]
    smp[pl.ds(p.d, 1)] = sm_sum[None]
    sm_all = Plane(p, lambda who: smp.at[who], ss_sp, rs_sp)
    sm_all.send()

    pg_all.take(0)
    for i in (1, 2, 3):
        pg_all.take_second(i)
    for t in range(3):
        for who in range(8):
            pg_f[t, who * line : (who + 1) * line, :] = pga[who, :, t * share : (t + 1) * share].astype(F32)
    out_copies.append(pltpu.make_async_copy(pg_f, pg_out, sem_out.at[1]))
    out_copies[-1].start()
    for i in (1, 2, 3):
        sm_all.take(i)
    up_all.take(0)
    ub_all.take(0)
    og_all.take(0)
    for i in (1, 2, 3):
        up_all.take_second(i)
        ub_all.take_second(i)
        og_all.take_second(i)
    for who in range(8):
        upg_f[:, who * part : (who + 1) * part] = uga[who].astype(F32)
        ubg_out[:, who * part : (who + 1) * part] = uba[who]
    out_copies.append(pltpu.make_async_copy(upg_f, upg_out, sem_out.at[2]))
    out_copies[-1].start()
    for who in range(8):
        owg_f[who * slab : (who + 1) * slab, :] = oga[who].astype(F32)
    out_copies.append(pltpu.make_async_copy(owg_f, owg_out, sem_out.at[3]))
    out_copies[-1].start()
    sm_all.take(0)
    for i in (1, 2, 3):
        sm_all.take_second(i)
    small_out[...] = jnp.sum(smp[...], 0)

    for group in (down_all, out_sum, pg_sums, pb_all, up_all, ub_all, pg_all, og_all, sm_all):
        group.finish()
    for k, t in enumerate(others):
        ug_copy(k, t).wait_send()
        ub_copy(k, t).wait_send()
        oz_copy(k, t).wait_send()
        sm_copy(k, t).wait_send()

    @pl.when(inner == 0)
    def _():
        for g in range(3):
            for c in range(pieces):
                from_end(g, c).wait_send()

    @pl.when(inner == 1)
    def _():
        for c in range(pieces):
            from_mid(0, c).wait_send()
            from_mid(1, c).wait_send()
            to_end(c).wait_send()

    for copy in out_copies:
        copy.wait()


def run_rear(first, mixed, own, lse, dctx, seg_ids, wq, x, dmid, g1, ug, dg, owg, ubg, small):
    rows, width = x.shape
    share = wq.shape[2]
    length = 4 * rows
    heads = share // HD
    part = dg.shape[0]
    slab = share // 8
    line = width // 8
    vm = pl.BlockSpec(memory_space=VMEM)
    hbm = pl.BlockSpec(memory_space=pl.ANY)
    outs = [
        (vm, (rows, width), BF), (vm, (8, width), F32), (hbm, (3, width, share), F32), (vm, (1, 3 * share), F32),
        (hbm, (share, width), F32), (hbm, (width, 8 * part), F32), (vm, (1, 8 * part), F32), (hbm, (8 * part, width), F32),
    ]
    token = (rows, width)
    seven = [DMA((7,)), DMA((7,))]
    three = [DMA((3,)), DMA((3,))]
    return pl.pallas_call(
        rear,
        out_shape=[jax.ShapeDtypeStruct(s, t) for _, s, t in outs],
        in_specs=[vm] * 16,
        out_specs=[m for m, _, _ in outs],
        scratch_shapes=[
            VMEM((3, length, share), F32), VMEM((length, 3 * share), BF), VMEM((heads, length, HD), F32),
            VMEM((4,) + token, BF), VMEM((3,) + token, BF), VMEM((2,) + token, BF), VMEM((3,) + token, BF),
            VMEM((width, 3 * share), BF), VMEM((4, line, 3 * share), BF), VMEM((3, line, 3 * share), BF),
            VMEM((3, line, 3 * share), BF), VMEM((8, line, 3 * share), BF), VMEM((8, 1, 3 * share), F32),
            VMEM((8, part, width), BF), VMEM((8, width, part), BF), VMEM((8, 1, part), F32), VMEM((8, slab, width), BF),
            VMEM((4, 4, slab, width), BF), VMEM((3, 4, slab, width), BF), VMEM((3, 4, slab, width), BF),
            VMEM((4, slab, width), BF), VMEM((3, slab, width), BF), VMEM((3, width, part), BF), VMEM((3, 1, part), F32),
            VMEM((8, width), F32), VMEM((3, 8, width), F32), VMEM((8, 8, width), F32),
            VMEM((3, width, share), F32), VMEM((share, width), F32), VMEM((width, 8 * part), F32), VMEM((8 * part, width), F32),
        ]
        + seven + seven + three + seven + three + seven + three + seven
        + seven + seven + seven + [DMA((3, 4)), DMA((3, 4)), DMA((3, 4)), DMA((2, 4))] + three + seven + [DMA((4,))],
        compiler_params=pltpu.CompilerParams(collective_id=1, has_side_effects=True, vmem_limit_bytes=63 << 20),
        name="rear",
    )(
        first, mixed, own, lse, dctx, seg_ids.reshape(1, length), seg_ids.reshape(length, 1), wq, x, dmid,
        g1.reshape(1, width), ug, dg, owg, ubg.reshape(4, 1, part), small,
    )


def shards(
    tokens, seg_ids, cotangent, first_gain, first_shift, project_weight, project_bias, out_weight, out_bias,
    second_gain, second_shift, up_weight, up_bias, down_weight, down_bias,
):
    first, mixed, own, lse, dctx, ug, owg, output, dmid, dg, ubg, small = run_front(
        tokens, cotangent, seg_ids, first_gain, first_shift, project_weight, project_bias, out_weight, out_bias,
        second_gain, second_shift, up_weight, up_bias, down_weight, down_bias,
    )
    tokens_grad, sums, project_grad, pbias_grad, outw_grad, up_grad, upbias_grad, down_grad = run_rear(
        first, mixed, own, lse, dctx, seg_ids, project_weight, tokens, dmid, first_gain, ug, dg, owg, ubg, small
    )
    pbias_grad = pbias_grad.reshape(project_bias.shape)
    upbias_grad = upbias_grad.reshape(up_bias.shape)
    reduced = (sums, project_grad, pbias_grad, outw_grad, up_grad, upbias_grad, down_grad)
    if lax.axis_size("dp") > 8:
        reduced = jax.tree.map(lambda v: v * 0.125, lax.psum(reduced, "dp"))
    sums, project_grad, pbias_grad, outw_grad, up_grad, upbias_grad, down_grad = reduced
    return (
        output, tokens_grad, sums[4], sums[5], project_grad, pbias_grad, outw_grad, sums[2], sums[0], sums[1],
        up_grad, upbias_grad, down_grad, sums[3],
    )


def solution(mesh):
    in_specs = (
        P(("dp", "mp"), None),
        P("dp"),
        P(("dp", "mp"), None),
        P(),
        P(),
        P(None, None, "mp"),
        P(None, "mp"),
        P("mp", None),
        P(),
        P(),
        P(),
        P(None, "mp"),
        P("mp"),
        P("mp", None),
        P(),
    )
    out_specs = (
        P(("dp", "mp"), None),
        P(("dp", "mp"), None),
        P(),
        P(),
        P(None, None, "mp"),
        P(None, "mp"),
        P("mp", None),
        P(),
        P(),
        P(),
        P(None, "mp"),
        P("mp"),
        P("mp", None),
        P(),
    )
    return jax.shard_map(shards, mesh=mesh, in_specs=in_specs, out_specs=out_specs, check_vma=False)
```

time: 609 us -> 268 us (0.44); the launches traced: 603 us -> 268 us
  waiting for transfers between devices: 342 us -> 0 us
  Pallas kernels: 79.4 us -> 249 us
  matrix products: 61.8 us -> 0 us
  blocking collectives: 55.4 us -> 0 us
  other arithmetic: 16.6 us -> 0.69 us
  between operations: 14.8 us -> 0.68 us
  local copies, waits for them, and re-layouts: 27.4 us -> 17.2 us
    pallas_call x1 -> x2, Pallas kernels: 79.4 us -> 249 us  [the longest x1 172 us: run_front(): pl.pallas_call(front, out_shape=[jax.ShapeDtypeStruct(s, t) for _, s, t i...]
    psum x1 -> x0, waiting for transfers between devices: 134 us -> none  [shards(): lax.psum((project_grad, pbias_grad, outw_grad), 'dp')]
    all_gather x3 -> x0, waiting for transfers between devices: 121 us -> none  [the longest x1 43.3 us: shards(): second_all = lax.all_gather(second_low, 'mp', axis=0, tiled=True)]
    reduce_scatter x3 -> x0, waiting for transfers between devices: 85.6 us -> none  [the longest x1 44.4 us: shards(): lax.psum_scatter(jnp.dot(hidden_low, down_weight, preferred_element_type=...]
    dot_general x20 -> x0, matrix products: 61.8 us -> none  [the longest x4 19 us: contract_rows(): lax.dot_general(left, right, (((0,), (0,)), ((), ())), preferred_element_...]
    psum x2 -> x0, blocking collectives: 55.4 us -> none  [the longest x1 40.9 us: shards(): lax.psum((first_gain_grad, first_shift_grad, outbias_grad, second_gain_gr...]
    reduce_sum x8 -> x0, other arithmetic: 7.51 us -> none  [the longest x1 3.24 us: shards(): outbias_grad = jnp.sum(middle_low.astype(jnp.float32), 0)]
    unnamed x50 -> x17, local copies, waits for them, and re-layouts: 19.3 us -> 13.3 us
  transfers between devices with their start and end apart: 7 -> 0, of which waited for: 7 -> 0; matrix products, arithmetic and copies ran while one was open for 8% -> 0% of each run, Pallas kernels for 0% -> 0%
where the time goes in v2:
time: 268 us
  Pallas kernels  249 us (93%)
  local copies, waits for them, and re-layouts  17.2 us (6%)
    pallas_call x1, Pallas kernels, run_front(): pl.pallas_call(front, out_shape=[jax.ShapeDtypeStruct(s, t) for _, s, t i...  172 us
    pallas_call x1, Pallas kernels, run_rear(): pl.pallas_call(rear, out_shape=[jax.ShapeDtypeStruct(s, t) for _, s, t in...  76.9 us
    unnamed x17, local copies, waits for them, and re-layouts  13.3 us

profile of v2, /device:TPU:0, one launch (start us, length us, event | category | flops | bytes accessed | tf_op | source)
XLA Modules:
  0.0 267.9 jit_solution(17729240867783047738)
XLA Ops:
  0.6 1.7 copy.29.segc
  2.4 172.5 %front.1 = (bf16[4,256,1024]{2,1,0:T(8,128)(2,1)}, bf16[1024,768]{1,0:T(8,128)(2,1)}, bf16[4,256,256]{2,1,0:T(8,128)(2,1)}, f32[2,1024,128]{2,1,0:T(8,128)}, bf1...) custom-call(bf16[256,1024]{1,0:T(8,128)(2,1)} %x_ref.3, ...), custom_call_target="tpu_custom_call" | custom-call | tf_op jit(solution)/shard_map/front/pallas_call | solution.py:502
  174.8 0.0 copy-start.3
  174.8 76.9 %rear.1 = (bf16[256,1024]{1,0:T(8,128)(2,1)}, f32[8,1024]{1,0:T(8,128)}, f32[3,1024,256]{2,1,0:T(8,128)}, f32[1,768]{1,0:T(1,128)}, f32[256,1024]{1,0:T(8,128)},...) custom-call(bf16[4,256,1024]{2,1,0:T(8,128)(2,1)} %get-tuple-element.35.first, ...), custom_call_target="tpu_custom_call" | custom-call | tf_op jit(solution)/shard_map/rear/pallas_call | solution.py:895
  251.7 0.7 reduce
  252.4 0.6 reshape.77
  253.0 1.6 fusion
  254.6 0.0 copy-done.3
  254.6 0.8 copy.38
  255.4 1.9 copy.39
  257.3 0.0 copy-start.2
  257.3 0.0 copy-start.1
  257.3 3.9 %copy.40 = f32[3,1024,256]{2,1,0:T(8,128)} copy(f32[3,1024,256]{2,1,0:T(8,128)} %get-tuple-element.78) | data formatting | bytes 6291456
  261.2 0.0 copy-done.2
  261.2 1.0 copy.41
  262.2 0.0 copy-done.1
  262.2 0.0 copy-start.4
  262.2 0.0 copy-start
  262.2 2.1 copy.42
  264.3 0.0 copy-done.4
  264.3 0.6 copy.43
  264.9 1.0 copy-done
  265.9 2.0 copy.44
Async XLA Ops:
  174.8 79.8 %copy-start.3 = (bf16[256,1024]{1,0:T(8,128)(2,1)S(1)}, bf16[256,1024]{1,0:T(8,128)(2,1)}, u32[]{:S(2)}) copy-start(bf16[256,1024]{1,0:T(8,128)(2,1)} %get-tuple-element.74) | copy-start | bytes 1572868
  257.3 3.9 %copy-start.2 = (f32[256,1024]{1,0:T(8,128)S(1)}, f32[256,1024]{1,0:T(8,128)}, u32[]{:S(2)}) copy-start(f32[256,1024]{1,0:T(8,128)} %get-tuple-element.80) | copy-start | bytes 3145732
  257.3 4.9 %copy-start.1 = (f32[1024,1024]{1,0:T(8,128)S(1)}, f32[1024,1024]{1,0:T(8,128)}, u32[]{:S(2)}) copy-start(f32[1024,1024]{1,0:T(8,128)} %get-tuple-element.84) | copy-start | bytes 12582916
  262.2 2.1 copy-start.4
  262.2 3.7 %copy-start = (f32[1024,1024]{1,0:T(8,128)S(1)}, f32[1024,1024]{1,0:T(8,128)}, u32[]{:S(2)}) copy-start(f32[1024,1024]{1,0:T(8,128)} %get-tuple-element.86) | copy-start | bytes 12582916

commit v3 on v0

v3 whole, which is shorter than its diff:
```python
import math

import jax
import jax.numpy as jnp
from jax import lax
from jax.experimental import pallas as pl
from jax.experimental.pallas import tpu as pltpu
from jax.sharding import PartitionSpec as P

HD = 128
EPS = 1e-05
BF = jnp.bfloat16
F32 = jnp.float32
MESH = pl.DeviceIdType.MESH
VMEM = pltpu.VMEM
DMA = pltpu.SemaphoreType.DMA
GELU_A = 0.7978845608
GELU_B = 0.044715


def mm(left, right):
    return jnp.dot(left, right, preferred_element_type=F32)


def mm_nt(left, right):
    return lax.dot_general(left, right, (((1,), (1,)), ((), ())), preferred_element_type=F32)


def mm_tn(left, right):
    return lax.dot_general(left, right, (((0,), (0,)), ((), ())), preferred_element_type=F32)


def remote(src, dst, ss, rs, device):
    return pltpu.make_async_remote_copy(
        src_ref=src, dst_ref=dst, send_sem=ss, recv_sem=rs, device_id=device, device_id_type=MESH
    )


def local(src, dst, sem):
    return pltpu.make_async_copy(src, dst, sem)


def barrier(devices):
    sem = pltpu.get_barrier_semaphore()
    for device in devices:
        pl.semaphore_signal(sem, 1, device_id=device, device_id_type=MESH)
    return lambda: pl.semaphore_wait(sem, len(devices))


def start(copy):
    copy.start()


def wait(copy):
    copy.wait()


def sent(copy):
    copy.wait_send()


def came(copy):
    copy.wait_recv()


def norm(values):
    mean = jnp.mean(values, -1, keepdims=True)
    centered = values - mean
    var = jnp.mean(centered * centered, -1, keepdims=True)
    scale = lax.rsqrt(var + EPS)
    return centered * scale, scale


def norm_back(grad, normed, scale, gain):
    scaled = grad * gain
    return scale * (
        scaled - jnp.mean(scaled, -1, keepdims=True) - normed * jnp.mean(scaled * normed, -1, keepdims=True)
    )


def gelu_parts(v):
    square = v * v
    t = jnp.tanh(GELU_A * v * (1.0 + GELU_B * square))
    half = 0.5 * (1.0 + t)
    slope = half + 0.5 * v * (1.0 - t * t) * (GELU_A * (1.0 + 3.0 * GELU_B * square))
    return v * half, slope


class Place:
    def __init__(self):
        self.z = lax.axis_index("mp")
        self.dp = lax.axis_index("dp")
        self.d = lax.rem(self.dp, 8)
        self.base = self.dp - self.d
        self.core = lax.rem(self.d, 2)
        self.column = self.d // 2
        bit_x = lax.rem(self.column, 2)
        bit_y = self.column // 2
        self.step_x = 1 - 2 * bit_x
        self.step_y = 2 - 4 * bit_y
        self.sibling = self.dp + 1 - 2 * self.core
        self.swapped = lax.rem(self.core + self.z // 2, 2)
        self.far = lax.rem(self.z + 2, 4)
        self.rank = lax.rem(self.z + 2 * self.swapped, 4)
        self.odd = lax.rem(self.z, 2)

    def column_at(self, i):
        return self.column + (i % 2) * self.step_x + (i // 2) * self.step_y

    def chip(self, i):
        return {"dp": self.base + 2 * self.column_at(i) + self.core, "mp": self.z}

    def along(self, z):
        return {"dp": self.dp, "mp": z}

    def to_sibling(self):
        return {"dp": self.sibling, "mp": self.z}

    def across(self):
        return {"dp": self.dp, "mp": self.z + 1 - 2 * self.odd}

    def partner(self):
        return {"dp": self.sibling, "mp": self.far}

    def rank_of(self, k):
        return lax.rem(self.rank + (k // 2) * (1 - 2 * self.odd) + 2 * (k % 2), 4)

    def at_home(self, body):
        pl.when(self.swapped == 0)(body)

    def if_swapped(self, body):
        pl.when(self.swapped == 1)(body)


class Gather:
    def __init__(self, p, buf, ss, rs):
        self.p, self.buf, self.ss, self.rs = p, buf, ss, rs

    def _copy(self, k, i, device):
        view = self.buf.at[self.p.rank_of(k)]
        return remote(view, view, self.ss.at[i], self.rs.at[i], device)

    def send(self):
        self._copy(0, 0, self.p.across()).start()
        self._copy(0, 1, self.p.to_sibling()).start()

    def take(self):
        self._copy(2, 0, self.p.across()).wait_recv()
        self._copy(2, 2, self.p.to_sibling()).start()

    def near(self):
        self._copy(1, 1, self.p.to_sibling()).wait_recv()

    def last(self):
        self._copy(3, 2, self.p.to_sibling()).wait_recv()

    def finish(self):
        self._copy(0, 0, self.p.across()).wait_send()
        self._copy(0, 1, self.p.to_sibling()).wait_send()
        self._copy(2, 2, self.p.to_sibling()).wait_send()


class Sum:
    def __init__(self, p, parts, got, out, into, ss, rs):
        self.p, self.parts, self.got, self.out, self.into, self.ss, self.rs = p, parts, got, out, into, ss, rs

    def _give(self, n):
        k = 1 + 2 * n
        return remote(
            self.parts.at[self.p.rank_of(k)], self.got.at[n], self.ss.at[n], self.rs.at[n], self.p.to_sibling()
        )

    def _ship(self):
        return remote(self.out, self.into, self.ss.at[2], self.rs.at[2], self.p.across())

    def _part(self, k):
        return self.parts[pl.ds(self.p.rank_of(k), 1)][0].astype(F32)

    def give_far(self):
        self._give(1).start()

    def give_near(self):
        self._give(0).start()

    def ship(self):
        self._give(1).wait_recv()
        self.out[...] = (self._part(2) + self.got[1].astype(F32)).astype(BF)
        self._ship().start()

    def total(self):
        self._give(0).wait_recv()
        total = self._part(0) + self.got[0].astype(F32)
        self._ship().wait_recv()
        return total + self.into[...].astype(F32)

    def finish(self):
        self._give(0).wait_send()
        self._give(1).wait_send()
        self._ship().wait_send()


class Weight:
    def __init__(self, p, src, buf, part, ss, rs):
        self.p, self.src, self.buf, self.part, self.ss, self.rs = p, src, buf, part, ss, rs

    def _own(self):
        return local(self.src, self.buf, self.ss.at[0])

    def _swap(self):
        column = self.p.column
        return remote(self.part(self.src, column), self.part(self.buf, column), self.ss.at[0], self.rs.at[0], self.p.partner())

    def _share(self, i, column):
        view = self.part(self.buf, column)
        return remote(view, view, self.ss.at[i], self.rs.at[i], self.p.chip(i))

    def home(self):
        self._own().start()

    def swap(self):
        self._swap().start()

    def take(self):
        self._swap().wait_recv()
        for i in (1, 2, 3):
            self._share(i, self.p.column).start()

    def ready(self):
        self.p.at_home(lambda: self._own().wait())

        @self.p.if_swapped
        def _():
            for i in (1, 2, 3):
                self._share(i, self.p.column_at(i)).wait_recv()

    def finish(self):
        self._swap().wait_send()
        for i in (1, 2, 3):
            self._share(i, self.p.column).wait_send()


class Grad:
    def __init__(self, p, buf, part, into, total, far, out, ss, rs):
        self.p, self.buf, self.part, self.into, self.sum, self.far, self.out = p, buf, part, into, total, far, out
        self.ss, self.rs = ss, rs

    def _scatter(self, i):
        view = self.part(self.buf, self.p.column_at(i))
        return remote(view, self.into.at[i - 1], self.ss.at[i], self.rs.at[i], self.p.chip(i))

    def _home(self):
        return remote(self.sum, self.far, self.ss.at[0], self.rs.at[0], self.p.along(self.p.far))

    def _spread(self, i):
        view = self.part(self.out, self.p.column)
        device = self.p.chip(i) if i else self.p.to_sibling()
        return remote(self.sum, view, self.ss.at[4 + i], self.rs.at[4 + i], device)

    def _arrived(self, i):
        view = self.part(self.out, self.p.column_at(i))
        return remote(self.sum, view, self.ss.at[4 + i], self.rs.at[4 + i], self.p.chip(i))

    def _relay(self, i):
        view = self.part(self.out, self.p.column_at(i))
        return remote(view, view, self.ss.at[7 + i], self.rs.at[7 + i], self.p.to_sibling())

    def _keep(self):
        return local(self.sum, self.part(self.out, self.p.column), self.ss.at[11])

    def scatter(self):
        for i in (1, 2, 3):
            self._scatter(i).start()

    def combine(self):
        total = self.part(self.buf, self.p.column)[...].astype(F32)
        for i in (1, 2, 3):
            self._scatter(i).wait_recv()
            total = total + self.into[i - 1].astype(F32)
        self.sum[...] = total.astype(BF)
        self.p.if_swapped(lambda: self._home().start())

    def final(self):
        self._home().wait_recv()
        self.sum[...] = (self.sum[...].astype(F32) + self.far[...].astype(F32)).astype(BF)
        for i in (1, 2, 3, 0):
            self._spread(i).start()
        self._keep().start()

    def relay(self):
        for i in (1, 2, 3):
            self._arrived(i).wait_recv()
            self._relay(i).start()

    def finish(self):
        for i in (1, 2, 3):
            self._scatter(i).wait_send()

        @self.p.at_home
        def _():
            for i in range(4):
                self._spread(i).wait_send()
                if i:
                    self._relay(i).wait_send()
            self._keep().wait()

        @self.p.if_swapped
        def _():
            self._home().wait_send()
            self._spread(0).wait_recv()
            for i in (1, 2, 3):
                self._relay(i).wait_recv()


class Plane:
    def __init__(self, p, buf, ss, rs):
        self.p, self.buf, self.ss, self.rs = p, buf, ss, rs

    def _copy(self, column, core, i, device):
        view = self.buf.at[2 * column + core]
        return remote(view, view, self.ss.at[i], self.rs.at[i], device)

    def send(self):
        p = self.p
        for i in (1, 2, 3):
            self._copy(p.column, p.core, i, p.chip(i)).start()
        self._copy(p.column, p.core, 0, p.to_sibling()).start()

    def take(self):
        p = self.p
        for i in (1, 2, 3):
            self._copy(p.column_at(i), p.core, i, p.chip(i)).wait_recv()
            self._copy(p.column_at(i), p.core, 3 + i, p.to_sibling()).start()

    def rest(self):
        p = self.p
        self._copy(p.column, 1 - p.core, 0, p.to_sibling()).wait_recv()
        for i in (1, 2, 3):
            self._copy(p.column_at(i), 1 - p.core, 3 + i, p.to_sibling()).wait_recv()

    def finish(self):
        p = self.p
        self._copy(p.column, p.core, 0, p.to_sibling()).wait_send()
        for i in (1, 2, 3):
            self._copy(p.column, p.core, i, p.chip(i)).wait_send()
            self._copy(p.column_at(i), p.core, 3 + i, p.to_sibling()).wait_send()


def layer(
    x_ref, cot, seg_ref, g1, b1, wq_ref, bq_ref, ow_ref, ob, g2, b2, up_ref, ub_ref, dn_ref, dwb,
    output, tokens_grad, small_out, pg_out, og_out, ug_out, dg_out,
    xs, seg, segc, first, second, dy, dmid, mixed, own, stats, wq, bq, ow, up, ub, dn,
    a_part, a_got, a_out, a_in, s_part, s_got, s_out, s_in, o_part, o_got, o_out, o_in, f_got, f_out, f_in,
    hidden, dpre, dg, ug, pg, og, dg_in, ug_in, pg_in, og_in, dg_sum, ug_sum, pg_sum, og_sum,
    dg_far, ug_far, pg_far, og_far, acc, middle, dmiddle, rows_out, sm, sm_in, smp,
    ss_in, rs_in, ss_first, rs_first, ss_second, rs_second, ss_dy, rs_dy, ss_dmid, rs_dmid,
    ss_a, rs_a, ss_s, rs_s, ss_o, rs_o, ss_f, rs_f, ss_wq, rs_wq, ss_ow, rs_ow, ss_up, rs_up, ss_dn, rs_dn,
    ss_dg, rs_dg, ss_ug, rs_ug, ss_pg, rs_pg, ss_og, rs_og, ss_sm, rs_sm, ss_sp, rs_sp,
):
    p = Place()
    rows, width = xs.shape
    share = wq.shape[2]
    heads = share // HD
    factor = 1.0 / math.sqrt(HD)
    length = 4 * rows
    others = [lax.rem(p.z + k, 4) for k in (1, 2, 3)]
    enter = barrier([p.to_sibling(), p.partner()] + [p.along(t) for t in others] + [p.chip(i) for i in (1, 2, 3)])
    rank = p.rank

    def strip(index):
        return pl.ds(pl.multiple_of(index * rows, rows), rows)

    def piece(count, axis):
        def view(ref, column):
            size = ref.shape[axis] // count
            cut = pl.ds(pl.multiple_of(column * size, size), size)
            return ref.at[:, cut] if axis else ref.at[cut]

        return view

    by_rows, by_second = piece(4, 0), piece(4, 1)
    wq_move = Weight(p, wq_ref, wq, by_second, ss_wq, rs_wq)
    ow_move = Weight(p, ow_ref, ow, by_rows, ss_ow, rs_ow)
    up_move = Weight(p, up_ref, up, by_rows, ss_up, rs_up)
    dn_move = Weight(p, dn_ref, dn, by_rows, ss_dn, rs_dn)
    first_all = Gather(p, first, ss_first, rs_first)
    second_all = Gather(p, second, ss_second, rs_second)
    dy_all = Gather(p, dy, ss_dy, rs_dy)
    dmid_all = Gather(p, dmid, ss_dmid, rs_dmid)
    a_sum = Sum(p, a_part, a_got, a_out, a_in, ss_a, rs_a)
    s_sum = Sum(p, s_part, s_got, s_out, s_in, ss_s, rs_s)
    o_sum = Sum(p, o_part, o_got, o_out, o_in, ss_o, rs_o)
    f_sum = Sum(p, a_part, f_got, f_out, f_in, ss_f, rs_f)
    dn_grad = Grad(p, dg, by_rows, dg_in, dg_sum, dg_far, dg_out, ss_dg, rs_dg)
    up_grad = Grad(p, ug, by_rows, ug_in, ug_sum, ug_far, ug_out, ss_ug, rs_ug)
    pj_grad = Grad(p, pg, by_second, pg_in, pg_sum, pg_far, pg_out, ss_pg, rs_pg)
    ow_grad = Grad(p, og, by_rows, og_in, og_sum, og_far, og_out, ss_og, rs_og)

    def x_home():
        return local(x_ref, xs, ss_in.at[0])

    def cot_home():
        return local(cot, dy.at[rank], ss_in.at[1])

    def x_swap():
        return remote(x_ref, xs, ss_in.at[0], rs_in.at[0], p.partner())

    def cot_swap(slot):
        return remote(cot, dy.at[slot], ss_in.at[1], rs_in.at[1], p.partner())

    def bq_swap():
        return remote(bq_ref, bq, ss_in.at[2], rs_in.at[2], p.partner())

    def ub_swap():
        return remote(ub_ref, ub, ss_in.at[3], rs_in.at[3], p.partner())

    def seg_give():
        return remote(seg_ref, seg, ss_in.at[4], rs_in.at[4], p.to_sibling())

    def tg_back():
        return remote(rows_out.at[0], tokens_grad, ss_in.at[5], rs_in.at[5], p.partner())

    def out_back():
        return remote(rows_out.at[1], output, ss_in.at[6], rs_in.at[6], p.partner())

    def tg_home():
        return local(rows_out.at[0], tokens_grad, ss_in.at[5])

    def out_home():
        return local(rows_out.at[1], output, ss_in.at[6])

    @p.at_home
    def _():
        x_home().start()
        cot_home().start()
        for move in (wq_move, ow_move, up_move, dn_move):
            move.home()
        bq[...] = bq_ref[...]
        ub[...] = ub_ref[...]
        seg[...] = seg_ref[...]

    enter()

    @p.if_swapped
    def _():
        x_swap().start()
        wq_move.swap()
        bq_swap().start()
        ub_swap().start()

    @p.at_home
    def _():
        seg_give().start()
        x_home().wait()

    p.if_swapped(lambda: x_swap().wait_recv())
    normed, _ = norm(xs[...].astype(F32))
    first[pl.ds(rank, 1)] = (normed * g1[...] + b1[...]).astype(BF)[None]
    first_all.send()

    @p.if_swapped
    def _():
        wq_move.take()
        ow_move.swap()
        up_move.swap()
        seg_give().wait_recv()
        bq_swap().wait_recv()
        ub_swap().wait_recv()

    segc[...] = jnp.transpose(jnp.broadcast_to(seg[0:1, :], (HD, length)))

    def project(k):
        s = p.rank_of(k)
        block = first[pl.ds(s, 1)][0]
        for t in range(3):
            value = mm(block, wq[t]) + bq[t : t + 1, :]
            mixed[strip(s), t * share : (t + 1) * share] = value.astype(BF)

    @p.at_home
    def _():
        wq_move.ready()
        project(0)

    first_all.take()

    @p.at_home
    def _():
        cot_home().wait()
        dy_all.send()
        project(2)

    @p.if_swapped
    def _():
        ow_move.take()
        cot_swap(p.z).start()
        dn_move.swap()
        wq_move.ready()
        project(0)
        project(2)

    first_all.near()
    project(1)
    first_all.last()
    project(3)

    for r in reversed(range(4)):
        span = (r + 1) * rows
        top = r * rows
        place_q = top + lax.broadcasted_iota(jnp.int32, (rows, span), 0)
        place_k = lax.broadcasted_iota(jnp.int32, (rows, span), 1)
        allowed = (segc[top : top + rows, 0:1] == seg[0:1, 0:span]) & (place_q >= place_k)
        for h in range(heads):
            q = mixed[top : top + rows, h * HD : (h + 1) * HD]
            k = mixed[0:span, share + h * HD : share + (h + 1) * HD]
            v = mixed[0:span, 2 * share + h * HD : 2 * share + (h + 1) * HD]
            scores = jnp.where(allowed, mm_nt(q, k) * factor, -1e30)
            peak = jnp.max(scores, -1, keepdims=True)
            expo = jnp.exp(scores - peak)
            total = jnp.sum(expo, -1, keepdims=True)
            probs = (expo / total).astype(BF)
            own[r, :, h * HD : (h + 1) * HD] = mm(probs, v).astype(BF)
            stats[h, top : top + rows, 0:1] = peak + jnp.log(total)
    ow_move.ready()
    for r in range(4):
        a_part[r] = mm(own[r], ow[...]).astype(BF)
    a_sum.give_far()
    a_sum.give_near()
    a_sum.ship()

    @p.if_swapped
    def _():
        up_move.take()
        cot_swap(rank).wait_recv()
        dy_all.send()
        dn_move.take()

    dy_all.take()
    middle[...] = xs[...].astype(F32) + (a_sum.total() + ob[...])
    normed, _ = norm(middle[...])
    second[pl.ds(rank, 1)] = (normed * g2[...] + b2[...]).astype(BF)[None]
    second_all.send()

    up_move.ready()
    dn_move.ready()

    def feed(k, carry):
        @pl.when(k == 1)
        def _():
            second_all.near()
            dy_all.near()

        @pl.when(k == 2)
        def _():
            second_all.take()

        @pl.when(k == 3)
        def _():
            second_all.last()
            dy_all.last()

        s = pl.ds(p.rank_of(k), 1)
        value, slope = gelu_parts(mm(second[s][0], up[...]) + ub[...])
        value = value.astype(BF)
        hidden[s] = value[None]
        back = (mm_nt(dy[s][0], dn[...]) * slope).astype(BF)
        dpre[s] = back[None]
        s_part[s] = mm_nt(back, up[...]).astype(BF)[None]

        @pl.when(k == 1)
        def _():
            s_sum.give_near()

        @pl.when(k == 3)
        def _():
            s_sum.give_far()

        o_part[s] = mm(value, dn[...]).astype(BF)[None]
        return carry

    lax.fori_loop(0, 4, feed, 0)
    s_sum.ship()
    o_sum.give_far()
    o_sum.give_near()
    units = hidden.shape[2]
    for c in range(4):
        cols = slice(c * units // 4, (c + 1) * units // 4)
        dg[cols, :] = mm_tn(hidden[:, :, cols].reshape(length, units // 4), dy[...].reshape(length, width)).astype(BF)
    dn_grad.scatter()
    for c in range(4):
        cols = slice(c * width // 4, (c + 1) * width // 4)
        ug[cols, :] = mm_tn(second[:, :, cols].reshape(length, width // 4), dpre[...].reshape(length, units)).astype(BF)
    up_grad.scatter()

    grad = dy[pl.ds(rank, 1)][0].astype(F32)
    total = s_sum.total()
    normed, scale = norm(middle[...])
    dmiddle[...] = grad + norm_back(total, normed, scale, g2[...])
    low = dmiddle[...].astype(BF)
    dmid[pl.ds(rank, 1)] = low[None]
    dmid_all.send()
    o_sum.ship()
    sm[...] = jnp.zeros(sm.shape, F32)
    sm[0:1, :] = jnp.sum(total * normed, 0, keepdims=True)
    sm[1:2, :] = jnp.sum(total, 0, keepdims=True)
    sm[2:3, :] = jnp.sum(low.astype(F32), 0, keepdims=True)
    sm[3:4, :] = jnp.sum(grad, 0, keepdims=True)
    bias_sum = jnp.sum(dpre[...].reshape(length, units).astype(F32), 0, keepdims=True)
    for q in range(4):
        sm[8 + q : 9 + q, :] = jnp.where(rank == q, bias_sum, 0.0)
    for t in range(3):
        acc[t] = jnp.zeros((length, share), F32)
    dmid_all.take()

    ctx_cols = slice(3 * share, 4 * share)

    def to_context(k):
        s = pl.ds(p.rank_of(k), 1)
        value = mm_nt(dmid[s][0], ow[...]).astype(BF)
        hidden[s, :, ctx_cols] = value[None]
        for h in range(heads):
            cols = slice(h * HD, (h + 1) * HD)
            product = value[:, cols].astype(F32) * own[s, :, cols][0].astype(F32)
            stats[h, strip(p.rank_of(k)), 1:2] = jnp.sum(product, -1, keepdims=True)

    to_context(0)
    dmid_all.near()
    to_context(1)
    to_context(2)
    dmid_all.last()
    to_context(3)
    og[...] = mm_tn(own[...].reshape(length, share), dmid[...].reshape(length, width)).astype(BF)
    ow_grad.scatter()
    a_sum.finish()

    mirror = 1 - p.odd
    for g in range(4):

        def block(e, carry):
            i = (g + e) + mirror * (3 - g - (g + e))
            j = g + mirror * (3 - (g + e) - g)
            qs, ks = strip(i), strip(j)
            place_q = i * rows + lax.broadcasted_iota(jnp.int32, (rows, rows), 0)
            place_k = j * rows + lax.broadcasted_iota(jnp.int32, (rows, rows), 1)
            allowed = (segc[qs, 0:1] == seg[0:1, ks]) & (place_q >= place_k)
            for h in range(heads):
                cols = slice(h * HD, (h + 1) * HD)
                q = mixed[qs, cols]
                k = mixed[ks, share + h * HD : share + (h + 1) * HD]
                v = mixed[ks, 2 * share + h * HD : 2 * share + (h + 1) * HD]
                head = hidden[pl.ds(i, 1), :, 3 * share + h * HD : 3 * share + (h + 1) * HD][0]
                scores = jnp.where(allowed, mm_nt(q, k) * factor, -1e30)
                probs = jnp.exp(scores - stats[h, qs, 0:1])
                acc[2, ks, cols] += mm_tn(probs.astype(BF), head)
                back = (probs * (mm_nt(head, v) - stats[h, qs, 1:2])).astype(BF)
                acc[0, qs, cols] += mm(back, k)
                acc[1, ks, cols] += mm_tn(back, q)
            return carry

        lax.fori_loop(0, 4 - g, block, 0)
        r = g + mirror * (3 - 2 * g)
        total = None
        for t in range(3):
            value = acc[t, strip(r), :]
            low = (value * factor if t < 2 else value).astype(BF)
            hidden[pl.ds(r, 1), :, t * share : (t + 1) * share] = low[None]
            term = mm_nt(low, wq[t])
            total = term if total is None else total + term
        a_part[pl.ds(r, 1)] = total.astype(BF)[None]
        if g % 2 == 0:
            pl.when(r == p.rank_of(3))(f_sum.give_far)
            pl.when(r == p.rank_of(2))(f_sum.ship)
        else:
            pl.when(r == p.rank_of(1))(f_sum.give_near)

    for t in range(3):
        cols = slice(t * share, (t + 1) * share)
        low = hidden[:, :, cols].reshape(length, share)
        pg[t] = mm_tn(first[...].reshape(length, width), low).astype(BF)
        bias = jnp.sum(low.astype(F32), 0, keepdims=True)
        line = (6, 7, 12)[t]
        for q in range(4):
            sm[line : line + 1, q * share : (q + 1) * share] = jnp.where(rank == q, bias, 0.0)
    pj_grad.scatter()
    dn_grad.combine()
    up_grad.combine()

    total = f_sum.total()
    normed, scale = norm(xs[...].astype(F32))
    rows_out[0] = (dmiddle[...] + norm_back(total, normed, scale, g1[...])).astype(BF)

    @p.at_home
    def _():
        tg_home().start()

    @p.if_swapped
    def _():
        tg_back().start()

    sm[4:5, :] = jnp.sum(total * normed, 0, keepdims=True)
    sm[5:6, :] = jnp.sum(total, 0, keepdims=True)

    def sm_copy(k, t):
        return remote(sm, sm_in.at[k], ss_sm.at[k], rs_sm.at[k], p.along(t))

    for k, t in enumerate(others):
        sm_copy(k, t).start()
    rows_out[1] = (middle[...] + (o_sum.total() + dwb[...])).astype(BF)

    @p.at_home
    def _():
        out_home().start()

    @p.if_swapped
    def _():
        out_back().start()

    ow_grad.combine()
    p.at_home(dn_grad.final)
    p.at_home(up_grad.final)
    pj_grad.combine()
    p.at_home(ow_grad.final)
    sm_sum = sm[...]
    for k, t in enumerate(others):
        sm_copy(k, t).wait_recv()
        sm_sum = sm_sum + sm_in[k]
    smp[pl.ds(p.d, 1)] = sm_sum[None]
    sm_all = Plane(p, smp, ss_sp, rs_sp)
    sm_all.send()
    p.at_home(dn_grad.relay)
    p.at_home(pj_grad.final)
    sm_all.take()
    p.at_home(up_grad.relay)
    sm_all.rest()
    small_out[...] = jnp.sum(smp[...], 0)
    p.at_home(ow_grad.relay)
    p.at_home(pj_grad.relay)

    for group in (first_all, second_all, dy_all, dmid_all, s_sum, o_sum, f_sum, sm_all):
        group.finish()
    for k, t in enumerate(others):
        sm_copy(k, t).wait_send()

    @p.at_home
    def _():
        seg_give().wait_send()
        tg_home().wait()
        out_home().wait()

    @p.if_swapped
    def _():
        for copy in (x_swap(), bq_swap(), ub_swap(), cot_swap(rank), tg_back(), out_back()):
            copy.wait_send()
        tg_back().wait_recv()
        out_back().wait_recv()
        for move in (wq_move, ow_move, up_move, dn_move):
            move.finish()

    for grad_sum in (dn_grad, up_grad, pj_grad, ow_grad):
        grad_sum.finish()


def run_layer(
    x, cot, seg_ids, g1, b1, wq, bq, ow, ob, g2, b2, upw, upb, dnw, dnb,
):
    rows, width = x.shape
    share = wq.shape[2]
    length = 4 * rows
    heads = share // HD
    units = upw.shape[1]
    vm = pl.BlockSpec(memory_space=VMEM)
    hbm = pl.BlockSpec(memory_space=pl.ANY)
    token = (rows, width)
    outs = [
        (hbm, token, BF), (hbm, token, BF), (vm, (16, width), F32), (hbm, (3, width, share), BF),
        (hbm, (share, width), BF), (hbm, (width, units), BF), (hbm, (units, width), BF),
    ]
    four = VMEM((4,) + token, BF)
    sums = [VMEM((2,) + token, BF), VMEM(token, BF), VMEM(token, BF)]
    quarters = [(units // 4, width), (width // 4, units), (3, width // 4, share), (share // 4, width)]
    pair = lambda n: [DMA((n,)), DMA((n,))]
    return pl.pallas_call(
        layer,
        out_shape=[jax.ShapeDtypeStruct(s, t) for _, s, t in outs],
        in_specs=[hbm, hbm, vm, vm, vm, hbm, vm, hbm, vm, vm, vm, hbm, vm, hbm, vm],
        out_specs=[m for m, _, _ in outs],
        scratch_shapes=[
            VMEM(token, BF), VMEM((8, length), jnp.int32), VMEM((length, HD), jnp.int32), four, four, four, four,
            VMEM((length, 3 * share), BF), VMEM((4, rows, share), BF), VMEM((heads, length, HD), F32),
            VMEM((3, width, share), BF), VMEM((3, share), F32), VMEM((share, width), BF), VMEM((width, units), BF),
            VMEM((1, units), F32), VMEM((units, width), BF),
            four, *sums, four, *sums, four, *sums, *sums,
            VMEM((4, rows, units), BF), VMEM((4, rows, units), BF),
            VMEM((units, width), BF), VMEM((width, units), BF), VMEM((3, width, share), BF), VMEM((share, width), BF),
            *[VMEM((3,) + q, BF) for q in quarters], *[VMEM(q, BF) for q in quarters], *[VMEM(q, BF) for q in quarters],
            VMEM((3, length, share), F32), VMEM(token, F32), VMEM(token, F32), VMEM((2,) + token, BF),
            VMEM((16, width), F32), VMEM((3, 16, width), F32), VMEM((8, 16, width), F32),
            *pair(7), *pair(3), *pair(3), *pair(3), *pair(3), *pair(3), *pair(3), *pair(3), *pair(3),
            *pair(4), *pair(4), *pair(4), *pair(4), *pair(12), *pair(12), *pair(12), *pair(12), *pair(3), *pair(7),
        ],
        compiler_params=pltpu.CompilerParams(collective_id=0, has_side_effects=True, vmem_limit_bytes=64 << 20),
        name="layer",
    )(
        x, cot, jnp.broadcast_to(seg_ids.reshape(1, length), (8, length)), g1.reshape(1, width), b1.reshape(1, width),
        wq, bq, ow, ob.reshape(1, width), g2.reshape(1, width), b2.reshape(1, width), upw, upb.reshape(1, units),
        dnw, dnb.reshape(1, width),
    )


def shards(
    tokens, seg_ids, cotangent, first_gain, first_shift, project_weight, project_bias, out_weight, out_bias,
    second_gain, second_shift, up_weight, up_bias, down_weight, down_bias,
):
    share = project_weight.shape[2]
    output, tokens_grad, sums, *grads = run_layer(
        tokens, cotangent, seg_ids, first_gain, first_shift, project_weight, project_bias, out_weight, out_bias,
        second_gain, second_shift, up_weight, up_bias, down_weight, down_bias,
    )
    reduced = (sums, *[g.astype(jnp.float32) for g in grads])
    if lax.axis_size("dp") > 8:
        reduced = jax.tree.map(lambda v: v * 0.125, lax.psum(reduced, "dp"))
    sums, project_grad, outw_grad, up_grad, down_grad = reduced
    z = lax.axis_index("mp")
    upbias_grad = lax.dynamic_index_in_dim(sums, 8 + z, 0, False)
    pbias_grad = lax.dynamic_slice_in_dim(jnp.stack([sums[6], sums[7], sums[12]]), z * share, share, 1)
    return (
        output, tokens_grad, sums[4], sums[5], project_grad, pbias_grad, outw_grad, sums[2], sums[0], sums[1],
        up_grad, upbias_grad, down_grad, sums[3],
    )


def solution(mesh):
    in_specs = (
        P(("dp", "mp"), None),
        P("dp"),
        P(("dp", "mp"), None),
        P(),
        P(),
        P(None, None, "mp"),
        P(None, "mp"),
        P("mp", None),
        P(),
        P(),
        P(),
        P(None, "mp"),
        P("mp"),
        P("mp", None),
        P(),
    )
    out_specs = (
        P(("dp", "mp"), None),
        P(("dp", "mp"), None),
        P(),
        P(),
        P(None, None, "mp"),
        P(None, "mp"),
        P("mp", None),
        P(),
        P(),
        P(),
        P(None, "mp"),
        P("mp"),
        P("mp", None),
        P(),
    )
    return jax.shard_map(shards, mesh=mesh, in_specs=in_specs, out_specs=out_specs, check_vma=False)
```

time: 665 us -> 242 us (0.36); the launches traced: 658 us -> 242 us
  waiting for transfers between devices: 436 us -> 0 us
  Pallas kernels: 0 us -> 225 us
  matrix products: 80.4 us -> 0 us
  blocking collectives: 56.1 us -> 0 us
  local copies, waits for them, and re-layouts: 30.5 us -> 5.44 us
  other arithmetic: 31 us -> 10.4 us
  between operations: 14.6 us -> 0.67 us
  loops' own time: 8.14 us -> 0 us
    pallas_call x0 -> x1, Pallas kernels: none -> 225 us  [run_layer(): pl.pallas_call(layer, out_shape=[jax.ShapeDtypeStruct(s, t) for _, s, t i...]
    all_gather x4 -> x0, waiting for transfers between devices: 174 us -> none  [the longest x1 45.4 us: shards(): first_all = lax.all_gather(first_low, 'mp', axis=0, tiled=True)]
    psum x1 -> x0, waiting for transfers between devices: 134 us -> none  [shards(): lax.psum((project_grad, pbias_grad, outw_grad), 'dp')]
    reduce_scatter x4 -> x0, waiting for transfers between devices: 127 us -> none  [the longest x1 44.1 us: shards(): lax.psum_scatter(jnp.dot(hidden_low, down_weight, preferred_element_type=...]
    dot_general x26 -> x0, matrix products: 80.4 us -> none  [the longest x4 19.1 us: times_transposed(): lax.dot_general(left, right, (((1,), (1,)), ((), ())), preferred_element_...]
    psum x2 -> x0, blocking collectives: 56.1 us -> none  [the longest x1 40.9 us: shards(): lax.psum((first_gain_grad, first_shift_grad, outbias_grad, second_gain_gr...]
    unnamed x67 -> x12, local copies, waits for them, and re-layouts: 18.5 us -> 1.6 us
    reduce_sum x10 -> x0, other arithmetic: 15 us -> none  [the longest x1 3.59 us: shards(): outbias_grad = jnp.sum(middle_low.astype(jnp.float32), 0)]
  transfers between devices with their start and end apart: 9 -> 0, of which waited for: 9 -> 0; matrix products, arithmetic and copies ran while one was open for 7% -> 0% of each run, Pallas kernels for 0% -> 0%
where the time goes in v3:
time: 242 us
  Pallas kernels  225 us (93%)
  other arithmetic  10.4 us (4%)
  local copies, waits for them, and re-layouts  5.44 us (2%)
    pallas_call x1, Pallas kernels, run_layer(): pl.pallas_call(layer, out_shape=[jax.ShapeDtypeStruct(s, t) for _, s, t i...  225 us
    convert_element_type x4, other arithmetic, shards(): reduced = (sums, *[g.astype(jnp.float32) for g in grads])  9.71 us

profile of v3, /device:TPU:0, one launch (start us, length us, event | category | flops | bytes accessed | tf_op | source)
XLA Modules:
  0.0 241.6 jit_solution(2962435332789376123)
XLA Ops:
  0.6 1.3 broadcast_in_dim.2.seg_ref
  2.0 225.1 %layer.1 = (bf16[256,1024]{1,0:T(8,128)(2,1)}, bf16[256,1024]{1,0:T(8,128)(2,1)}, f32[16,1024]{1,0:T(8,128)}, bf16[3,1024,256]{2,1,0:T(8,128)(2,1)}, bf16[256,10...) custom-call(bf16[256,1024]{1,0:T(8,128)(2,1)} %x_ref.1, bf16[256,1024]{1,0:T(8,128)(2,1)} %cot.1, ...), custom_call_target="tpu_custom_call" | custom-call | tf_op jit(solution)/shard_map/layer/pallas_call | solution.py:780
  227.0 1.8 fusion.1
  228.8 0.8 slice.28
  229.6 0.7 fusion
  230.2 0.0 copy-start
  230.2 4.2 %convert_element_type.14 = f32[1024,1024]{1,0:T(8,128)} convert(bf16[1024,1024]{1,0:T(8,128)(2,1)} %get-tuple-element.26) | non-fusion elementwise | flops 1048576 | bytes 6291456 | tf_op jit(solution)/shard_map/convert_element_type | solution.py:817
  234.5 0.0 copy-done
  234.5 0.0 copy-start.1
  234.5 2.5 %convert_element_type.15 = f32[1024,1024]{1,0:T(8,128)} convert(bf16[1024,1024]{1,0:T(8,128)(2,1)S(1)} %copy-done) | non-fusion elementwise | flops 1048576 | bytes 6291456 | tf_op jit(solution)/shard_map/convert_element_type | solution.py:817
  237.0 0.0 copy-done.1
  237.0 0.0 copy-start.2
  237.0 0.0 copy-start.4
  237.0 1.9 convert_element_type.12
  238.9 0.0 copy-start.3
  238.9 0.0 copy-done.2
  238.9 1.1 convert_element_type.13
  240.0 0.0 copy-done.4
  240.0 0.8 copy.31
  240.8 0.0 copy-done.3
  240.8 0.8 copy.32
Async XLA Ops:
  230.2 4.2 %copy-start = (bf16[1024,1024]{1,0:T(8,128)(2,1)S(1)}, bf16[1024,1024]{1,0:T(8,128)(2,1)}, u32[]{:S(2)}) copy-start(bf16[1024,1024]{1,0:T(8,128)(2,1)} %get-tuple-element.27) | copy-start | bytes 6291460
  234.5 2.5 %copy-start.1 = (bf16[3,1024,256]{2,1,0:T(8,128)(2,1)S(1)}, bf16[3,1024,256]{2,1,0:T(8,128)(2,1)}, u32[]{:S(2)}) copy-start(bf16[3,1024,256]{2,1,0:T(8,128)(2,1)} %get-tuple-element.24) | copy-start | bytes 4718596
  237.0 1.9 copy-start.2
  237.0 3.0 %copy-start.4 = (bf16[256,1024]{1,0:T(8,128)(2,1)S(1)}, bf16[256,1024]{1,0:T(8,128)(2,1)}, u32[]{:S(2)}) copy-start(bf16[256,1024]{1,0:T(8,128)(2,1)} %get-tuple-element.50) | copy-start | bytes 1572868
  238.9 1.9 copy-start.3

commit v4 on v3

v4 whole, which is shorter than its diff:
```python
import math

import jax
import jax.numpy as jnp
from jax import lax
from jax.experimental import pallas as pl
from jax.experimental.pallas import tpu as pltpu
from jax.sharding import PartitionSpec as P

HD = 128
EPS = 1e-05
BF = jnp.bfloat16
F32 = jnp.float32
MESH = pl.DeviceIdType.MESH
VMEM = pltpu.VMEM
DMA = pltpu.SemaphoreType.DMA
GELU_A = 0.7978845608
GELU_B = 0.044715


def mm(left, right):
    return jnp.dot(left, right, preferred_element_type=F32)


def mm_nt(left, right):
    return lax.dot_general(left, right, (((1,), (1,)), ((), ())), preferred_element_type=F32)


def mm_tn(left, right):
    return lax.dot_general(left, right, (((0,), (0,)), ((), ())), preferred_element_type=F32)


def remote(src, dst, ss, rs, device):
    return pltpu.make_async_remote_copy(
        src_ref=src, dst_ref=dst, send_sem=ss, recv_sem=rs, device_id=device, device_id_type=MESH
    )


def local(src, dst, sem):
    return pltpu.make_async_copy(src, dst, sem)


def barrier(devices):
    sem = pltpu.get_barrier_semaphore()
    for device in devices:
        pl.semaphore_signal(sem, 1, device_id=device, device_id_type=MESH)
    return lambda: pl.semaphore_wait(sem, len(devices))


def start(copy):
    copy.start()


def wait(copy):
    copy.wait()


def sent(copy):
    copy.wait_send()


def came(copy):
    copy.wait_recv()


def norm(values):
    mean = jnp.mean(values, -1, keepdims=True)
    centered = values - mean
    var = jnp.mean(centered * centered, -1, keepdims=True)
    scale = lax.rsqrt(var + EPS)
    return centered * scale, scale


def norm_back(grad, normed, scale, gain):
    scaled = grad * gain
    return scale * (
        scaled - jnp.mean(scaled, -1, keepdims=True) - normed * jnp.mean(scaled * normed, -1, keepdims=True)
    )


def gelu_parts(v):
    square = v * v
    t = jnp.tanh(GELU_A * v * (1.0 + GELU_B * square))
    half = 0.5 * (1.0 + t)
    slope = half + 0.5 * v * (1.0 - t * t) * (GELU_A * (1.0 + 3.0 * GELU_B * square))
    return v * half, slope


class Place:
    def __init__(self):
        self.z = lax.axis_index("mp")
        self.dp = lax.axis_index("dp")
        self.d = lax.rem(self.dp, 8)
        self.base = self.dp - self.d
        self.core = lax.rem(self.d, 2)
        self.column = self.d // 2
        bit_x = lax.rem(self.column, 2)
        bit_y = self.column // 2
        self.step_x = 1 - 2 * bit_x
        self.step_y = 2 - 4 * bit_y
        self.sibling = self.dp + 1 - 2 * self.core
        self.swapped = lax.rem(self.core + self.z // 2, 2)
        self.far = lax.rem(self.z + 2, 4)
        self.rank = lax.rem(self.z + 2 * self.swapped, 4)
        self.odd = lax.rem(self.z, 2)

    def column_at(self, i):
        return self.column + (i % 2) * self.step_x + (i // 2) * self.step_y

    def chip(self, i):
        return {"dp": self.base + 2 * self.column_at(i) + self.core, "mp": self.z}

    def along(self, z):
        return {"dp": self.dp, "mp": z}

    def to_sibling(self):
        return {"dp": self.sibling, "mp": self.z}

    def across(self):
        return {"dp": self.dp, "mp": self.z + 1 - 2 * self.odd}

    def partner(self):
        return {"dp": self.sibling, "mp": self.far}

    def rank_of(self, k):
        return lax.rem(self.rank + (k // 2) * (1 - 2 * self.odd) + 2 * (k % 2), 4)

    def at_home(self, body):
        pl.when(self.swapped == 0)(body)

    def if_swapped(self, body):
        pl.when(self.swapped == 1)(body)


class Gather:
    def __init__(self, p, buf, ss, rs):
        self.p, self.buf, self.ss, self.rs = p, buf, ss, rs
        self.half = buf.shape[1] // 2

    def _copy(self, k, i, c, device):
        view = self.buf.at[self.p.rank_of(k), pl.ds(c * self.half, self.half)]
        return remote(view, view, self.ss.at[i, c], self.rs.at[i, c], device)

    def send(self, c):
        self._copy(0, 0, c, self.p.across()).start()
        self._copy(0, 1, c, self.p.to_sibling()).start()

    def take(self, c):
        self._copy(2, 0, c, self.p.across()).wait_recv()
        self._copy(2, 2, c, self.p.to_sibling()).start()

    def near(self, c):
        self._copy(1, 1, c, self.p.to_sibling()).wait_recv()

    def last(self, c):
        self._copy(3, 2, c, self.p.to_sibling()).wait_recv()

    def both(self, step):
        step(0)
        step(1)

    def finish(self):
        for c in range(2):
            self._copy(0, 0, c, self.p.across()).wait_send()
            self._copy(0, 1, c, self.p.to_sibling()).wait_send()
            self._copy(2, 2, c, self.p.to_sibling()).wait_send()


class Sum:
    def __init__(self, p, parts, got, out, into, ss, rs):
        self.p, self.parts, self.got, self.out, self.into, self.ss, self.rs = p, parts, got, out, into, ss, rs
        self.half = parts.shape[1] // 2

    def _cut(self, c):
        return pl.ds(c * self.half, self.half)

    def _give(self, n, c):
        src = self.parts.at[self.p.rank_of(1 + 2 * n), self._cut(c)]
        return remote(src, self.got.at[n, self._cut(c)], self.ss.at[n, c], self.rs.at[n, c], self.p.to_sibling())

    def _ship(self, c):
        cut = self._cut(c)
        return remote(self.out.at[cut], self.into.at[cut], self.ss.at[2, c], self.rs.at[2, c], self.p.across())

    def _part(self, k, c):
        return self.parts[pl.ds(self.p.rank_of(k), 1), self._cut(c)][0].astype(F32)

    def give_far(self, c):
        self._give(1, c).start()

    def give_near(self, c):
        self._give(0, c).start()

    def ship(self, c):
        self._give(1, c).wait_recv()
        self.out[self._cut(c), :] = (self._part(2, c) + self.got[1, self._cut(c)].astype(F32)).astype(BF)
        self._ship(c).start()

    def done(self, r):
        for k, step in ((3, self.give_far), (2, self.ship), (1, self.give_near)):

            @pl.when(r == self.p.rank_of(k))
            def _():
                step(0)
                step(1)

    def total(self, c):
        self._give(0, c).wait_recv()
        total = self._part(0, c) + self.got[0, self._cut(c)].astype(F32)
        self._ship(c).wait_recv()
        return total + self.into[self._cut(c), :].astype(F32)

    def finish(self):
        for c in range(2):
            self._give(0, c).wait_send()
            self._give(1, c).wait_send()
            self._ship(c).wait_send()


class Weight:
    def __init__(self, p, src, buf, ss, rs, pieces):
        self.p, self.src, self.buf, self.ss, self.rs, self.pieces = p, src, buf, ss, rs, pieces
        self.size = buf.shape[0] // (4 * pieces)

    def _cut(self, ref, column, n):
        return ref.at[pl.ds(pl.multiple_of((column * self.pieces + n) * self.size, self.size), self.size)]

    def _own(self):
        return local(self.src, self.buf, self.ss.at[0, 0])

    def _swap(self, n):
        src, dst = self._cut(self.src, self.p.column, n), self._cut(self.buf, self.p.column, n)
        return remote(src, dst, self.ss.at[0, n], self.rs.at[0, n], self.p.partner())

    def _share(self, i, column, n):
        view = self._cut(self.buf, column, n)
        return remote(view, view, self.ss.at[i, n], self.rs.at[i, n], self.p.chip(i))

    def home(self):
        self._own().start()

    def swap(self, n=0):
        self._swap(n).start()

    def take(self, n=0):
        self._swap(n).wait_recv()
        for i in (1, 2, 3):
            self._share(i, self.p.column, n).start()

    def ready(self):
        self.p.at_home(lambda: self._own().wait())

        @self.p.if_swapped
        def _():
            for n in range(self.pieces):
                for i in (1, 2, 3):
                    self._share(i, self.p.column_at(i), n).wait_recv()

    def finish(self):
        for n in range(self.pieces):
            self._swap(n).wait_send()
            for i in (1, 2, 3):
                self._share(i, self.p.column, n).wait_send()


class Grad:
    def __init__(self, p, buf, into, last, total, far, out, ss, rs):
        self.p, self.buf, self.into, self.last, self.sum, self.far, self.out = p, buf, into, last, total, far, out
        self.ss, self.rs = ss, rs
        self.size = buf.shape[0] // 8

    def _at(self, ref, column, n):
        return ref.at[pl.ds(pl.multiple_of((2 * column + n) * self.size, self.size), self.size)]

    def _own(self, n):
        return self.sum.at[pl.ds(n * self.size, self.size)]

    def _step(self, n, m):
        return m if n == 0 or m == 3 else 3 - m

    def _column(self, n, m):
        return self.p.column_at(self._step(n, m)) if m else self.p.column

    def _chip(self, n, m):
        return self.p.chip(self._step(n, m))

    def _copy(self, src, dst, i, n, device):
        return remote(src, dst, self.ss.at[i, n], self.rs.at[i, n], device)

    def _first(self, n, k):
        src = self._at(self.buf, self._column(n, (1, 3)[k]), n)
        return self._copy(src, self.into.at[n, k], k, n, self._chip(n, 1))

    def _second(self, n):
        return self._copy(self.into.at[n, 1], self.last.at[n], 2, n, self._chip(n, 2))

    def _home(self):
        return self._copy(self.sum, self.far, 3, 0, self.p.along(self.p.far))

    def _keep(self):
        return local(self.sum, self.out.at[pl.ds(pl.multiple_of(2 * self.p.column * self.size, 2 * self.size), 2 * self.size)], self.ss.at[3, 1])

    def _spread(self, n, m):
        return self._copy(self._own(n), self._at(self.out, self.p.column, n), 3 + m, n, self._chip(n, m))

    def _arrived(self, n, m):
        return self._copy(self._own(n), self._at(self.out, self._column(n, m), n), 3 + m, n, self._chip(n, m))

    def _pass(self, n):
        view = self._at(self.out, self._column(n, 2), n)
        return self._copy(view, view, 6, n, self._chip(n, 1))

    def _passed(self, n):
        view = self._at(self.out, self._column(n, 3), n)
        return self._copy(view, view, 6, n, self._chip(n, 1))

    def _hand(self, n, m):
        view = self._at(self.out, self._column(n, m), n)
        return self._copy(view if m else self._own(n), view, 7 + m, n, self.p.to_sibling())

    def scatter(self):
        for n in range(2):
            self._first(n, 1).start()
            self._first(n, 0).start()

    def middle(self):
        for n in range(2):
            self._first(n, 1).wait_recv()
            value = self._at(self.buf, self._column(n, 2), n)[...].astype(F32) + self.into[n, 1].astype(F32)
            self.into[n, 1] = value.astype(BF)
            self._second(n).start()

    def combine(self):
        for n in range(2):
            self._first(n, 0).wait_recv()
            self._second(n).wait_recv()
            total = self._at(self.buf, self.p.column, n)[...].astype(F32) + self.into[n, 0].astype(F32)
            self._own(n)[...] = (total + self.last[n].astype(F32)).astype(BF)
        self.p.if_swapped(lambda: self._home().start())

    def final(self):
        self._home().wait_recv()
        self.sum[...] = (self.sum[...].astype(F32) + self.far[...].astype(F32)).astype(BF)
        for n in range(2):
            self._spread(n, 2).start()
            self._spread(n, 1).start()
        for n in range(2):
            self._hand(n, 0).start()
        self._keep().start()

    def relay(self):
        for n in range(2):
            self._arrived(n, 2).wait_recv()
            self._pass(n).start()
            self._hand(n, 2).start()

    def relay_last(self):
        for n in range(2):
            self._arrived(n, 1).wait_recv()
            self._hand(n, 1).start()
            self._passed(n).wait_recv()
            self._hand(n, 3).start()

    def finish(self):
        for n in range(2):
            self._first(n, 0).wait_send()
            self._first(n, 1).wait_send()
            self._second(n).wait_send()

        @self.p.at_home
        def _():
            for n in range(2):
                for m in (1, 2):
                    self._spread(n, m).wait_send()
                self._pass(n).wait_send()
                for m in range(4):
                    self._hand(n, m).wait_send()
            self._keep().wait()

        @self.p.if_swapped
        def _():
            self._home().wait_send()
            for n in range(2):
                for m in range(4):
                    self._hand(n, m).wait_recv()


class Plane:
    def __init__(self, p, buf, ss, rs):
        self.p, self.buf, self.ss, self.rs = p, buf, ss, rs

    def _copy(self, column, core, i, device):
        view = self.buf.at[2 * column + core]
        return remote(view, view, self.ss.at[i], self.rs.at[i], device)

    def send(self):
        p = self.p
        for i in (1, 2, 3):
            self._copy(p.column, p.core, i, p.chip(i)).start()
        self._copy(p.column, p.core, 0, p.to_sibling()).start()

    def take(self):
        p = self.p
        for i in (1, 2, 3):
            self._copy(p.column_at(i), p.core, i, p.chip(i)).wait_recv()
            self._copy(p.column_at(i), p.core, 3 + i, p.to_sibling()).start()

    def rest(self):
        p = self.p
        self._copy(p.column, 1 - p.core, 0, p.to_sibling()).wait_recv()
        for i in (1, 2, 3):
            self._copy(p.column_at(i), 1 - p.core, 3 + i, p.to_sibling()).wait_recv()

    def finish(self):
        p = self.p
        self._copy(p.column, p.core, 0, p.to_sibling()).wait_send()
        for i in (1, 2, 3):
            self._copy(p.column, p.core, i, p.chip(i)).wait_send()
            self._copy(p.column_at(i), p.core, 3 + i, p.to_sibling()).wait_send()


def layer(
    x_ref, cot, seg_ref, g1_ref, b1_ref, wq_ref, bq_ref, ow_ref, ob_ref, g2_ref, b2_ref, up_ref, ub_ref, dn_ref, db_ref,
    output, tokens_grad, small_out, pg_out, og_out, ug_out, dg_out,
    xs, seg, segc, first, second, dy, dmid, mixed, own, probs, delta, wq, bq, ow, up, ub, dn,
    a_part, a_got, a_out, a_in, s_part, s_got, s_out, s_in, o_part, o_got, o_out, o_in,
    hidden, dpre, dg, ug, pg, og, dg_in, ug_in, pg_in, og_in, dg_last, ug_last, pg_last, og_last, dg_sum, ug_sum, pg_sum, og_sum,
    dg_far, ug_far, pg_far, og_far, g1, b1, ob, g2, b2, dwb, acc, middle, dmiddle, rows_out, sm, sm_in, smp,
    ss_vec, ss_in, rs_in, ss_first, rs_first, ss_second, rs_second, ss_dy, rs_dy, ss_dmid, rs_dmid,
    ss_a, rs_a, ss_s, rs_s, ss_o, rs_o, ss_f, rs_f, ss_wq, rs_wq, ss_ow, rs_ow, ss_up, rs_up, ss_dn, rs_dn,
    ss_dg, rs_dg, ss_ug, rs_ug, ss_pg, rs_pg, ss_og, rs_og, ss_sm, rs_sm, ss_sp, rs_sp,
):
    p = Place()
    rows, width = xs.shape
    half = rows // 2
    share = wq.shape[2]
    heads = share // HD
    factor = 1.0 / math.sqrt(HD)
    length = 4 * rows
    others = [lax.rem(p.z + k, 4) for k in (1, 2, 3)]
    enter = barrier([p.to_sibling(), p.partner()] + [p.along(t) for t in others] + [p.chip(i) for i in (1, 2, 3)])
    rank = p.rank
    halves = [slice(0, half), slice(half, rows)]

    def strip(index):
        return pl.ds(pl.multiple_of(index * rows, rows), rows)

    wq_moves = [Weight(p, wq_ref.at[t], wq.at[t], ss_wq.at[t], rs_wq.at[t], 1) for t in range(3)]
    ow_move = Weight(p, ow_ref, ow, ss_ow, rs_ow, 1)
    up_move = Weight(p, up_ref, up, ss_up, rs_up, 2)
    dn_move = Weight(p, dn_ref, dn, ss_dn, rs_dn, 2)
    moves = (*wq_moves, ow_move, up_move, dn_move)
    first_all = Gather(p, first, ss_first, rs_first)
    second_all = Gather(p, second, ss_second, rs_second)
    dy_all = Gather(p, dy, ss_dy, rs_dy)
    dmid_all = Gather(p, dmid, ss_dmid, rs_dmid)
    a_sum = Sum(p, a_part, a_got, a_out, a_in, ss_a, rs_a)
    s_sum = Sum(p, s_part, s_got, s_out, s_in, ss_s, rs_s)
    o_sum = Sum(p, o_part, o_got, o_out, o_in, ss_o, rs_o)
    f_sum = Sum(p, a_part, a_got, a_out, a_in, ss_f, rs_f)
    dn_grad = Grad(p, dg, dg_in, dg_last, dg_sum, dg_far, dg_out, ss_dg, rs_dg)
    up_grad = Grad(p, ug, ug_in, ug_last, ug_sum, ug_far, ug_out, ss_ug, rs_ug)
    ow_grad = Grad(p, og, og_in, og_last, og_sum, og_far, og_out, ss_og, rs_og)
    pj_grads = [
        Grad(
            p, pg.at[t], pg_in.at[t], pg_last.at[t], pg_sum.at[t], pg_far.at[t], pg_out.at[t], ss_pg.at[t], rs_pg.at[t]
        )
        for t in range(3)
    ]

    def x_home():
        return local(x_ref, xs, ss_in.at[0])

    def cot_home():
        return local(cot, dy.at[rank], ss_in.at[1])

    def x_swap(c):
        cut = pl.ds(c * half, half)
        return remote(x_ref.at[cut], xs.at[cut], ss_in.at[7 + c], rs_in.at[7 + c], p.partner())

    def cot_swap(slot):
        return remote(cot, dy.at[slot], ss_in.at[1], rs_in.at[1], p.partner())

    def bq_swap():
        return remote(bq_ref, bq, ss_in.at[2], rs_in.at[2], p.partner())

    def ub_swap():
        return remote(ub_ref, ub, ss_in.at[3], rs_in.at[3], p.partner())

    def seg_give():
        return remote(seg_ref, seg, ss_in.at[4], rs_in.at[4], p.to_sibling())

    def back_swap(n, out, c):
        cut = pl.ds(c * half, half)
        i = 9 + 2 * n + c
        return remote(rows_out.at[n, cut], out.at[cut], ss_in.at[i], rs_in.at[i], p.partner())

    def back_home(n, out, c):
        cut = pl.ds(c * half, half)
        return local(rows_out.at[n, cut], out.at[cut], ss_in.at[9 + 2 * n + c])

    def put_back(n, out, c):
        p.at_home(lambda: back_home(n, out, c).start())
        p.if_swapped(lambda: back_swap(n, out, c).start())

    vectors = [
        local(a, b, ss_vec.at[i])
        for i, (a, b) in enumerate(
            ((g1_ref, g1), (b1_ref, b1), (ob_ref, ob), (g2_ref, g2), (b2_ref, b2), (db_ref, dwb))
        )
    ]
    kept = [local(a, b, ss_vec.at[6 + i]) for i, (a, b) in enumerate(((bq_ref, bq), (ub_ref, ub), (seg_ref, seg)))]

    @p.at_home
    def _():
        x_home().start()

    for copy in vectors:
        copy.start()

    @p.at_home
    def _():
        for copy in kept:
            copy.start()
        for move in moves:
            move.home()
        cot_home().start()

    enter()

    @p.if_swapped
    def _():
        x_swap(0).start()
        x_swap(1).start()

    @p.at_home
    def _():
        seg_give().start()
        x_home().wait()
        for copy in kept:
            copy.wait()

    for copy in vectors:
        copy.wait()
    for c in range(2):

        @p.if_swapped
        def _():
            x_swap(c).wait_recv()
            wq_moves[c].swap()

        normed, _ = norm(xs[halves[c], :].astype(F32))
        first[pl.ds(rank, 1), halves[c]] = (normed * g1[...] + b1[...]).astype(BF)[None]
        first_all.send(c)

    @p.if_swapped
    def _():
        bq_swap().start()
        wq_moves[2].swap()
        wq_moves[0].take()
        ow_move.swap()
        wq_moves[1].take()
        ub_swap().start()
        up_move.swap(0)
        wq_moves[2].take()
        up_move.swap(1)
        seg_give().wait_recv()
        bq_swap().wait_recv()

    segc[...] = jnp.transpose(jnp.broadcast_to(seg[0:1, :], (HD, length)))

    def project(k):
        s = p.rank_of(k)
        block = first[pl.ds(s, 1)][0]
        for t in range(3):
            value = mm(block, wq[t]) + bq[t : t + 1, :]
            mixed[strip(s), t * share : (t + 1) * share] = value.astype(BF)

    @p.at_home
    def _():
        for move in wq_moves:
            move.ready()
        project(0)

    first_all.both(first_all.take)

    @p.at_home
    def _():
        project(2)

    @p.if_swapped
    def _():
        for move in wq_moves:
            move.ready()
        project(0)
        project(2)
        ow_move.take()

    first_all.both(first_all.near)
    project(1)
    first_all.both(first_all.last)
    project(3)

    @p.if_swapped
    def _():
        up_move.take(0)
        dn_move.swap(0)
        dn_move.swap(1)
        ub_swap().wait_recv()

    @p.at_home
    def _():
        cot_home().wait()
        dy_all.both(dy_all.send)

    ow_move.ready()
    for r in reversed(range(4)):
        span = (r + 1) * rows
        top = r * rows
        place_q = top + lax.broadcasted_iota(jnp.int32, (rows, span), 0)
        place_k = lax.broadcasted_iota(jnp.int32, (rows, span), 1)
        allowed = (segc[top : top + rows, 0:1] == seg[0:1, 0:span]) & (place_q >= place_k)
        for h in range(heads):
            q = mixed[top : top + rows, h * HD : (h + 1) * HD]
            k = mixed[0:span, share + h * HD : share + (h + 1) * HD]
            v = mixed[0:span, 2 * share + h * HD : 2 * share + (h + 1) * HD]
            scores = jnp.where(allowed, mm_nt(q, k) * factor, -1e30)
            expo = jnp.exp(scores - jnp.max(scores, -1, keepdims=True))
            low = (expo / jnp.sum(expo, -1, keepdims=True)).astype(BF)
            for j in range(r + 1):
                probs[h, r * (r + 1) // 2 + j] = low[:, j * rows : (j + 1) * rows]
            own[r, :, h * HD : (h + 1) * HD] = mm(low, v).astype(BF)
        a_part[r] = mm(own[r], ow[...]).astype(BF)
        a_sum.done(r)

    @p.if_swapped
    def _():
        cot_swap(p.z).start()
        up_move.take(1)

    for c in range(2):
        cut = halves[c]
        middle[cut, :] = xs[cut, :].astype(F32) + (a_sum.total(c) + ob[...])
        normed, _ = norm(middle[cut, :])
        second[pl.ds(rank, 1), cut] = (normed * g2[...] + b2[...]).astype(BF)[None]
        second_all.send(c)

    @p.if_swapped
    def _():
        dn_move.take(0)
        dn_move.take(1)


    up_move.ready()

    class Rows:
        def __init__(self, k):
            late = k // 2
            self.top = p.rank_of(k - late * (k - 2))
            self.low = p.rank_of(k + late * (3 - k))
            self.at_top = pl.ds(pl.multiple_of(late * (k - 2) * half, half), half)
            self.at_low = pl.ds(pl.multiple_of(half - late * (3 - k) * half, half), half)

        def load(self, ref):
            return jnp.concatenate([ref[pl.ds(self.top, 1), self.at_top][0], ref[pl.ds(self.low, 1), self.at_low][0]], 0)

        def store(self, ref, value):
            ref[pl.ds(self.top, 1), self.at_top] = value[None, :half]
            ref[pl.ds(self.low, 1), self.at_low] = value[None, half:]

    def feed(k, carry):
        @pl.when(k == 1)
        def _():
            second_all.both(second_all.near)

        @pl.when(k == 2)
        def _():
            @p.if_swapped
            def _():
                cot_swap(rank).wait_recv()
                dy_all.both(dy_all.send)

            second_all.take(0)
            second_all.last(0)

        @pl.when(k == 3)
        def _():
            second_all.take(1)
            second_all.last(1)

        at = Rows(k)
        value, slope = gelu_parts(mm(at.load(second), up[...]) + ub[...])
        at.store(hidden, value.astype(BF))
        at.store(dpre, slope.astype(BF))
        return carry

    lax.fori_loop(0, 4, feed, 0)

    dn_move.ready()
    dy_all.both(dy_all.take)
    dy_all.both(dy_all.near)
    dy_all.both(dy_all.last)

    def feed_back(n, carry):
        k = 2 + n - 4 * (n // 2)
        at = Rows(k)
        back = (mm_nt(at.load(dy), dn[...]) * at.load(dpre).astype(F32)).astype(BF)
        at.store(dpre, back)
        at.store(s_part, mm_nt(back, up[...]).astype(BF))

        @pl.when(k == 2)
        def _():
            s_sum.give_far(0)

        @pl.when(k == 3)
        def _():
            s_sum.give_far(1)
            s_sum.ship(0)

        @pl.when(k == 0)
        def _():
            s_sum.ship(1)

        @pl.when(k == 1)
        def _():
            s_sum.give_near(0)
            s_sum.give_near(1)

        at.store(o_part, mm(at.load(hidden), dn[...]).astype(BF))
        return carry

    lax.fori_loop(0, 4, feed_back, 0)
    for c in range(2):
        o_sum.give_far(c)
        o_sum.give_near(c)
    units = hidden.shape[2]
    for c in range(4):
        cols = slice(c * units // 4, (c + 1) * units // 4)
        dg[cols, :] = mm_tn(hidden[:, :, cols].reshape(length, units // 4), dy[...].reshape(length, width)).astype(BF)
    dn_grad.scatter()

    sm[...] = jnp.zeros(sm.shape, F32)
    for c in range(2):
        cut = halves[c]
        grad = dy[pl.ds(rank, 1), cut][0].astype(F32)
        total = s_sum.total(c)
        normed, scale = norm(middle[cut, :])
        dmiddle[cut, :] = grad + norm_back(total, normed, scale, g2[...])
        low = dmiddle[cut, :].astype(BF)
        dmid[pl.ds(rank, 1), cut] = low[None]
        dmid_all.send(c)
        sm[0:1, :] += jnp.sum(total * normed, 0, keepdims=True)
        sm[1:2, :] += jnp.sum(total, 0, keepdims=True)
        sm[2:3, :] += jnp.sum(low.astype(F32), 0, keepdims=True)
        sm[3:4, :] += jnp.sum(grad, 0, keepdims=True)
    dn_grad.middle()
    for c in range(4):
        cols = slice(c * width // 4, (c + 1) * width // 4)
        ug[cols, :] = mm_tn(second[:, :, cols].reshape(length, width // 4), dpre[...].reshape(length, units)).astype(BF)
    up_grad.scatter()
    bias_sum = jnp.sum(dpre[...].reshape(length, units).astype(F32), 0, keepdims=True)
    for q in range(4):
        sm[8 + q : 9 + q, :] = jnp.where(rank == q, bias_sum, 0.0)
    for t in range(3):
        acc[t] = jnp.zeros((length, share), F32)
    a_sum.finish()

    ctx_cols = slice(3 * share, 4 * share)

    def to_context(k):
        s = pl.ds(p.rank_of(k), 1)
        value = mm_nt(dmid[s][0], ow[...]).astype(BF)
        hidden[s, :, ctx_cols] = value[None]
        for h in range(heads):
            cols = slice(h * HD, (h + 1) * HD)
            product = value[:, cols].astype(F32) * own[s, :, cols][0].astype(F32)
            delta[h, strip(p.rank_of(k)), 0:1] = jnp.sum(product, -1, keepdims=True)

    to_context(0)
    dmid_all.both(dmid_all.near)
    to_context(1)
    dmid_all.both(dmid_all.take)
    o_sum.ship(0)
    o_sum.ship(1)
    to_context(2)
    dmid_all.both(dmid_all.last)
    to_context(3)

    mirror = 1 - p.z // 2
    dn_grad.combine()
    for g in range(4):

        def block(e, carry):
            i = (g + e) + mirror * (3 - g - (g + e))
            j = g + mirror * (3 - (g + e) - g)
            qs, ks = strip(i), strip(j)
            for h in range(heads):
                cols = slice(h * HD, (h + 1) * HD)
                q = mixed[qs, cols]
                k = mixed[ks, share + h * HD : share + (h + 1) * HD]
                v = mixed[ks, 2 * share + h * HD : 2 * share + (h + 1) * HD]
                head = hidden[pl.ds(i, 1), :, 3 * share + h * HD : 3 * share + (h + 1) * HD][0]
                low = probs[h, pl.ds(i * (i + 1) // 2 + j, 1)][0]
                acc[2, ks, cols] += mm_tn(low, head)
                back = (low.astype(F32) * (mm_nt(head, v) - delta[h, qs, 0:1])).astype(BF)
                acc[0, qs, cols] += mm(back, k)
                acc[1, ks, cols] += mm_tn(back, q)
            return carry

        lax.fori_loop(0, 4 - g, block, 0)
        r = g + mirror * (3 - 2 * g)
        total = None
        for t in range(3):
            value = acc[t, strip(r), :]
            low = (value * factor if t < 2 else value).astype(BF)
            hidden[pl.ds(r, 1), :, t * share : (t + 1) * share] = low[None]
            term = mm_nt(low, wq[t])
            total = term if total is None else total + term
        a_part[pl.ds(r, 1)] = total.astype(BF)[None]
        f_sum.done(r)
        if g == 0:
            up_grad.middle()
        if g == 2:
            up_grad.combine()
            for c in range(2):
                cut = halves[c]
                rows_out[1, cut] = (middle[cut, :] + (o_sum.total(c) + dwb[...])).astype(BF)
                put_back(1, output, c)
        if g == 1:
            og[...] = mm_tn(own[...].reshape(length, share), dmid[...].reshape(length, width)).astype(BF)
            ow_grad.scatter()
    p.at_home(dn_grad.final)
    for t in range(3):
        cols = slice(t * share, (t + 1) * share)
        low = hidden[:, :, cols].reshape(length, share)
        pg[t] = mm_tn(first[...].reshape(length, width), low).astype(BF)
        pj_grads[t].scatter()
        bias = jnp.sum(low.astype(F32), 0, keepdims=True)
        line = (6, 7, 12)[t]
        for q in range(4):
            sm[line : line + 1, q * share : (q + 1) * share] = jnp.where(rank == q, bias, 0.0)
    for c in range(2):
        cut = halves[c]
        total = f_sum.total(c)
        normed, scale = norm(xs[cut, :].astype(F32))
        rows_out[0, cut] = (dmiddle[cut, :] + norm_back(total, normed, scale, g1[...])).astype(BF)
        put_back(0, tokens_grad, c)
        sm[4:5, :] += jnp.sum(total * normed, 0, keepdims=True)
        sm[5:6, :] += jnp.sum(total, 0, keepdims=True)

    def sm_copy(k, t):
        return remote(sm, sm_in.at[k], ss_sm.at[k], rs_sm.at[k], p.along(t))

    for k, t in enumerate(others):
        sm_copy(k, t).start()
    late = (ow_grad, *pj_grads)
    p.at_home(dn_grad.relay)
    for grad_sum in late:
        grad_sum.middle()
    p.at_home(up_grad.final)
    for grad_sum in late:
        grad_sum.combine()
    sm_sum = sm[...]
    for k, t in enumerate(others):
        sm_copy(k, t).wait_recv()
        sm_sum = sm_sum + sm_in[k]
    smp[pl.ds(p.d, 1)] = sm_sum[None]
    sm_all = Plane(p, smp, ss_sp, rs_sp)
    sm_all.send()
    p.at_home(dn_grad.relay_last)
    p.at_home(up_grad.relay)
    for grad_sum in late:
        p.at_home(grad_sum.final)
    sm_all.take()
    p.at_home(up_grad.relay_last)
    sm_all.rest()
    small_out[...] = jnp.sum(smp[...], 0)
    for grad_sum in late:
        p.at_home(grad_sum.relay)
    for grad_sum in late:
        p.at_home(grad_sum.relay_last)

    for group in (first_all, second_all, dy_all, dmid_all, s_sum, o_sum, f_sum, sm_all):
        group.finish()
    for k, t in enumerate(others):
        sm_copy(k, t).wait_send()

    @p.at_home
    def _():
        seg_give().wait_send()
        for c in range(2):
            back_home(0, tokens_grad, c).wait()
            back_home(1, output, c).wait()

    @p.if_swapped
    def _():
        for copy in (x_swap(0), x_swap(1), bq_swap(), ub_swap(), cot_swap(rank)):
            copy.wait_send()
        for c in range(2):
            back_swap(0, tokens_grad, c).wait()
            back_swap(1, output, c).wait()
        for move in moves:
            move.finish()

    for grad_sum in (dn_grad, up_grad, ow_grad, *pj_grads):
        grad_sum.finish()


def run_layer(x, cot, seg_ids, g1, b1, wq, bq, ow, ob, g2, b2, upw, upb, dnw, dnb):
    rows, width = x.shape
    share = wq.shape[2]
    length = 4 * rows
    heads = share // HD
    units = upw.shape[1]
    vm = pl.BlockSpec(memory_space=VMEM)
    hbm = pl.BlockSpec(memory_space=pl.ANY)
    token = (rows, width)
    outs = [
        (hbm, token, BF), (hbm, token, BF), (vm, (16, width), F32), (hbm, (3, width, share), BF),
        (hbm, (share, width), BF), (hbm, (width, units), BF), (hbm, (units, width), BF),
    ]
    four = VMEM((4,) + token, BF)
    sums = [VMEM((2,) + token, BF), VMEM(token, BF), VMEM(token, BF)]
    dn_q, up_q, ow_q = (units // 4, width), (width // 4, units), (share // 4, width)
    pj_q = (width // 4, share)
    eighths = [((), (units // 8, width)), ((), (width // 8, units)), ((3,), (width // 8, share)), ((), (share // 8, width))]
    pair = lambda *n: [DMA(n), DMA(n)]
    return pl.pallas_call(
        layer,
        out_shape=[jax.ShapeDtypeStruct(s, t) for _, s, t in outs],
        in_specs=[hbm] * 15,
        out_specs=[m for m, _, _ in outs],
        scratch_shapes=[
            VMEM(token, BF), VMEM((1, length), jnp.int32), VMEM((length, HD), jnp.int32), four, four, four, four,
            VMEM((length, 3 * share), BF), VMEM((4, rows, share), BF), VMEM((heads, 10, rows, rows), BF),
            VMEM((heads, length, 1), F32),
            VMEM((3, width, share), BF), VMEM((3, share), F32), VMEM((share, width), BF), VMEM((width, units), BF),
            VMEM((1, units), F32), VMEM((units, width), BF),
            four, *sums, four, *sums, four, *sums,
            VMEM((4, rows, units), BF), VMEM((4, rows, units), BF),
            VMEM((units, width), BF), VMEM((width, units), BF), VMEM((3, width, share), BF), VMEM((share, width), BF),
            *[VMEM(lead + (2, 2) + q, BF) for lead, q in eighths], *[VMEM(lead + (2,) + q, BF) for lead, q in eighths],
            *2 * [VMEM(dn_q, BF), VMEM(up_q, BF), VMEM((3,) + pj_q, BF), VMEM(ow_q, BF)],
            *6 * [VMEM((1, width), F32)], VMEM((3, length, share), F32), VMEM(token, F32), VMEM(token, F32), VMEM((2,) + token, BF),
            VMEM((16, width), F32), VMEM((3, 16, width), F32), VMEM((8, 16, width), F32),
            DMA((9,)), *pair(13), *pair(3, 2), *pair(3, 2), *pair(3, 2), *pair(3, 2), *pair(3, 2), *pair(3, 2), *pair(3, 2),
            *pair(3, 2), *pair(3, 4, 1), *pair(4, 1), *pair(4, 2), *pair(4, 2), *pair(11, 2), *pair(11, 2), *pair(3, 11, 2), *pair(11, 2),
            *pair(3), *pair(7),
        ],
        compiler_params=pltpu.CompilerParams(collective_id=0, has_side_effects=True, vmem_limit_bytes=64 << 20),
        name="layer",
    )(
        x, cot, seg_ids.reshape(1, length), g1.reshape(1, width), b1.reshape(1, width), wq, bq, ow,
        ob.reshape(1, width), g2.reshape(1, width), b2.reshape(1, width), upw, upb.reshape(1, units), dnw,
        dnb.reshape(1, width),
    )


def widen(sm, out, tg, pg, og, ug, dg, out_o, tg_o, pg_o, og_o, ug_o, dg_o, pb_o, ub_o, *rest):
    for src, dst in ((out, out_o), (tg, tg_o), (pg, pg_o), (og, og_o), (ug, ug_o), (dg, dg_o)):
        dst[...] = src[...].astype(dst.dtype)

    @pl.when(pl.program_id(0) == 0)
    def _():
        z = lax.axis_index("mp")
        share = pb_o.shape[1]
        for t, line in enumerate((6, 7, 12)):
            pb_o[t : t + 1, :] = sm[line : line + 1, pl.ds(pl.multiple_of(z * share, share), share)]
        ub_o[...] = sm[pl.ds(8 + z, 1), :][0]
        for line, dst in enumerate(rest):
            dst[...] = sm[line, :]


def run_widen(sm, out, tg, pg, og, ug, dg):
    steps = 4

    def cut(v, axis):
        shape = list(v.shape)
        shape[axis] //= steps
        return pl.BlockSpec(tuple(shape), lambda i: tuple(i if a == axis else 0 for a in range(v.ndim)))

    def whole(shape):
        return pl.BlockSpec(shape, lambda i: tuple(0 for _ in shape))

    wide = [(out, 0, BF), (tg, 0, BF), (pg, 1, F32), (og, 0, F32), (ug, 0, F32), (dg, 0, F32)]
    width = sm.shape[1]
    small = [(3, pg.shape[2]), (width,)] + [(width,)] * 6
    return pl.pallas_call(
        widen,
        grid=(steps,),
        out_shape=[jax.ShapeDtypeStruct(v.shape, t) for v, _, t in wide] + [jax.ShapeDtypeStruct(s, F32) for s in small],
        in_specs=[whole(sm.shape)] + [cut(v, a) for v, a, _ in wide],
        out_specs=[cut(v, a) for v, a, _ in wide] + [whole(s) for s in small],
        compiler_params=pltpu.CompilerParams(vmem_limit_bytes=60 << 20),
        name="widen",
    )(sm, out, tg, pg, og, ug, dg)


def shards(
    tokens, seg_ids, cotangent, first_gain, first_shift, project_weight, project_bias, out_weight, out_bias,
    second_gain, second_shift, up_weight, up_bias, down_weight, down_bias,
):
    output, tokens_grad, *sums = run_layer(
        tokens, cotangent, seg_ids, first_gain, first_shift, project_weight, project_bias, out_weight, out_bias,
        second_gain, second_shift, up_weight, up_bias, down_weight, down_bias,
    )
    if lax.axis_size("dp") > 8:
        sums = [v.astype(jnp.float32) * 0.125 for v in sums]
        sums = list(lax.psum(tuple(sums), "dp"))
    output, tokens_grad, pg, og, ug, dg, pb, ub, g2g, b2g, obg, dbg, g1g, b1g = run_widen(
        sums[0], output, tokens_grad, *sums[1:]
    )
    return output, tokens_grad, g1g, b1g, pg, pb, og, obg, g2g, b2g, ug, ub, dg, dbg


def solution(mesh):
    in_specs = (
        P(("dp", "mp"), None),
        P("dp"),
        P(("dp", "mp"), None),
        P(),
        P(),
        P(None, None, "mp"),
        P(None, "mp"),
        P("mp", None),
        P(),
        P(),
        P(),
        P(None, "mp"),
        P("mp"),
        P("mp", None),
        P(),
    )
    out_specs = (
        P(("dp", "mp"), None),
        P(("dp", "mp"), None),
        P(),
        P(),
        P(None, None, "mp"),
        P(None, "mp"),
        P("mp", None),
        P(),
        P(),
        P(),
        P(None, "mp"),
        P("mp"),
        P("mp", None),
        P(),
    )
    return jax.shard_map(shards, mesh=mesh, in_specs=in_specs, out_specs=out_specs, check_vma=False)
```

time: 242 us -> 209 us (0.86)
  Pallas kernels: 225 us -> 208 us
  other arithmetic: 10.4 us -> 0 us
  local copies, waits for them, and re-layouts: 5.44 us -> 0 us
    pallas_call x1, Pallas kernels: 225 us -> 200 us  [run_layer(): pl.pallas_call(layer, out_shape=[jax.ShapeDtypeStruct(s, t) for _, s, t i...]
    convert_element_type x4 -> x0, other arithmetic: 9.71 us -> none  [shards(): reduced = (sums, *[g.astype(jnp.float32) for g in grads])]
    pallas_call x0 -> x1, Pallas kernels: none -> 8.56 us  [run_widen(): pl.pallas_call(widen, grid=(steps,), out_shape=[jax.ShapeDtypeStruct(v.sh...]
    slice x2 -> x0, local copies, waits for them, and re-layouts: 2.53 us -> none  [the longest x1 1.77 us: shards(): sums[3]]
where the time goes in v4:
time: 209 us
  Pallas kernels  208 us (100%)
    pallas_call x1, Pallas kernels, run_layer(): pl.pallas_call(layer, out_shape=[jax.ShapeDtypeStruct(s, t) for _, s, t i...  200 us
    pallas_call x1, Pallas kernels, run_widen(): pl.pallas_call(widen, grid=(steps,), out_shape=[jax.ShapeDtypeStruct(v.sh...  8.56 us

profile of v4, /device:TPU:0, one launch (start us, length us, event | category | flops | bytes accessed | tf_op | source)
XLA Modules:
  0.0 209.1 jit_solution(9166637561578958196)
XLA Ops:
  0.7 199.7 %layer.1 = (bf16[256,1024]{1,0:T(8,128)(2,1)}, bf16[256,1024]{1,0:T(8,128)(2,1)}, f32[16,1024]{1,0:T(8,128)}, bf16[3,1024,256]{2,1,0:T(8,128)(2,1)}, bf16[256,10...) custom-call(bf16[256,1024]{1,0:T(8,128)(2,1)} %x_ref.1, bf16[256,1024]{1,0:T(8,128)(2,1)} %cot.1, ...), custom_call_target="tpu_custom_call" | custom-call | tf_op jit(solution)/shard_map/layer/pallas_call | solution.py:928
  200.3 8.6 %widen.1 = (bf16[256,1024]{1,0:T(8,128)(2,1)}, bf16[256,1024]{1,0:T(8,128)(2,1)}, f32[3,1024,256]{2,1,0:T(8,128)}, f32[256,1024]{1,0:T(8,128)}, f32[1024,1024]{1...) custom-call(f32[16,1024]{1,0:T(8,128)} %get-tuple-element.35.sm, ...), custom_call_target="tpu_custom_call" | custom-call | tf_op jit(solution)/shard_map/widen/pallas_call | solution.py:988

commit v5 on v4

--- a/solution.py
+++ b/solution.py
@@ -603,9 +603,7 @@
 
     @p.if_swapped
     def _():
-        up_move.take(0)
         dn_move.swap(0)
-        dn_move.swap(1)
         ub_swap().wait_recv()
 
     @p.at_home
@@ -636,6 +634,8 @@
     @p.if_swapped
     def _():
         cot_swap(p.z).start()
+        dn_move.swap(1)
+        up_move.take(0)
         up_move.take(1)
 
     for c in range(2):
@@ -779,15 +779,13 @@
     to_context(0)
     dmid_all.both(dmid_all.near)
     to_context(1)
+    dn_grad.combine()
     dmid_all.both(dmid_all.take)
-    o_sum.ship(0)
-    o_sum.ship(1)
     to_context(2)
     dmid_all.both(dmid_all.last)
     to_context(3)
 
     mirror = 1 - p.z // 2
-    dn_grad.combine()
     for g in range(4):
 
         def block(e, carry):
@@ -822,14 +820,12 @@
             up_grad.middle()
         if g == 2:
             up_grad.combine()
-            for c in range(2):
-                cut = halves[c]
-                rows_out[1, cut] = (middle[cut, :] + (o_sum.total(c) + dwb[...])).astype(BF)
-                put_back(1, output, c)
+            p.at_home(dn_grad.final)
         if g == 1:
             og[...] = mm_tn(own[...].reshape(length, share), dmid[...].reshape(length, width)).astype(BF)
             ow_grad.scatter()
-    p.at_home(dn_grad.final)
+    o_sum.ship(0)
+    o_sum.ship(1)
     for t in range(3):
         cols = slice(t * share, (t + 1) * share)
         low = hidden[:, :, cols].reshape(length, share)
@@ -858,8 +854,13 @@
     for grad_sum in late:
         grad_sum.middle()
     p.at_home(up_grad.final)
+    p.at_home(dn_grad.relay_last)
     for grad_sum in late:
         grad_sum.combine()
+    for c in range(2):
+        cut = halves[c]
+        rows_out[1, cut] = (middle[cut, :] + (o_sum.total(c) + dwb[...])).astype(BF)
+        put_back(1, output, c)
     sm_sum = sm[...]
     for k, t in enumerate(others):
         sm_copy(k, t).wait_recv()
@@ -867,7 +868,6 @@
     smp[pl.ds(p.d, 1)] = sm_sum[None]
     sm_all = Plane(p, smp, ss_sp, rs_sp)
     sm_all.send()
-    p.at_home(dn_grad.relay_last)
     p.at_home(up_grad.relay)
     for grad_sum in late:
         p.at_home(grad_sum.final)
@@ -972,7 +972,7 @@
 
 
 def run_widen(sm, out, tg, pg, og, ug, dg):
-    steps = 4
+    steps = 2
 
     def cut(v, axis):
         shape = list(v.shape)

time: 209 us -> 204 us (0.976)
  Pallas kernels: 208 us -> 203 us
    pallas_call x1, Pallas kernels: 200 us -> 196 us  [run_layer(): pl.pallas_call(layer, out_shape=[jax.ShapeDtypeStruct(s, t) for _, s, t i...]
where the time goes in v5:
time: 204 us
  Pallas kernels  203 us (100%)
    pallas_call x1, Pallas kernels, run_layer(): pl.pallas_call(layer, out_shape=[jax.ShapeDtypeStruct(s, t) for _, s, t i...  196 us
    pallas_call x1, Pallas kernels, run_widen(): pl.pallas_call(widen, grid=(steps,), out_shape=[jax.ShapeDtypeStruct(v.sh...  7.45 us

profile of v5, /device:TPU:0, one launch (start us, length us, event | category | flops | bytes accessed | tf_op | source)
XLA Modules:
  0.0 203.9 jit_solution(4524376225620889079)
XLA Ops:
  0.7 195.6 %layer.1 = (bf16[256,1024]{1,0:T(8,128)(2,1)}, bf16[256,1024]{1,0:T(8,128)(2,1)}, f32[16,1024]{1,0:T(8,128)}, bf16[3,1024,256]{2,1,0:T(8,128)(2,1)}, bf16[256,10...) custom-call(bf16[256,1024]{1,0:T(8,128)(2,1)} %x_ref.1, bf16[256,1024]{1,0:T(8,128)(2,1)} %cot.1, ...), custom_call_target="tpu_custom_call" | custom-call | tf_op jit(solution)/shard_map/layer/pallas_call | solution.py:928
  196.3 7.4 %widen.1 = (bf16[256,1024]{1,0:T(8,128)(2,1)}, bf16[256,1024]{1,0:T(8,128)(2,1)}, f32[3,1024,256]{2,1,0:T(8,128)}, f32[256,1024]{1,0:T(8,128)}, f32[1024,1024]{1...) custom-call(f32[16,1024]{1,0:T(8,128)} %get-tuple-element.35.sm, ...), custom_call_target="tpu_custom_call" | custom-call | tf_op jit(solution)/shard_map/widen/pallas_call | solution.py:988
